TPU v7x, 128 devices: a whole 4x4x4 slice. The times are simulated.
128 devices in a mesh: replica: 4 (over y), section: 8 (over x, z_lo), tensor: 4 (over z_hi, core).
Axes of the slice: x: 4, y: 4, z: 4 (z_hi: 2, z_lo: 2; z = z_hi * 2 + z_lo), core: 2. Of those that a mesh axis runs over, the one named last changes fastest.
Arguments:
- inputs: bfloat16 [4, 4, 128, 12288], P('replica', None, 'tensor'), may hold values from -0.375 to 0.375
- cotangent: bfloat16 [4, 4, 128, 12288], P('replica', None, 'tensor'), may hold values from -36 to 36
- micro_counts: int32 [4], replicated, may hold values from 1 to 4
- bounds: int32 [4, 9], replicated, may hold values from 0 to 8, as said below
- holder_down: bfloat16 [4, 8, 2, 64, 12288], P('replica', 'section'), may hold values from -0.25 to 0.25, as said below
- holder_up: bfloat16 [4, 8, 2, 64, 12288], P('replica', 'section'), may hold values from -0.25 to 0.25, as said below
- master_down: float32 [8, 64, 12288], P('section', None, ('replica', 'tensor')), may hold values from -0.25 to 0.25
- master_up: float32 [8, 64, 12288], P('section', None, ('replica', 'tensor')), may hold values from -0.25 to 0.25
- moment_down: float32 [8, 64, 12288], P('section', None, ('replica', 'tensor')), may hold values from -4 to 4
- moment_up: float32 [8, 64, 12288], P('section', None, ('replica', 'tensor')), may hold values from -4 to 4
- second_down: float32 [8, 64, 12288], P('section', None, ('replica', 'tensor')), may hold values from 0.01 to 1
- second_up: float32 [8, 64, 12288], P('section', None, ('replica', 'tensor')), may hold values from 0.01 to 1
Outputs:
- new_holder_down: bfloat16 [4, 8, 2, 64, 12288], P('replica', 'section')
- new_holder_up: bfloat16 [4, 8, 2, 64, 12288], P('replica', 'section')
- new_master_down: float32 [8, 64, 12288], P('section', None, ('replica', 'tensor'))
- new_master_up: float32 [8, 64, 12288], P('section', None, ('replica', 'tensor'))
- new_moment_down: float32 [8, 64, 12288], P('section', None, ('replica', 'tensor'))
- new_moment_up: float32 [8, 64, 12288], P('section', None, ('replica', 'tensor'))
- new_second_down: float32 [8, 64, 12288], P('section', None, ('replica', 'tensor'))
- new_second_up: float32 [8, 64, 12288], P('section', None, ('replica', 'tensor'))
Inputs may be any that keep to these rules, and one draw needn't show every extreme that they name: `bounds`: each row starts at 0, never falls and ends at 8; the sections that hold layers come first, 7 to 8 of them and at least one, and their layer counts differ by at most one; a layer l held by section s satisfies s <= l <= s + 1; a section holds at most 2 layers, and some section of replica 0 holds exactly 2. `holder_down`: each used slot holds master_down's layer that lives there by bounds, rounded to bfloat16; unused slots are zeros. `holder_up`: each used slot holds master_up's layer that lives there by bounds, rounded to bfloat16; unused slots are zeros.
All inputs are finite; a program needn't handle non-finite values.
Results may differ from a plain program's by a relative error of at most 0.006.
Values may be sent and summed in bfloat16 or wider, within the bound.
A program may use at most 192 MiB of HBM per device.

v0:
```python
import math

import jax
import jax.numpy as jnp
from jax import lax
from jax.sharding import PartitionSpec as P

norm_eps = 1e-06
learn_rate = 0.01
beta_one = 0.9
beta_two = 0.95
decay_rate = 0.1
adam_eps = 1e-08
first_fix = 0.9999734386011124
second_fix = 0.9940794707796659


def shifted(block, axis, distance):
    devices = range(lax.axis_size(axis))
    route = [(i - distance, i) for i in devices if i - distance in devices]
    return lax.ppermute(block, axis, route)


def layer_forward(hidden, down_w, up_w):
    features = hidden.shape[-1]
    ranks = down_w.shape[0]
    widened = hidden.astype(jnp.float32)
    inverse = lax.rsqrt(jnp.mean(widened * widened, axis=-1, keepdims=True) + norm_eps)
    normed = (widened * inverse).astype(jnp.bfloat16)
    projected = lax.dot_general(
        normed, down_w, (((1,), (1,)), ((), ())), preferred_element_type=jnp.float32
    ) / math.sqrt(features)
    active = jax.nn.silu(projected).astype(jnp.bfloat16)
    branch = jnp.dot(active, up_w, preferred_element_type=jnp.float32) / math.sqrt(ranks)
    return (widened + branch).astype(jnp.bfloat16)


def layer_backward(hidden, down_w, up_w, incoming):
    features = hidden.shape[-1]
    ranks = down_w.shape[0]
    widened = hidden.astype(jnp.float32)
    inverse = lax.rsqrt(jnp.mean(widened * widened, axis=-1, keepdims=True) + norm_eps)
    normed = (widened * inverse).astype(jnp.bfloat16)
    projected = lax.dot_general(
        normed, down_w, (((1,), (1,)), ((), ())), preferred_element_type=jnp.float32
    ) / math.sqrt(features)
    active = jax.nn.silu(projected).astype(jnp.bfloat16)
    sigmoid_u = jax.nn.sigmoid(projected)
    d_active = lax.dot_general(
        incoming, up_w, (((1,), (1,)), ((), ())), preferred_element_type=jnp.float32
    ) / math.sqrt(ranks)
    d_inner = (d_active * sigmoid_u * (1.0 + projected * (1.0 - sigmoid_u))).astype(jnp.bfloat16)
    grad_up = lax.dot_general(
        active, incoming, (((0,), (0,)), ((), ())), preferred_element_type=jnp.float32
    ) / math.sqrt(ranks)
    grad_down = lax.dot_general(
        d_inner, normed, (((0,), (0,)), ((), ())), preferred_element_type=jnp.float32
    ) / math.sqrt(features)
    d_normed = jnp.dot(d_inner, down_w, preferred_element_type=jnp.float32) / math.sqrt(features)
    mixed = jnp.mean(d_normed * widened, axis=-1, keepdims=True)
    d_wide = incoming.astype(jnp.float32) + inverse * (
        d_normed - widened * inverse * inverse * mixed
    )
    return (d_wide.astype(jnp.bfloat16), grad_down, grad_up)


def section_forward(hidden, downs, ups, present):
    for slot_index in range(len(present)):
        hidden = jnp.where(
            present[slot_index], layer_forward(hidden, downs[slot_index], ups[slot_index]), hidden
        )
    return hidden


def section_backward(hidden, downs, ups, present, incoming):
    stored = []
    for slot_index in range(len(present)):
        stored.append(hidden)
        if slot_index + 1 < len(present):
            hidden = jnp.where(
                present[slot_index],
                layer_forward(hidden, downs[slot_index], ups[slot_index]),
                hidden,
            )
    grads_down = [None] * len(present)
    grads_up = [None] * len(present)
    for slot_index in reversed(range(len(present))):
        d_hidden, g_down, g_up = layer_backward(
            stored[slot_index], downs[slot_index], ups[slot_index], incoming
        )
        incoming = jnp.where(present[slot_index], d_hidden, incoming)
        grads_down[slot_index] = jnp.where(present[slot_index], g_down, 0.0)
        grads_up[slot_index] = jnp.where(present[slot_index], g_up, 0.0)
    return (incoming, jnp.stack([jnp.stack(grads_down), jnp.stack(grads_up)]))


def pass_along(block_in, distance):
    return shifted(block_in, "section", distance)


def owner_window(pieces, first_layer, section_at, present):
    window = []
    for distance in range(2):
        total = jnp.zeros_like(pieces[:, 0])
        for slot_index in range(len(present)):
            matching = present[slot_index] & (first_layer + slot_index - section_at == distance)
            total = jnp.where(matching, pieces[:, slot_index], total)
        window.append(total)
    return window


def holder_slots(window, first_layer, section_at, present):
    filled = []
    for slot_index in range(len(present)):
        chosen = jnp.zeros_like(window[0])
        for distance in range(len(window)):
            matching = present[slot_index] & (first_layer + slot_index - section_at == distance)
            chosen = jnp.where(matching, window[distance], chosen)
        filled.append(chosen)
    return jnp.stack(filled, axis=1)


def on_device(
    inputs,
    cotangent,
    micro_counts,
    bounds,
    holder_down,
    holder_up,
    master_down,
    master_up,
    moment_down,
    moment_up,
    second_down,
    second_up,
):
    replica_at = lax.axis_index("replica")
    section_at = lax.axis_index("section")
    sections = lax.axis_size("section")
    micros = inputs.shape[1]
    slots = holder_down.shape[2]
    first_layer = bounds[replica_at, section_at]
    after_layer = bounds[replica_at, section_at + 1]
    counted = micro_counts[replica_at]
    present = [first_layer + slot_index < after_layer for slot_index in range(slots)]
    downs = holder_down[0, 0]
    ups = holder_up[0, 0]
    own_inputs = inputs[0]
    own_cotangent = cotangent[0]
    blank = jnp.zeros(own_inputs.shape[1:], jnp.bfloat16)

    def forward_tick(carry, time_step):
        incoming, stored = carry
        micro_index = time_step - section_at
        in_range = (micro_index >= 0) & (micro_index < micros)
        clipped = jnp.clip(micro_index, 0, micros - 1)
        entering = jnp.where(
            section_at == 0, lax.dynamic_index_in_dim(own_inputs, clipped, 0, False), incoming
        )
        previous = lax.dynamic_index_in_dim(stored, clipped, 0, False)
        stored = lax.dynamic_update_index_in_dim(
            stored, jnp.where(in_range, entering, previous), clipped, 0
        )
        leaving = section_forward(entering, downs, ups, present)
        return ((pass_along(leaving, 1), stored), None)

    (_, stored), _ = lax.scan(
        forward_tick, (blank, jnp.zeros_like(own_inputs)), jnp.arange(micros + sections - 1)
    )
    grads_blank = jnp.zeros((2, slots) + downs.shape[1:], jnp.float32)

    def backward_tick(carry, time_step):
        incoming, grads = carry
        micro_index = time_step - (sections - 1 - section_at)
        in_range = (micro_index >= 0) & (micro_index < micros)
        clipped = jnp.clip(micro_index, 0, micros - 1)
        taking = in_range & (clipped < counted)
        arriving = jnp.where(
            section_at == sections - 1,
            lax.dynamic_index_in_dim(own_cotangent, clipped, 0, False),
            incoming,
        )
        arriving = jnp.where(taking, arriving, jnp.zeros_like(arriving))
        saved_input = lax.dynamic_index_in_dim(stored, clipped, 0, False)
        leaving, added = section_backward(saved_input, downs, ups, present, arriving)
        return ((pass_along(leaving, -1), grads + added), None)

    (_, grads), _ = lax.scan(backward_tick, (blank, grads_blank), jnp.arange(micros + sections - 1))
    window = owner_window(grads, first_layer, section_at, present)
    owned = window[0] + shifted(window[1].astype(jnp.bfloat16), "section", 1).astype(jnp.float32)
    gradient = lax.psum_scatter(
        owned.astype(jnp.bfloat16), ("replica", "tensor"), scatter_dimension=2, tiled=True
    ).astype(jnp.float32)
    params = jnp.stack([master_down[0], master_up[0]])
    moments = jnp.stack([moment_down[0], moment_up[0]])
    seconds = jnp.stack([second_down[0], second_up[0]])
    new_moments = beta_one * moments + (1.0 - beta_one) * gradient
    new_seconds = beta_two * seconds + (1.0 - beta_two) * gradient * gradient
    new_params = params - learn_rate * (
        new_moments / first_fix / (jnp.sqrt(new_seconds / second_fix) + adam_eps)
        + decay_rate * params
    )
    shares = new_params.astype(jnp.bfloat16)
    whole = lax.all_gather(shares, ("replica", "tensor"), axis=2, tiled=True)
    following = shifted(whole, "section", -1)
    placed = holder_slots([whole, following], first_layer, section_at, present)
    return (
        placed[0][None, None],
        placed[1][None, None],
        new_params[0][None],
        new_params[1][None],
        new_moments[0][None],
        new_moments[1][None],
        new_seconds[0][None],
        new_seconds[1][None],
    )


def solution(mesh):
    in_specs = (
        P("replica", None, "tensor", None),
        P("replica", None, "tensor", None),
        P(),
        P(),
        P("replica", "section", None, None, None),
        P("replica", "section", None, None, None),
        P("section", None, ("replica", "tensor")),
        P("section", None, ("replica", "tensor")),
        P("section", None, ("replica", "tensor")),
        P("section", None, ("replica", "tensor")),
        P("section", None, ("replica", "tensor")),
        P("section", None, ("replica", "tensor")),
    )
    out_specs = (
        P("replica", "section", None, None, None),
        P("replica", "section", None, None, None),
        P("section", None, ("replica", "tensor")),
        P("section", None, ("replica", "tensor")),
        P("section", None, ("replica", "tensor")),
        P("section", None, ("replica", "tensor")),
        P("section", None, ("replica", "tensor")),
        P("section", None, ("replica", "tensor")),
    )
    return jax.shard_map(
        on_device, mesh=mesh, in_specs=in_specs, out_specs=out_specs, check_vma=False
    )
```

profile of v0, /device:TPU:1, one launch (start us, length us, event | category | flops | bytes accessed | tf_op | source)
XLA Modules:
  0.0 1175.6 jit_solution(2589263025337062308)
XLA Ops:
  16.2 354.0 %while.28 = (s32[]{:T(128)}, bf16[32,12288]{1,0:T(8,128)(2,1)}, bf16[4,32,12288]{2,1,0:T(8,128)(2,1)}, pred[]{:T(512)}, pred[]{:T(512)}, /*index=5*/pred[]{:T(51...) while((s32[]{:T(128)}, bf16[32,12288]{1,0:T(8,128)(2,1)}, ...), condition=%wide.region_3.4_spmd, body=%wide.region_0.3_spmd.sunk | while | flops 210788416 | bytes 23596576 | solution.py:167
  22.1 4.6 fusion.207
  26.7 4.5 fusion.208
  31.2 5.6 collective-permute-start
  36.8 15.6 %collective-permute-done = bf16[32,12288]{1,0:T(8,128)(2,1)} collective-permute-done((bf16[32,12288]{1,0:T(8,128)(2,1)}, bf16[32,12288]{1,0:T(8,128)(2,1)}, u32[]{:S(2)}, u32[]{:S(2)}) %collective-permute-start) | collective-permute-done | bytes 786464 | tf_op jit(solution)/shard_map/while/body/eval_jaxpr/ppermute | solution.py:21
  58.2 4.6 fusion.207
  62.9 4.5 fusion.208
  67.4 5.3 collective-permute-start
  72.7 14.6 %collective-permute-done = bf16[32,12288]{1,0:T(8,128)(2,1)} collective-permute-done((bf16[32,12288]{1,0:T(8,128)(2,1)}, bf16[32,12288]{1,0:T(8,128)(2,1)}, u32[]{:S(2)}, u32[]{:S(2)}) %collective-permute-start) | collective-permute-done | bytes 786464 | tf_op jit(solution)/shard_map/while/body/eval_jaxpr/ppermute | solution.py:21
  93.2 4.6 fusion.207
  97.9 4.5 fusion.208
  102.4 5.3 collective-permute-start
  107.7 13.7 %collective-permute-done = bf16[32,12288]{1,0:T(8,128)(2,1)} collective-permute-done((bf16[32,12288]{1,0:T(8,128)(2,1)}, bf16[32,12288]{1,0:T(8,128)(2,1)}, u32[]{:S(2)}, u32[]{:S(2)}) %collective-permute-start) | collective-permute-done | bytes 786464 | tf_op jit(solution)/shard_map/while/body/eval_jaxpr/ppermute | solution.py:21
  127.3 4.6 fusion.207
  131.9 4.5 fusion.208
  136.4 5.7 collective-permute-start
  142.1 12.8 %collective-permute-done = bf16[32,12288]{1,0:T(8,128)(2,1)} collective-permute-done((bf16[32,12288]{1,0:T(8,128)(2,1)}, bf16[32,12288]{1,0:T(8,128)(2,1)}, u32[]{:S(2)}, u32[]{:S(2)}) %collective-permute-start) | collective-permute-done | bytes 786464 | tf_op jit(solution)/shard_map/while/body/eval_jaxpr/ppermute | solution.py:21
  160.8 4.6 fusion.207
  165.4 4.5 fusion.208
  170.0 6.2 collective-permute-start
  176.1 11.9 %collective-permute-done = bf16[32,12288]{1,0:T(8,128)(2,1)} collective-permute-done((bf16[32,12288]{1,0:T(8,128)(2,1)}, bf16[32,12288]{1,0:T(8,128)(2,1)}, u32[]{:S(2)}, u32[]{:S(2)}) %collective-permute-start) | collective-permute-done | bytes 786464 | tf_op jit(solution)/shard_map/while/body/eval_jaxpr/ppermute | solution.py:21
  193.9 4.6 fusion.207
  198.6 4.5 fusion.208
  203.1 6.2 collective-permute-start
  209.3 10.9 collective-permute-done
  226.1 4.6 fusion.207
  230.8 4.5 fusion.208
  235.3 6.2 collective-permute-start
  241.5 10.0 collective-permute-done
  257.4 4.6 fusion.207
  262.0 4.5 fusion.208
  266.5 6.2 collective-permute-start
  272.7 9.1 collective-permute-done
  287.7 4.6 fusion.207
  292.4 4.5 fusion.208
  296.9 6.2 collective-permute-start
  303.1 8.3 collective-permute-done
  317.3 4.6 fusion.207
  321.9 4.5 fusion.208
  326.4 6.2 collective-permute-start
  332.6 8.3 collective-permute-done
  346.8 4.6 fusion.207
  351.5 4.5 fusion.208
  356.0 5.9 collective-permute-start
  361.9 8.3 collective-permute-done
  371.1 489.2 %while.29 = (s32[]{:T(128)}, bf16[32,12288]{1,0:T(8,128)(2,1)}, f32[2,2,64,12288]{3,2,1,0:T(8,128)}, pred[]{:T(512)}, pred[]{:T(512)}, /*index=5*/s32[11]{0:T(12...) while((s32[]{:T(128)}, bf16[32,12288]{1,0:T(8,128)(2,1)}, ...), condition=%wide.region_9.10_spmd.clone, body=%wide.region_4.9_spmd.clone.sunk | while | flops 591865920 | bytes 180199120 | solution.py:188
  405.2 5.4 maximum_add_fusion.2
  444.6 10.9 maximum_add_fusion.2
  489.6 10.9 maximum_add_fusion.2
  534.6 10.9 maximum_add_fusion.2
  579.6 10.9 maximum_add_fusion.2
  624.5 10.9 maximum_add_fusion.2
  669.5 10.9 maximum_add_fusion.2
  714.5 10.9 maximum_add_fusion.2
  759.4 10.9 maximum_add_fusion.2
  804.4 10.9 maximum_add_fusion.2
  849.4 10.9 maximum_add_fusion.2
  860.3 6.7 fusion.139
  866.9 12.0 %collective-permute-start.2 = (bf16[2,64,12288]{2,1,0:T(8,128)(2,1)}, bf16[2,64,12288]{2,1,0:T(8,128)(2,1)S(1)}, u32[]{:S(2)}, u32[]{:S(2)}) collective-permute-start(bf16[2,64,12288]{2,1,0:T(8,128)(2,1)} %fusion.139), channel_id=1, source_target_pairs={{0,4},{4,8},{8,12},{12,16},{16,20},{20,24},{24,28},{1,5},{5,9},{9,... | collective-permute-start | bytes 9437192 | tf_op jit(solution)/shard_map/ppermute | solution.py:21
  879.0 56.3 %collective-permute-done.2 = bf16[2,64,12288]{2,1,0:T(8,128)(2,1)S(1)} collective-permute-done((bf16[2,64,12288]{2,1,0:T(8,128)(2,1)}, bf16[2,64,12288]{2,1,0:T(8,128)(2,1)S(1)}, u32[]{:S(2)}, u32[]{:S(2)}) %collective-permute-start.2) | collective-permute-done | bytes 3145760 | tf_op jit(solution)/shard_map/ppermute | solution.py:21
  935.3 6.8 fusion.138
  943.1 93.6 %reduce-scatter.2.cloned.1.call-done = bf16[2,64,768]{2,1,0:T(8,128)(2,1)} async-done(((bf16[2,64,12288]{2,1,0:T(8,128)(2,1)}), bf16[2,64,768]{2,1,0:T(8,128)(2,1)}) %reduce-scatter.2.cloned.1.call-update) | async-done | bytes 196624 | tf_op jit(solution)/shard_map/reduce_scatter | solution.py:191
  1038.7 53.4 %all-gather.2.cloned.1.call-done = bf16[2,64,12288]{2,1,0:T(8,128)(2,1)} async-done(((bf16[2,64,768]{2,1,0:T(8,128)(2,1)}), bf16[2,64,12288]{2,1,0:T(8,128)(2,1)}) %all-gather.2.cloned.1.call-update) | async-done | bytes 3145744 | tf_op jit(solution)/shard_map/all_gather | solution.py:204
  1095.0 68.6 %collective-permute-done.3 = bf16[2,64,12288]{2,1,0:T(8,128)(2,1)S(1)} collective-permute-done((bf16[2,64,12288]{2,1,0:T(8,128)(2,1)}, bf16[2,64,12288]{2,1,0:T(8,128)(2,1)S(1)}, u32[]{:S(2)}, u32[]{:S(2)}) %collective-permute-start.3) | collective-permute-done | bytes 3145760 | tf_op jit(solution)/shard_map/ppermute | solution.py:21
  (485 shorter events, 434.0 us)
Async XLA Ops:
  7.2 9.0 copy-start
  7.2 1029.6 %reduce-scatter.2.cloned.1.call-start = ((), (), s32[]{:S(2)}) async-start(), calls=%async_computation.1 | async-start | bytes 3342336 | tf_op jit(solution)/shard_map/reduce_scatter | solution.py:191
  31.2 21.1 %collective-permute-start = (bf16[32,12288]{1,0:T(8,128)(2,1)}, bf16[32,12288]{1,0:T(8,128)(2,1)}, u32[]{:S(2)}, u32[]{:S(2)}) collective-permute-start(bf16[32,12288]{1,0:T(8,128)(2,1)} %fusion.208), channel_id=1, source_target_pairs={{0,4},{4,8},{8,12},{12,16},{16,20},{20,24},{24,28},{1,5},{5,9},{9,... | collective-permute-start | bytes 2359304 | tf_op jit(solution)/shard_map/while/body/eval_jaxpr/ppermute | solution.py:21
  67.4 19.9 %collective-permute-start = (bf16[32,12288]{1,0:T(8,128)(2,1)}, bf16[32,12288]{1,0:T(8,128)(2,1)}, u32[]{:S(2)}, u32[]{:S(2)}) collective-permute-start(bf16[32,12288]{1,0:T(8,128)(2,1)} %fusion.208), channel_id=1, source_target_pairs={{0,4},{4,8},{8,12},{12,16},{16,20},{20,24},{24,28},{1,5},{5,9},{9,... | collective-permute-start | bytes 2359304 | tf_op jit(solution)/shard_map/while/body/eval_jaxpr/ppermute | solution.py:21
  102.4 19.0 %collective-permute-start = (bf16[32,12288]{1,0:T(8,128)(2,1)}, bf16[32,12288]{1,0:T(8,128)(2,1)}, u32[]{:S(2)}, u32[]{:S(2)}) collective-permute-start(bf16[32,12288]{1,0:T(8,128)(2,1)} %fusion.208), channel_id=1, source_target_pairs={{0,4},{4,8},{8,12},{12,16},{16,20},{20,24},{24,28},{1,5},{5,9},{9,... | collective-permute-start | bytes 2359304 | tf_op jit(solution)/shard_map/while/body/eval_jaxpr/ppermute | solution.py:21
  136.4 18.4 %collective-permute-start = (bf16[32,12288]{1,0:T(8,128)(2,1)}, bf16[32,12288]{1,0:T(8,128)(2,1)}, u32[]{:S(2)}, u32[]{:S(2)}) collective-permute-start(bf16[32,12288]{1,0:T(8,128)(2,1)} %fusion.208), channel_id=1, source_target_pairs={{0,4},{4,8},{8,12},{12,16},{16,20},{20,24},{24,28},{1,5},{5,9},{9,... | collective-permute-start | bytes 2359304 | tf_op jit(solution)/shard_map/while/body/eval_jaxpr/ppermute | solution.py:21
  170.0 18.1 %collective-permute-start = (bf16[32,12288]{1,0:T(8,128)(2,1)}, bf16[32,12288]{1,0:T(8,128)(2,1)}, u32[]{:S(2)}, u32[]{:S(2)}) collective-permute-start(bf16[32,12288]{1,0:T(8,128)(2,1)} %fusion.208), channel_id=1, source_target_pairs={{0,4},{4,8},{8,12},{12,16},{16,20},{20,24},{24,28},{1,5},{5,9},{9,... | collective-permute-start | bytes 2359304 | tf_op jit(solution)/shard_map/while/body/eval_jaxpr/ppermute | solution.py:21
  203.1 17.1 %collective-permute-start = (bf16[32,12288]{1,0:T(8,128)(2,1)}, bf16[32,12288]{1,0:T(8,128)(2,1)}, u32[]{:S(2)}, u32[]{:S(2)}) collective-permute-start(bf16[32,12288]{1,0:T(8,128)(2,1)} %fusion.208), channel_id=1, source_target_pairs={{0,4},{4,8},{8,12},{12,16},{16,20},{20,24},{24,28},{1,5},{5,9},{9,... | collective-permute-start | bytes 2359304 | tf_op jit(solution)/shard_map/while/body/eval_jaxpr/ppermute | solution.py:21
  235.3 16.2 %collective-permute-start = (bf16[32,12288]{1,0:T(8,128)(2,1)}, bf16[32,12288]{1,0:T(8,128)(2,1)}, u32[]{:S(2)}, u32[]{:S(2)}) collective-permute-start(bf16[32,12288]{1,0:T(8,128)(2,1)} %fusion.208), channel_id=1, source_target_pairs={{0,4},{4,8},{8,12},{12,16},{16,20},{20,24},{24,28},{1,5},{5,9},{9,... | collective-permute-start | bytes 2359304 | tf_op jit(solution)/shard_map/while/body/eval_jaxpr/ppermute | solution.py:21
  266.5 15.3 %collective-permute-start = (bf16[32,12288]{1,0:T(8,128)(2,1)}, bf16[32,12288]{1,0:T(8,128)(2,1)}, u32[]{:S(2)}, u32[]{:S(2)}) collective-permute-start(bf16[32,12288]{1,0:T(8,128)(2,1)} %fusion.208), channel_id=1, source_target_pairs={{0,4},{4,8},{8,12},{12,16},{16,20},{20,24},{24,28},{1,5},{5,9},{9,... | collective-permute-start | bytes 2359304 | tf_op jit(solution)/shard_map/while/body/eval_jaxpr/ppermute | solution.py:21
  296.9 14.5 %collective-permute-start = (bf16[32,12288]{1,0:T(8,128)(2,1)}, bf16[32,12288]{1,0:T(8,128)(2,1)}, u32[]{:S(2)}, u32[]{:S(2)}) collective-permute-start(bf16[32,12288]{1,0:T(8,128)(2,1)} %fusion.208), channel_id=1, source_target_pairs={{0,4},{4,8},{8,12},{12,16},{16,20},{20,24},{24,28},{1,5},{5,9},{9,... | collective-permute-start | bytes 2359304 | tf_op jit(solution)/shard_map/while/body/eval_jaxpr/ppermute | solution.py:21
  326.4 14.5 %collective-permute-start = (bf16[32,12288]{1,0:T(8,128)(2,1)}, bf16[32,12288]{1,0:T(8,128)(2,1)}, u32[]{:S(2)}, u32[]{:S(2)}) collective-permute-start(bf16[32,12288]{1,0:T(8,128)(2,1)} %fusion.208), channel_id=1, source_target_pairs={{0,4},{4,8},{8,12},{12,16},{16,20},{20,24},{24,28},{1,5},{5,9},{9,... | collective-permute-start | bytes 2359304 | tf_op jit(solution)/shard_map/while/body/eval_jaxpr/ppermute | solution.py:21
  356.0 14.2 %collective-permute-start = (bf16[32,12288]{1,0:T(8,128)(2,1)}, bf16[32,12288]{1,0:T(8,128)(2,1)}, u32[]{:S(2)}, u32[]{:S(2)}) collective-permute-start(bf16[32,12288]{1,0:T(8,128)(2,1)} %fusion.208), channel_id=1, source_target_pairs={{0,4},{4,8},{8,12},{12,16},{16,20},{20,24},{24,28},{1,5},{5,9},{9,... | collective-permute-start | bytes 2359304 | tf_op jit(solution)/shard_map/while/body/eval_jaxpr/ppermute | solution.py:21
  371.1 4.7 copy-start.1
  372.5 3.3 copy-start.11
  392.0 18.5 %collective-permute-start.1 = (bf16[32,12288]{1,0:T(8,128)(2,1)}, bf16[32,12288]{1,0:T(8,128)(2,1)}, u32[]{:S(2)}, u32[]{:S(2)}) collective-permute-start(bf16[32,12288]{1,0:T(8,128)(2,1)} %fusion.231), channel_id=1, source_target_pairs={{4,0},{8,4},{12,8},{16,12},{20,16},{24,20},{28,24},{5,1},{9,5},{13... | collective-permute-start | bytes 2359304 | tf_op jit(solution)/shard_map/while/body/eval_jaxpr/ppermute | solution.py:21
  405.1 5.4 copy-start.2
  410.6 4.7 copy-start.1
  412.0 3.3 copy-start.11
  431.5 24.0 %collective-permute-start.1 = (bf16[32,12288]{1,0:T(8,128)(2,1)}, bf16[32,12288]{1,0:T(8,128)(2,1)}, u32[]{:S(2)}, u32[]{:S(2)}) collective-permute-start(bf16[32,12288]{1,0:T(8,128)(2,1)} %fusion.231), channel_id=1, source_target_pairs={{4,0},{8,4},{12,8},{16,12},{20,16},{24,20},{28,24},{5,1},{9,5},{13... | collective-permute-start | bytes 2359304 | tf_op jit(solution)/shard_map/while/body/eval_jaxpr/ppermute | solution.py:21
  444.6 10.9 copy-start.2
  455.5 4.7 copy-start.1
  456.9 3.3 copy-start.11
  476.5 24.0 %collective-permute-start.1 = (bf16[32,12288]{1,0:T(8,128)(2,1)}, bf16[32,12288]{1,0:T(8,128)(2,1)}, u32[]{:S(2)}, u32[]{:S(2)}) collective-permute-start(bf16[32,12288]{1,0:T(8,128)(2,1)} %fusion.231), channel_id=1, source_target_pairs={{4,0},{8,4},{12,8},{16,12},{20,16},{24,20},{28,24},{5,1},{9,5},{13... | collective-permute-start | bytes 2359304 | tf_op jit(solution)/shard_map/while/body/eval_jaxpr/ppermute | solution.py:21
  489.6 10.9 copy-start.2
  500.5 4.7 copy-start.1
  501.9 3.3 copy-start.11
  521.5 24.0 %collective-permute-start.1 = (bf16[32,12288]{1,0:T(8,128)(2,1)}, bf16[32,12288]{1,0:T(8,128)(2,1)}, u32[]{:S(2)}, u32[]{:S(2)}) collective-permute-start(bf16[32,12288]{1,0:T(8,128)(2,1)} %fusion.231), channel_id=1, source_target_pairs={{4,0},{8,4},{12,8},{16,12},{20,16},{24,20},{28,24},{5,1},{9,5},{13... | collective-permute-start | bytes 2359304 | tf_op jit(solution)/shard_map/while/body/eval_jaxpr/ppermute | solution.py:21
  534.6 10.9 copy-start.2
  545.5 4.7 copy-start.1
  546.9 3.3 copy-start.11
  566.4 24.0 %collective-permute-start.1 = (bf16[32,12288]{1,0:T(8,128)(2,1)}, bf16[32,12288]{1,0:T(8,128)(2,1)}, u32[]{:S(2)}, u32[]{:S(2)}) collective-permute-start(bf16[32,12288]{1,0:T(8,128)(2,1)} %fusion.231), channel_id=1, source_target_pairs={{4,0},{8,4},{12,8},{16,12},{20,16},{24,20},{28,24},{5,1},{9,5},{13... | collective-permute-start | bytes 2359304 | tf_op jit(solution)/shard_map/while/body/eval_jaxpr/ppermute | solution.py:21
  579.5 10.9 copy-start.2
  590.4 4.7 copy-start.1
  591.8 3.3 copy-start.11
  611.4 24.0 %collective-permute-start.1 = (bf16[32,12288]{1,0:T(8,128)(2,1)}, bf16[32,12288]{1,0:T(8,128)(2,1)}, u32[]{:S(2)}, u32[]{:S(2)}) collective-permute-start(bf16[32,12288]{1,0:T(8,128)(2,1)} %fusion.231), channel_id=1, source_target_pairs={{4,0},{8,4},{12,8},{16,12},{20,16},{24,20},{28,24},{5,1},{9,5},{13... | collective-permute-start | bytes 2359304 | tf_op jit(solution)/shard_map/while/body/eval_jaxpr/ppermute | solution.py:21
  624.5 10.9 copy-start.2
  635.4 4.7 copy-start.1
  636.8 3.3 copy-start.11
  656.4 24.0 %collective-permute-start.1 = (bf16[32,12288]{1,0:T(8,128)(2,1)}, bf16[32,12288]{1,0:T(8,128)(2,1)}, u32[]{:S(2)}, u32[]{:S(2)}) collective-permute-start(bf16[32,12288]{1,0:T(8,128)(2,1)} %fusion.231), channel_id=1, source_target_pairs={{4,0},{8,4},{12,8},{16,12},{20,16},{24,20},{28,24},{5,1},{9,5},{13... | collective-permute-start | bytes 2359304 | tf_op jit(solution)/shard_map/while/body/eval_jaxpr/ppermute | solution.py:21
  669.5 10.9 copy-start.2
  680.4 4.7 copy-start.1
  681.8 3.3 copy-start.11
  701.3 24.0 %collective-permute-start.1 = (bf16[32,12288]{1,0:T(8,128)(2,1)}, bf16[32,12288]{1,0:T(8,128)(2,1)}, u32[]{:S(2)}, u32[]{:S(2)}) collective-permute-start(bf16[32,12288]{1,0:T(8,128)(2,1)} %fusion.231), channel_id=1, source_target_pairs={{4,0},{8,4},{12,8},{16,12},{20,16},{24,20},{28,24},{5,1},{9,5},{13... | collective-permute-start | bytes 2359304 | tf_op jit(solution)/shard_map/while/body/eval_jaxpr/ppermute | solution.py:21
  714.4 10.9 copy-start.2
  725.4 4.7 copy-start.1
  726.7 3.3 copy-start.11
  746.3 24.0 %collective-permute-start.1 = (bf16[32,12288]{1,0:T(8,128)(2,1)}, bf16[32,12288]{1,0:T(8,128)(2,1)}, u32[]{:S(2)}, u32[]{:S(2)}) collective-permute-start(bf16[32,12288]{1,0:T(8,128)(2,1)} %fusion.231), channel_id=1, source_target_pairs={{4,0},{8,4},{12,8},{16,12},{20,16},{24,20},{28,24},{5,1},{9,5},{13... | collective-permute-start | bytes 2359304 | tf_op jit(solution)/shard_map/while/body/eval_jaxpr/ppermute | solution.py:21
  759.4 10.9 copy-start.2
  770.3 4.7 copy-start.1
  771.7 3.3 copy-start.11
  791.3 24.0 %collective-permute-start.1 = (bf16[32,12288]{1,0:T(8,128)(2,1)}, bf16[32,12288]{1,0:T(8,128)(2,1)}, u32[]{:S(2)}, u32[]{:S(2)}) collective-permute-start(bf16[32,12288]{1,0:T(8,128)(2,1)} %fusion.231), channel_id=1, source_target_pairs={{4,0},{8,4},{12,8},{16,12},{20,16},{24,20},{28,24},{5,1},{9,5},{13... | collective-permute-start | bytes 2359304 | tf_op jit(solution)/shard_map/while/body/eval_jaxpr/ppermute | solution.py:21
  804.4 10.9 copy-start.2
  815.3 4.7 copy-start.1
  816.7 3.3 copy-start.11
  836.2 24.0 %collective-permute-start.1 = (bf16[32,12288]{1,0:T(8,128)(2,1)}, bf16[32,12288]{1,0:T(8,128)(2,1)}, u32[]{:S(2)}, u32[]{:S(2)}) collective-permute-start(bf16[32,12288]{1,0:T(8,128)(2,1)} %fusion.231), channel_id=1, source_target_pairs={{4,0},{8,4},{12,8},{16,12},{20,16},{24,20},{28,24},{5,1},{9,5},{13... | collective-permute-start | bytes 2359304 | tf_op jit(solution)/shard_map/while/body/eval_jaxpr/ppermute | solution.py:21
  849.4 10.9 copy-start.2
  866.9 68.4 %collective-permute-start.2 = (bf16[2,64,12288]{2,1,0:T(8,128)(2,1)}, bf16[2,64,12288]{2,1,0:T(8,128)(2,1)S(1)}, u32[]{:S(2)}, u32[]{:S(2)}) collective-permute-start(bf16[2,64,12288]{2,1,0:T(8,128)(2,1)} %fusion.139), channel_id=1, source_target_pairs={{0,4},{4,8},{8,12},{12,16},{16,20},{20,24},{24,28},{1,5},{5,9},{9,... | collective-permute-start | bytes 9437192 | tf_op jit(solution)/shard_map/ppermute | solution.py:21
  942.1 94.6 %copy-start.7 = (f32[1,64,768]{2,1,0:T(8,128)S(1)}, f32[1,64,768]{2,1,0:T(8,128)}, u32[]{:S(2)}) copy-start(f32[1,64,768]{2,1,0:T(8,128)} %param.25) | copy-start | bytes 589828
  942.1 94.6 %copy-start.8 = (f32[1,64,768]{2,1,0:T(8,128)S(1)}, f32[1,64,768]{2,1,0:T(8,128)}, u32[]{:S(2)}) copy-start(f32[1,64,768]{2,1,0:T(8,128)} %param.24) | copy-start | bytes 589828
  942.1 94.6 %copy-start.9 = (f32[1,64,768]{2,1,0:T(8,128)S(1)}, f32[1,64,768]{2,1,0:T(8,128)}, u32[]{:S(2)}) copy-start(f32[1,64,768]{2,1,0:T(8,128)} %param.27) | copy-start | bytes 589828
  942.1 94.6 %copy-start.10 = (f32[1,64,768]{2,1,0:T(8,128)S(1)}, f32[1,64,768]{2,1,0:T(8,128)}, u32[]{:S(2)}) copy-start(f32[1,64,768]{2,1,0:T(8,128)} %param.26) | copy-start | bytes 589828
  942.2 149.9 %all-gather.2.cloned.1.call-start = ((), (), s32[]{:S(2)}) async-start(), calls=%async_computation.2 | async-start | bytes 3342336 | tf_op jit(solution)/shard_map/all_gather | solution.py:204
  1092.1 71.5 %collective-permute-start.3 = (bf16[2,64,12288]{2,1,0:T(8,128)(2,1)}, bf16[2,64,12288]{2,1,0:T(8,128)(2,1)S(1)}, u32[]{:S(2)}, u32[]{:S(2)}) collective-permute-start(bf16[2,64,12288]{2,1,0:T(8,128)(2,1)} %all-gather.2.cloned.1.call-done), channel_id=1, source_target_pairs={{4,0},{8,4},{12,8},{16,12},{20,16},{24,20},{28,24},{5,1},{9,5},{13... | collective-permute-start | bytes 9437192 | tf_op jit(solution)/shard_map/ppermute | solution.py:21
  (35 other events, 63.7 us)
Sparse Core Ops, SparseCore 0:
  942.3 94.4 reduce-scatter.1
  1039.7 52.3 all-gather.1
where the time goes:
time: 1180 us
  waiting for transfers between devices  395 us (33%)
  matrix products  314 us (27%)
  other arithmetic  268 us (23%)
  starting transfers between devices  92.2 us (8%)
  local copies, waits for them, and re-layouts  65.3 us (6%)
  loops' own time  23.8 us (2%)
  between operations  17.4 us (1%)
    ppermute x24, waiting for transfers between devices, shifted(): return lax.ppermute(block, axis, route)  248 us
    dot_general x33, matrix products, layer_forward(): jnp.dot(active, up_w, preferred_element_type=jnp.float32) / math.sqrt(ranks)  120 us
    add x11, other arithmetic, backward_tick(): return ((pass_along(leaving, -1), grads + added), None)  114 us
    reduce_scatter x1, waiting for transfers between devices, on_device(): lax.psum_scatter(owned.astype(jnp.bfloat16), ('replica', 'tensor'), scatt...  93.6 us
    ppermute x24, starting transfers between devices, shifted(): return lax.ppermute(block, axis, route)  92.1 us
    all_gather x1, waiting for transfers between devices, on_device(): whole = lax.all_gather(shares, ('replica', 'tensor'), axis=2, tiled=True)  53.4 us
    dot_general x22, matrix products, layer_backward(): lax.dot_general(active, incoming, (((0,), (0,)), ((), ())), preferred_ele...  50 us
    another operation x11, other arithmetic, section_backward(): return (incoming, jnp.stack([jnp.stack(grads_down), jnp.stack(grads_up)]))  48.2 us
  transfers between devices with their start and end apart: 26, of which 15 were waited for; matrix products, arithmetic and copies ran while one was open for 21% of the time, Pallas kernels for 0%

commit v1 on v0

v1 whole, which is shorter than its diff:
```python
import functools
import math

import jax
import jax.numpy as jnp
from jax import lax
from jax.experimental import pallas as pl
from jax.experimental.pallas import tpu as pltpu
from jax.sharding import PartitionSpec as P

norm_eps = 1e-06
learn_rate = 0.01
beta_one = 0.9
beta_two = 0.95
decay_rate = 0.1
adam_eps = 1e-08
first_fix = 0.9999734386011124
second_fix = 0.9940794707796659
plane = ("replica", "tensor")


def dot_t(left, right):
    return lax.dot_general(
        left, right, (((1,), (1,)), ((), ())), preferred_element_type=jnp.float32
    )


def dot_n(left, right):
    return jnp.dot(left, right, preferred_element_type=jnp.float32)


def layers_kernel(features, tokens_per, meta, z, square, gram, coef, mixing, hb, rate, a_s, w_s, a_all):
    layers, _, tokens, wide = z.shape
    rank = wide // 2
    root = 1.0 / math.sqrt(features)
    section, counted = meta[layers], meta[layers + 1]
    row = lax.broadcasted_iota(jnp.int32, (tokens, 1), 0)
    taken = row < counted * tokens_per

    def picked(kind, layer):
        first = z[layer, kind][:, :rank]
        if layer == 0:
            return first.astype(jnp.float32)
        before = z[layer - 1, kind]
        code = meta[layer]
        other = jnp.where(code == 1, before[:, rank:], before[:, :rank])
        return jnp.where(code == 0, first, other).astype(jnp.float32)

    norm = square[...]
    state = jnp.concatenate([picked(1, l) for l in range(layers)], axis=1)
    a_all[...] = jnp.zeros_like(a_all)
    slopes, inner, rhos = [], [], []
    for l in range(layers):
        at = slice(l * rank, (l + 1) * rank)
        hb[l] = state
        rho = lax.rsqrt(jnp.maximum(norm, 0.0) * (1.0 / features) + norm_eps)
        product = picked(0, l)
        if l:
            product = product + dot_t(a_all[...], gram[l, :rank])
        u = product * (rho * root)
        sigma = jax.nn.sigmoid(u)
        active = (u * sigma * (1.0 / math.sqrt(rank))).astype(jnp.bfloat16)
        a_s[l] = active
        a_all[:, at] = active
        added = dot_n(active, gram[l, rank:])
        wide_a = active.astype(jnp.float32)
        norm = norm + jnp.sum(wide_a * (2.0 * state[:, at] + added[:, at]), axis=1, keepdims=True)
        state = state + added
        slopes.append(sigma * (1.0 + u * (1.0 - sigma)) * (1.0 / math.sqrt(rank)))
        inner.append(u)
        rhos.append(rho)
    back = jnp.concatenate(
        [jnp.where(taken, picked(2, l), 0.0) for l in range(layers)], axis=1
    )
    gamma = jnp.zeros((tokens, 1), jnp.float32)
    for l in reversed(range(layers)):
        at = slice(l * rank, (l + 1) * rank)
        e = back[:, at] * slopes[l]
        rho = rhos[l]
        w = (e * (rho * root)).astype(jnp.bfloat16)
        w_s[l] = w
        rate[l] = gamma
        c = rho * rho * jnp.sum(e * inner[l], axis=1, keepdims=True) * (1.0 / features)
        gamma = gamma + c
        if l:
            back = back + dot_n(w, gram[l, :rank]) - c * hb[l]
    own_w = w_s[section].astype(jnp.float32)
    own_a = a_s[section].astype(jnp.float32)
    own_rate = rate[section]
    nothing = jnp.zeros((tokens, rank), jnp.float32)
    left = jnp.concatenate(
        [
            jnp.concatenate([own_w, -own_rate * own_a], axis=1),
            jnp.concatenate([nothing, jnp.where(taken, own_a, 0.0)], axis=1),
        ],
        axis=0,
    )
    coef[...] = left.T.astype(jnp.bfloat16)
    pair = jnp.concatenate(
        [jnp.concatenate([own_w, nothing], axis=1), jnp.concatenate([nothing, own_a], axis=1)], axis=0
    ).T.astype(jnp.bfloat16)
    for l in range(layers):
        la = a_s[l].astype(jnp.float32)
        top = jnp.concatenate([nothing, jnp.where(l < section, la, 0.0)], axis=1)
        scaled = jnp.where(l <= section, own_rate, rate[l]) * la
        bottom = jnp.concatenate([jnp.where(l > section, w_s[l].astype(jnp.float32), 0.0), -scaled], axis=1)
        rhs = jnp.concatenate([top, bottom], axis=0).astype(jnp.bfloat16)
        mixing[:, l * wide : (l + 1) * wide] = dot_n(pair, rhs)


def run_layers(features, tokens_per, meta, z, square, gram):
    layers, _, tokens, wide = z.shape
    rank = wide // 2
    vmem = pl.BlockSpec(memory_space=pltpu.VMEM)
    return pl.pallas_call(
        functools.partial(layers_kernel, features, tokens_per),
        out_shape=(
            jax.ShapeDtypeStruct((wide, 2 * tokens), jnp.bfloat16),
            jax.ShapeDtypeStruct((wide, layers * wide), jnp.float32),
        ),
        in_specs=[pl.BlockSpec(memory_space=pltpu.SMEM), vmem, vmem, vmem],
        out_specs=(vmem, vmem),
        scratch_shapes=[
            pltpu.VMEM((layers, tokens, layers * rank), jnp.float32),
            pltpu.VMEM((layers, tokens, 1), jnp.float32),
            pltpu.VMEM((layers, tokens, rank), jnp.bfloat16),
            pltpu.VMEM((layers, tokens, rank), jnp.bfloat16),
            pltpu.VMEM((tokens, layers * rank), jnp.bfloat16),
        ],
        compiler_params=pltpu.CompilerParams(vmem_limit_bytes=32 * 2**20),
        name="layers",
    )(meta, z, square, gram)


def on_device(
    inputs, cotangent, micro_counts, bounds, holder_down, holder_up,
    master_down, master_up, moment_down, moment_up, second_down, second_up,
):
    replica_at = lax.axis_index("replica")
    section_at = lax.axis_index("section")
    layers = lax.axis_size("section")
    micros, per, features = inputs.shape[1:]
    slots, rank = holder_down.shape[2:4]
    tokens = micros * per
    first_layers = bounds[replica_at]
    layer_ids = jnp.arange(layers, dtype=jnp.int32)
    here = (first_layers[:-1] == layer_ids) & (first_layers[1:] > layer_ids)
    previous = jnp.concatenate([first_layers[:1], first_layers[:-2]])
    codes = jnp.where(here, 0, jnp.where(previous == layer_ids, 2, 1)).astype(jnp.int32)
    meta = jnp.concatenate([codes, section_at[None].astype(jnp.int32), micro_counts[replica_at][None]])

    hidden = inputs[0].reshape(tokens, features)
    last = cotangent[0].reshape(tokens, features)
    downs = holder_down[0, 0].reshape(slots * rank, features)
    ups = holder_up[0, 0].reshape(slots * rank, features)
    z = jnp.stack([dot_t(hidden, downs), dot_t(hidden, ups), dot_t(last, ups)]).astype(jnp.bfloat16)
    widened = hidden.astype(jnp.float32)
    square = jnp.sum(widened * widened, axis=1, keepdims=True)

    params = jnp.concatenate([master_down[0], master_up[0]], axis=0)
    moments = jnp.concatenate([moment_down[0], moment_up[0]], axis=0)
    seconds = jnp.concatenate([second_down[0], second_up[0]], axis=0)
    rows = lax.all_gather(params.astype(jnp.bfloat16), "section")
    z = lax.all_gather(z, "section")
    ups_rows = rows[:, rank:].reshape(layers * rank, -1)
    part = dot_t(rows[section_at], ups_rows)
    gram = lax.all_gather(lax.psum(part, plane).astype(jnp.bfloat16), "section")
    coef, mixing = run_layers(features, per, meta, z, square, gram)
    grads = dot_n(coef[:, :tokens], hidden) + dot_n(coef[:, tokens:], last)
    gradient = lax.psum_scatter(
        grads.astype(jnp.bfloat16), plane, scatter_dimension=1, tiled=True
    ).astype(jnp.float32)
    mixing = lax.psum(mixing, plane).astype(jnp.bfloat16)
    gradient = gradient + dot_n(mixing, rows.reshape(2 * layers * rank, -1))

    new_moments = beta_one * moments + (1.0 - beta_one) * gradient
    new_seconds = beta_two * seconds + (1.0 - beta_two) * gradient * gradient
    new_params = params - learn_rate * (
        new_moments / first_fix / (jnp.sqrt(new_seconds / second_fix) + adam_eps)
        + decay_rate * params
    )
    share = new_params.astype(jnp.bfloat16)
    after = lax.ppermute(share, "section", [(i, i - 1) for i in range(1, layers)])
    whole = lax.all_gather(jnp.stack([share, after]), plane, axis=2, tiled=True)
    whole = whole.reshape(2, 2, rank, features)
    first, end = first_layers[section_at], first_layers[section_at + 1]
    slot_zero = jnp.where(end > first, jnp.where(first == section_at, whole[0], whole[1]), 0)
    slot_one = jnp.where(end > first + 1, whole[1], 0)
    placed = jnp.stack([slot_zero, slot_one], axis=1)
    return (
        placed[0][None, None], placed[1][None, None],
        new_params[None, :rank], new_params[None, rank:],
        new_moments[None, :rank], new_moments[None, rank:],
        new_seconds[None, :rank], new_seconds[None, rank:],
    )


def solution(mesh):
    owned = P("section", None, ("replica", "tensor"))
    held = P("replica", "section", None, None, None)
    tokens = P("replica", None, "tensor", None)
    return jax.shard_map(
        on_device,
        mesh=mesh,
        in_specs=(tokens, tokens, P(), P(), held, held) + (owned,) * 6,
        out_specs=(held, held) + (owned,) * 6,
        check_vma=False,
    )
```

time: 1180 us -> 352 us (0.30)
  matrix products: 314 us -> 15.3 us
  waiting for transfers between devices: 395 us -> 116 us
  other arithmetic: 268 us -> 13.1 us
  blocking collectives: 0 us -> 173 us
  starting transfers between devices: 92.2 us -> 1.44 us
  local copies, waits for them, and re-layouts: 65.3 us -> 9.4 us
  loops' own time: 23.8 us -> 0 us
    dot_general x143 -> x7, matrix products: 314 us -> 15.3 us  [the longest x3 9 us: dot_n(): return jnp.dot(left, right, preferred_element_type=jnp.float32)]
    ppermute x24 -> x1, waiting for transfers between devices: 248 us -> 5.11 us  [on_device(): lax.ppermute(share, 'section', [(i, i - 1) for i in range(1, layers)])]
    psum x0 -> x2, blocking collectives: none -> 141 us  [the longest x1 73.9 us: on_device(): mixing = lax.psum(mixing, plane).astype(jnp.bfloat16)]
    add x11 -> x0, other arithmetic: 114 us -> none  [backward_tick(): return ((pass_along(leaving, -1), grads + added), None)]
    ppermute x24 -> x1, starting transfers between devices: 92.1 us -> 1.28 us  [on_device(): lax.ppermute(share, 'section', [(i, i - 1) for i in range(1, layers)])]
    reduce_scatter x1, waiting for transfers between devices: 93.6 us -> 3.77 us  [on_device(): lax.psum_scatter(grads.astype(jnp.bfloat16), plane, scatter_dimension=1,...]
    all_gather x1 -> x3, waiting for transfers between devices: 53.4 us -> 107 us  [the longest x1 59.5 us: on_device(): whole = lax.all_gather(jnp.stack([share, after]), plane, axis=2, tiled=True)]
    another operation x12 -> x4, other arithmetic: 50.3 us -> 2.86 us  [the longest x11 48.2 us: section_backward(): return (incoming, jnp.stack([jnp.stack(grads_down), jnp.stack(grads_up)]))]
  transfers between devices with their start and end apart: 26 -> 5, of which waited for: 15 -> 5; matrix products, arithmetic and copies ran while one was open for 21% -> 4% of each run, Pallas kernels for 0% -> 0%
where the time goes in v1:
time: 352 us
  blocking collectives  173 us (49%)
  waiting for transfers between devices  116 us (33%)
  between operations  17.2 us (5%)
  matrix products  15.3 us (4%)
  other arithmetic  13.1 us (4%)
  local copies, waits for them, and re-layouts  9.4 us (3%)
  Pallas kernels  6.03 us (2%)
    psum x1, blocking collectives, on_device(): mixing = lax.psum(mixing, plane).astype(jnp.bfloat16)  73.9 us
    psum x1, blocking collectives, on_device(): gram = lax.all_gather(lax.psum(part, plane).astype(jnp.bfloat16), 'section')  67.3 us
    all_gather x1, waiting for transfers between devices, on_device(): whole = lax.all_gather(jnp.stack([share, after]), plane, axis=2, tiled=True)  59.5 us
    all_gather x1, waiting for transfers between devices, on_device(): rows = lax.all_gather(params.astype(jnp.bfloat16), 'section')  41.3 us
    all_gather x1, blocking collectives, on_device(): z = lax.all_gather(z, 'section')  31.9 us
    dot_general x3, matrix products, dot_n(): return jnp.dot(left, right, preferred_element_type=jnp.float32)  9 us
  transfers between devices with their start and end apart: 5, of which 5 were waited for; matrix products, arithmetic and copies ran while one was open for 4% of the time, Pallas kernels for 0%

profile of v1, /device:TPU:1, one launch (start us, length us, event | category | flops | bytes accessed | tf_op | source)
XLA Modules:
  0.0 351.6 jit_solution(4133660809627213090)
XLA Ops:
  7.2 0.0 copy-start
  7.2 0.0 copy-start.8
  7.2 0.0 copy-start.7
  7.2 0.0 all-gather.5.cloned.1.call-start
  7.2 1.1 convert.21
  8.3 0.9 convert.22
  9.3 0.7 pad_maximum_fusion.3
  10.0 0.0 all-gather.5.cloned.1.call-update
  10.0 0.0 all-gather.9.cloned.1.call-start
  10.1 2.6 multiply_reduce_fusion
  12.7 0.1 broadcast_in_dim.53.square
  12.8 0.0 copy-done.8
  12.8 0.6 dynamic_slice.18
  13.4 0.0 copy-done.7
  13.4 0.1 and_select_fusion
  13.5 41.3 %all-gather.5.cloned.1.call-done = bf16[8,128,768]{2,1,0:T(8,128)(2,1)} async-done(((bf16[1,128,768]{2,1,0:T(8,128)(2,1)}), bf16[8,128,768]{2,1,0:T(8,128)(2,1)}) %all-gather.5.cloned.1.call-update) | async-done | bytes 1572880 | tf_op jit(solution)/shard_map/all_gather | solution.py:163
  54.8 1.2 slice.87
  56.0 1.3 fusion.11
  57.3 67.3 %all-reduce.2 = bf16[128,512]{1,0:T(8,128)(2,1)} all-reduce(f32[128,512]{1,0:T(8,128)S(1)} %fusion.11), channel_id=1, replica_groups=mesh['replica'=4,'section'=8,'tensor'=4] {'replica','tensor'}, use_global_device_ids=true, to_apply=%region_1.2 | all-reduce | flops 65536 | bytes 393216 | tf_op jit(solution)/shard_map/psum | solution.py:167
  124.6 0.0 all-gather.9.cloned.1.call-update
  124.6 0.0 reduce-scatter.2.cloned.1.call-start
  124.7 0.7 pad_add_fusion.meta
  125.4 0.0 copy-done
  125.4 0.0 copy-start.4
  125.4 0.0 copy-start.5
  125.4 3.0 fusion.7
  128.4 0.0 copy-done.4
  128.4 0.8 copy-done.5
  129.2 0.0 copy-start.6
  129.2 1.0 fusion.6
  130.2 0.9 copy-done.6
  131.1 1.0 fusion.5
  132.1 31.9 %all_gather.17.z = bf16[8,3,128,128]{3,2,1,0:T(8,128)(2,1)} all-gather(bf16[1,3,128,128]{3,2,1,0:T(8,128)(2,1)S(1)} %pad_maximum_fusion.4), channel_id=1, replica_groups=mesh['replica'=4,'section'=8,'tensor'=4] {'section'}, dimensions={0}, use_global_device_ids=true | all-gather | bytes 884736 | tf_op jit(solution)/shard_map/all_gather | solution.py:164
  164.0 6.4 %all-gather.9.cloned.1.call-done = bf16[1024,512]{1,0:T(8,128)(2,1)} async-done(((bf16[128,512]{1,0:T(8,128)(2,1)}), bf16[1024,512]{1,0:T(8,128)(2,1)}) %all-gather.9.cloned.1.call-update) | async-done | bytes 1048592 | tf_op jit(solution)/shard_map/all_gather | solution.py:167
  170.4 0.0 copy-start.1
  170.4 1.1 copy-done.1
  171.5 0.0 copy-start.2
  171.5 1.2 copy-done.2
  172.8 6.0 %layers.1 = (bf16[128,256]{1,0:T(8,128)(2,1)S(1)}, f32[128,1024]{1,0:T(8,128)S(1)}) custom-call(s32[10]{0:T(128)S(1)} %pad_add_fusion.meta, bf16[8,3,128,128]{3,2,1,0:T(8,128)(2,1)S(1)} %copy-done.1, f32[128,1]{1,0:T(8,128)S(1)} %broadcast_in_dim.53.square, bf16[8,128,512]{2,1,0:T(8,128)(2,1)S(1)} %bitcast.70), custom_call_target="tpu_custom_call" | custom-call | tf_op jit(solution)/shard_map/layers/pallas_call | solution.py:115
  178.8 0.0 copy-start.3
  178.8 3.0 fusion.15
  181.8 0.0 copy-done.3
  181.9 2.6 fusion
  184.5 0.0 reduce-scatter.2.cloned.1.call-update
  184.5 0.0 all-gather.7.cloned.1.call-start
  184.6 73.9 %all-reduce.3 = bf16[128,1024]{1,0:T(8,128)(2,1)} all-reduce(f32[128,1024]{1,0:T(8,128)} %copy-done.3), channel_id=1, replica_groups=mesh['replica'=4,'section'=8,'tensor'=4] {'replica','tensor'}, use_global_device_ids=true, to_apply=%region_3.4 | all-reduce | flops 131072 | bytes 786432 | tf_op jit(solution)/shard_map/psum | solution.py:173
  258.5 3.8 %reduce-scatter.2.cloned.1.call-done = bf16[128,768]{1,0:T(8,128)(2,1)} async-done(((bf16[128,12288]{1,0:T(8,128)(2,1)}), bf16[128,768]{1,0:T(8,128)(2,1)}) %reduce-scatter.2.cloned.1.call-update) | async-done | bytes 196624 | tf_op jit(solution)/shard_map/reduce_scatter | solution.py:170
  262.3 3.3 fusion.18
  265.6 1.3 collective-permute-start
  266.9 5.1 %collective-permute-done = bf16[128,768]{1,0:T(8,128)(2,1)S(1)} collective-permute-done((bf16[128,768]{1,0:T(8,128)(2,1)S(1)}, bf16[128,768]{1,0:T(8,128)(2,1)S(1)}, u32[]{:S(2)}, u32[]{:S(2)}) %collective-permute-start) | collective-permute-done | bytes 196640 | tf_op jit(solution)/shard_map/ppermute | solution.py:183
  272.0 0.8 pad_maximum_fusion.2
  272.8 0.0 all-gather.7.cloned.1.call-update
  272.8 0.6 fusion.21
  276.7 0.8 slice_bitcast_fusion.4
  277.4 2.1 slice_bitcast_fusion
  279.5 59.5 %all-gather.7.cloned.1.call-done = bf16[2,128,12288]{2,1,0:T(8,128)(2,1)} async-done(((bf16[2,128,768]{2,1,0:T(8,128)(2,1)}), bf16[2,128,12288]{2,1,0:T(8,128)(2,1)}) %all-gather.7.cloned.1.call-update) | async-done | bytes 6291472 | tf_op jit(solution)/shard_map/all_gather | solution.py:184
  339.0 3.1 broadcast_select_fusion
  342.1 3.0 fusion.3
  (3 shorter events, 0.0 us)
Async XLA Ops:
  7.2 118.2 %copy-start = (bf16[1,4,32,12288]{3,2,1,0:T(8,128)(2,1)S(1)}, bf16[1,4,32,12288]{3,2,1,0:T(8,128)(2,1)}, u32[]{:S(2)}) copy-start(bf16[1,4,32,12288]{3,2,1,0:T(8,128)(2,1)} %param.13) | copy-start | bytes 9437188
  7.2 5.6 %copy-start.8 = (s32[4]{0:T(128)S(1)}, s32[4]{0:T(128)}, u32[]{:S(2)}) copy-start(s32[4]{0:T(128)} %param.14) | copy-start | bytes 52
  7.2 6.2 %copy-start.7 = (s32[4,9]{1,0:T(4,128)S(1)}, s32[4,9]{1,0:T(4,128)}, u32[]{:S(2)}) copy-start(s32[4,9]{1,0:T(4,128)} %param.15) | copy-start | bytes 436
  7.2 47.6 %all-gather.5.cloned.1.call-start = ((), (), s32[]{:S(2)}) async-start(), calls=%async_computation.1 | async-start | bytes 1769472 | tf_op jit(solution)/shard_map/all_gather | solution.py:163
  10.0 160.4 %all-gather.9.cloned.1.call-start = ((), (), s32[]{:S(2)}) async-start(), calls=%async_computation.4 | async-start | bytes 1179648 | tf_op jit(solution)/shard_map/all_gather | solution.py:167
  124.6 137.6 %reduce-scatter.2.cloned.1.call-start = ((), (), s32[]{:S(2)}) async-start(), calls=%async_computation.2 | async-start | bytes 3342336 | tf_op jit(solution)/shard_map/reduce_scatter | solution.py:170
  125.4 3.0 copy-start.4
  125.4 3.8 %copy-start.5 = (bf16[1,1,2,64,12288]{4,3,2,1,0:T(8,128)(2,1)S(1)}, bf16[1,1,2,64,12288]{4,3,2,1,0:T(8,128)(2,1)}, u32[]{:S(2)}) copy-start(bf16[1,1,2,64,12288]{4,3,2,1,0:T(8,128)(2,1)} %param.17) | copy-start | bytes 9437188
  129.2 1.9 copy-start.6
  170.4 1.1 copy-start.1
  171.5 1.2 copy-start.2
  178.8 3.1 copy-start.3
  184.5 154.5 %all-gather.7.cloned.1.call-start = ((), (), s32[]{:S(2)}) async-start(), calls=%async_computation.3 | async-start | bytes 6684672 | tf_op jit(solution)/shard_map/all_gather | solution.py:184
  265.6 6.4 %collective-permute-start = (bf16[128,768]{1,0:T(8,128)(2,1)S(1)}, bf16[128,768]{1,0:T(8,128)(2,1)S(1)}, u32[]{:S(2)}, u32[]{:S(2)}) collective-permute-start(bf16[128,768]{1,0:T(8,128)(2,1)S(1)} %get-tuple-element.12), channel_id=1, source_target_pairs={{4,0},{8,4},{12,8},{16,12},{20,16},{24,20},{28,24},{5,1},{9,5},{13... | collective-permute-start | bytes 589832 | tf_op jit(solution)/shard_map/ppermute | solution.py:183
Sparse Core Ops, SparseCore 0:
  10.3 44.5 all-gather.4
  124.8 45.5 all-gather.8
  184.6 77.5 reduce-scatter.1
  272.9 66.0 all-gather.6

commit v2 on v1

--- a/solution.py
+++ b/solution.py
@@ -16,7 +16,6 @@
 adam_eps = 1e-08
 first_fix = 0.9999734386011124
 second_fix = 0.9940794707796659
-plane = ("replica", "tensor")
 
 
 def dot_t(left, right):
@@ -96,16 +95,19 @@
         axis=0,
     )
     coef[...] = left.T.astype(jnp.bfloat16)
-    pair = jnp.concatenate(
-        [jnp.concatenate([own_w, nothing], axis=1), jnp.concatenate([nothing, own_a], axis=1)], axis=0
-    ).T.astype(jnp.bfloat16)
-    for l in range(layers):
-        la = a_s[l].astype(jnp.float32)
-        top = jnp.concatenate([nothing, jnp.where(l < section, la, 0.0)], axis=1)
-        scaled = jnp.where(l <= section, own_rate, rate[l]) * la
-        bottom = jnp.concatenate([jnp.where(l > section, w_s[l].astype(jnp.float32), 0.0), -scaled], axis=1)
-        rhs = jnp.concatenate([top, bottom], axis=0).astype(jnp.bfloat16)
-        mixing[:, l * wide : (l + 1) * wide] = dot_n(pair, rhs)
+    own_left = own_a.T.astype(jnp.bfloat16)
+    own_down = own_w.T.astype(jnp.bfloat16)
+    before = jnp.concatenate([jnp.where(l < section, a_s[l], jnp.zeros_like(a_s[l])) for l in range(layers)], axis=1)
+    beyond = jnp.concatenate([jnp.where(l > section, w_s[l], jnp.zeros_like(w_s[l])) for l in range(layers)], axis=1)
+    scaled = jnp.concatenate(
+        [
+            (jnp.where(l <= section, own_rate, rate[l]) * a_s[l].astype(jnp.float32)).astype(jnp.bfloat16)
+            for l in range(layers)
+        ],
+        axis=1,
+    )
+    mixing[:rank] = (dot_n(own_down, before) + dot_n(own_left, beyond)).astype(jnp.bfloat16)
+    mixing[rank:] = (-dot_n(own_left, scaled)).astype(jnp.bfloat16)
 
 
 def run_layers(features, tokens_per, meta, z, square, gram):
@@ -116,7 +118,7 @@
         functools.partial(layers_kernel, features, tokens_per),
         out_shape=(
             jax.ShapeDtypeStruct((wide, 2 * tokens), jnp.bfloat16),
-            jax.ShapeDtypeStruct((wide, layers * wide), jnp.float32),
+            jax.ShapeDtypeStruct((wide, layers * rank), jnp.bfloat16),
         ),
         in_specs=[pl.BlockSpec(memory_space=pltpu.SMEM), vmem, vmem, vmem],
         out_specs=(vmem, vmem),
@@ -130,6 +132,331 @@
         compiler_params=pltpu.CompilerParams(vmem_limit_bytes=32 * 2**20),
         name="layers",
     )(meta, z, square, gram)
+
+
+MESH = pl.DeviceIdType.MESH
+
+
+def place():
+    tensor = lax.axis_index("tensor")
+    return lax.axis_index("replica"), lax.axis_index("section"), tensor // 2, tensor % 2
+
+
+def remote(source, target, sems, at, device):
+    return pltpu.make_async_remote_copy(
+        src_ref=source, dst_ref=target, send_sem=sems[0].at[at], recv_sem=sems[1].at[at],
+        device_id=device, device_id_type=MESH,
+    )
+
+
+def greet(devices):
+    barrier = pltpu.get_barrier_semaphore()
+    for device in devices:
+        pl.semaphore_signal(barrier, inc=1, device_id=device, device_id_type=MESH)
+    pl.semaphore_wait(barrier, len(devices))
+
+
+def section_peers(replica, section, chip, core, sections):
+    return [(replica, lax.rem(section + d, sections), chip * 2 + core) for d in range(1, sections)]
+
+
+def plane_peers(replica, section, chip, core, replicas):
+    found = []
+    for dr in range(replicas):
+        for dz in range(2):
+            for dc in range(2):
+                if dr or dz or dc:
+                    there = lax.rem(replica + dr, replicas)
+                    tensor = lax.rem(chip + dz, 2) * 2 + lax.rem(core + dc, 2)
+                    found.append(((there, section, tensor), there * 4 + tensor))
+    return found
+
+
+def plane_sum(pieces, box, sems, me, peers):
+    copies = []
+    for i, (device, number) in enumerate(peers):
+        copy = remote(pieces.at[number], box.at[me], sems, i, device)
+        copy.start()
+        copies.append(copy)
+    box[me] = pieces[me]
+    for copy in copies:
+        copy.wait()
+    total = box[0].astype(jnp.float32)
+    for i in range(1, box.shape[0]):
+        total = total + box[i].astype(jnp.float32)
+    return total
+
+
+def cut(value, pieces):
+    _, height, width = pieces.shape
+    across = value.shape[1] // width
+    for i in range(pieces.shape[0]):
+        y, x = i // across * height, i % across * width
+        pieces[i] = value[y : y + height, x : x + width].astype(pieces.dtype)
+
+
+def collect_kernel(replicas, sections, mine, z, rows, zs, gram, pieces, box, spread, *sems):
+    replica, section, chip, core = place()
+    row_sems, z_sems, sum_sems, piece_sems, plane_sems, core_sems = (sems[2 * i : 2 * i + 2] for i in range(6))
+    me = replica * 4 + chip * 2 + core
+    along = section_peers(replica, section, chip, core, sections)
+    peers = plane_peers(replica, section, chip, core, replicas)
+    greet(along + [device for device, _ in peers])
+    rank = rows.shape[1]
+    row_copies, z_copies = [], []
+    for i, device in enumerate(along):
+        row_copies.append(remote(mine.at[pl.ds(rank, rank)], rows.at[section], row_sems, i, device))
+        row_copies[-1].start()
+    for i, device in enumerate(along):
+        z_copies.append(remote(z, zs.at[section], z_sems, i, device))
+        z_copies[-1].start()
+    rows[section] = mine[rank:]
+    zs[section] = z[...]
+    for copy in row_copies:
+        copy.wait()
+    part = dot_t(mine[...], rows[...].reshape(sections * rank, -1))
+    cut(part, pieces)
+    total = plane_sum(pieces, box, sum_sems, me, peers)
+    spread[me, section] = total.astype(spread.dtype)
+    copies = []
+    for i, device in enumerate(along):
+        copies.append(remote(spread.at[me, section], spread.at[me, section], piece_sems, i, device))
+        copies[-1].start()
+    for copy in copies:
+        copy.wait()
+    sibling = (replica, section, chip * 2 + 1 - core)
+    same = [(device, number, i) for i, (device, number) in enumerate(peers) if i % 2 == 1]
+    copies = []
+    for i, (device, number, _) in enumerate(same):
+        copies.append(remote(spread.at[me], spread.at[me], plane_sems, i, device))
+        copies[-1].start()
+    swaps = [remote(spread.at[me], spread.at[me], core_sems, 7, sibling)]
+    swaps[0].start()
+    for i, copy in enumerate(copies):
+        copy.wait_recv()
+        dr, dz = (i + 1) // 2, (i + 1) % 2
+        source = lax.rem(replica + replicas - dr, replicas) * 4 + lax.rem(chip + dz, 2) * 2 + core
+        swaps.append(remote(spread.at[source], spread.at[source], core_sems, i, sibling))
+        swaps[-1].start()
+    for copy in copies:
+        copy.wait_send()
+    for copy in swaps:
+        copy.wait()
+    _, _, height, width = spread.shape
+    across = gram.shape[2] // width
+    for i in range(spread.shape[0]):
+        y, x = i // across * height, i % across * width
+        gram[:, y : y + height, x : x + width] = spread[i]
+    for copy in z_copies:
+        copy.wait()
+
+
+def dma_pairs(counts):
+    return [pltpu.SemaphoreType.DMA((n,)) for n in counts for _ in range(2)]
+
+
+def collect(mine, z):
+    replicas, sections = lax.axis_size("replica"), lax.axis_size("section")
+    wide, columns = mine.shape
+    rank = wide // 2
+    size = replicas * 4
+    vmem = pl.BlockSpec(memory_space=pltpu.VMEM)
+    height, width = 16, wide * sections * rank // size // 16
+    return pl.pallas_call(
+        functools.partial(collect_kernel, replicas, sections),
+        out_shape=(
+            jax.ShapeDtypeStruct((sections, rank, columns), jnp.bfloat16),
+            jax.ShapeDtypeStruct((sections,) + z.shape, jnp.bfloat16),
+            jax.ShapeDtypeStruct((sections, wide, sections * rank), jnp.bfloat16),
+        ),
+        in_specs=[vmem, vmem],
+        out_specs=(vmem, vmem, vmem),
+        scratch_shapes=[
+            pltpu.VMEM((size, height, width), jnp.bfloat16),
+            pltpu.VMEM((size, height, width), jnp.bfloat16),
+            pltpu.VMEM((size, sections, height, width), jnp.bfloat16),
+        ] + dma_pairs((sections - 1, sections - 1, size - 1, sections - 1, size // 2 - 1, size // 2)),
+        compiler_params=pltpu.CompilerParams(collective_id=1, has_side_effects=True, vmem_limit_bytes=40 * 2**20),
+        name="collect",
+    )(mine, z)
+
+
+def reduce_kernel(
+    replicas, sections, grads, mixing, mine, out, mixed, rows, half, chips, inbox, pieces, box, spread, *sems
+):
+    replica, section, chip, core = place()
+    half_sems, chip_sems, row_sems, sum_sems, spread_sems = (sems[2 * i : 2 * i + 2] for i in range(5))
+    me = replica * 4 + chip * 2 + core
+    along = section_peers(replica, section, chip, core, sections)
+    peers = plane_peers(replica, section, chip, core, replicas)
+    greet(along + [device for device, _ in peers])
+    sibling = (replica, section, chip * 2 + 1 - core)
+    columns = out.shape[1]
+    order = [(2, 1), (2, 0), (1, 1), (3, 1), (1, 0), (3, 0), (0, 1), (0, 0)]
+    there = [(lax.rem(replica + dr, replicas), lax.rem(chip + dz, 2)) for dr, dz in order]
+
+    def block(r, z, c):
+        return pl.ds(pl.multiple_of((r * 4 + z * 2 + c) * columns, 128), columns)
+
+    halves = []
+    for i, (r, z) in enumerate(there):
+        halves.append(remote(grads.at[:, block(r, z, 1 - core)], half.at[i], half_sems, i, sibling))
+        halves[-1].start()
+    cut(mixing[...], pieces)
+    small = []
+    for i, (device, number) in enumerate(peers):
+        small.append(remote(pieces.at[number], box.at[me], sum_sems, i, device))
+        small[-1].start()
+    box[me] = pieces[me]
+    row_copies = []
+    for i, device in enumerate(along):
+        row_copies.append(remote(mine.at[pl.ds(0, mine.shape[0] // 2)], rows.at[section], row_sems, i, device))
+        row_copies[-1].start()
+    rows[section] = mine[: mine.shape[0] // 2]
+    sends = []
+    for i, (r, z) in enumerate(there):
+        halves[i].wait()
+        chips[i] = (
+            grads[:, block(r, z, core)].astype(jnp.float32) + half[i].astype(jnp.float32)
+        ).astype(chips.dtype)
+        if i < len(there) - 1:
+            sends.append(remote(chips.at[i], inbox.at[i], chip_sems, i, (r, section, z * 2 + core)))
+            sends[-1].start()
+    for copy in small:
+        copy.wait()
+    total = box[0].astype(jnp.float32)
+    for i in range(1, box.shape[0]):
+        total = total + box[i].astype(jnp.float32)
+    spread[me] = total.astype(spread.dtype)
+    small = []
+    for i, (device, number) in enumerate(peers):
+        small.append(remote(spread.at[me], spread.at[me], spread_sems, i, device))
+        small[-1].start()
+    out[...] = chips[len(there) - 1].astype(jnp.float32)
+    for i, copy in enumerate(sends):
+        copy.wait()
+        out[...] += inbox[i].astype(jnp.float32)
+    for copy in small:
+        copy.wait()
+    _, height, width = spread.shape
+    across = mixed.shape[1] // width
+    for i in range(spread.shape[0]):
+        y, x = i // across * height, i % across * width
+        mixed[y : y + height, x : x + width] = spread[i]
+    for copy in row_copies:
+        copy.wait()
+
+
+def reduce(grads, mixing, mine):
+    replicas, sections = lax.axis_size("replica"), lax.axis_size("section")
+    size = replicas * 4
+    wide, columns = mine.shape
+    height, width = 16, mixing.size // size // 16
+    vmem = pl.BlockSpec(memory_space=pltpu.VMEM)
+    block = (size // 2, wide, columns)
+    return pl.pallas_call(
+        functools.partial(reduce_kernel, replicas, sections),
+        out_shape=(
+            jax.ShapeDtypeStruct((wide, columns), jnp.float32),
+            jax.ShapeDtypeStruct(mixing.shape, jnp.bfloat16),
+            jax.ShapeDtypeStruct((sections, wide // 2, columns), jnp.bfloat16),
+        ),
+        in_specs=[vmem] * 3,
+        out_specs=(vmem,) * 3,
+        scratch_shapes=[pltpu.VMEM(block, jnp.bfloat16)] * 3 + [pltpu.VMEM((size, height, width), jnp.bfloat16)] * 3
+        + dma_pairs((size // 2, size // 2 - 1, sections - 1, size - 1, size - 1)),
+        compiler_params=pltpu.CompilerParams(collective_id=2, has_side_effects=True, vmem_limit_bytes=40 * 2**20),
+        name="reduce",
+    )(grads, mixing, mine)
+
+
+def publish_kernel(replicas, sections, share, out, shift_send, shift_recv, *sems):
+    replica, section, chip, core = place()
+    far_sems, core_sems = sems[:2], sems[2:]
+    columns = share.shape[1]
+    before = lax.rem(section + sections - 1, sections)
+    after = lax.rem(section + 1, sections)
+    other = 1 - chip
+    up, down, across = (lax.rem(replica + d, replicas) for d in (1, replicas - 1, 2))
+    tensor = chip * 2 + core
+    here = (replica, section, tensor)
+    sibling = (replica, section, chip * 2 + 1 - core)
+    partner = (replica, section, other * 2 + core)
+    above, below = (up, section, tensor), (down, section, tensor)
+    greet([(replica, before, tensor), (replica, after, tensor), sibling, partner, above, below])
+
+    def block(window, r, z):
+        return out.at[window, :, pl.ds(pl.multiple_of((r * 4 + z * 2 + core) * columns, 128), columns)]
+
+    started = {}
+    def send(window, kind, r, z, device):
+        copy = remote(block(window, r, z), block(window, r, z), far_sems, window * 7 + kind, device)
+        copy.start()
+        started[window, kind] = copy
+
+    swaps = []
+
+    def swap(window, r, z):
+        number = len(swaps)
+        copy = remote(block(window, r, z), block(window, r, z), core_sems, number, sibling)
+        copy.start()
+        swaps.append(copy)
+
+    own = pl.ds(pl.multiple_of((replica * 4 + tensor) * columns, 128), columns)
+    shift = pltpu.make_async_remote_copy(
+        src_ref=share, dst_ref=out.at[1, :, own], send_sem=shift_send, recv_sem=shift_recv,
+        device_id=(replica, before, tensor), device_id_type=MESH,
+    )
+    shift.start()
+    out[0, :, own] = share[...]
+    for window in range(2):
+        if window:
+            shift.wait()
+        send(window, 0, replica, chip, partner)
+        send(window, 1, replica, chip, above)
+        send(window, 3, replica, chip, below)
+        swap(window, replica, chip)
+    for window in range(2):
+        started[window, 0].wait_recv()
+        send(window, 2, replica, other, above)
+        send(window, 4, replica, other, below)
+        swap(window, replica, other)
+    for window in range(2):
+        started[window, 1].wait_recv()
+        send(window, 5, down, chip, above)
+        swap(window, down, chip)
+        started[window, 3].wait_recv()
+        swap(window, up, chip)
+    for window in range(2):
+        started[window, 4].wait_recv()
+        send(window, 6, up, other, below)
+        swap(window, up, other)
+        started[window, 2].wait_recv()
+        swap(window, down, other)
+    for window in range(2):
+        started[window, 5].wait_recv()
+        swap(window, across, chip)
+        started[window, 6].wait_recv()
+        swap(window, across, other)
+    for copy in started.values():
+        copy.wait_send()
+    for copy in swaps:
+        copy.wait()
+
+
+def publish(share):
+    replicas, sections = lax.axis_size("replica"), lax.axis_size("section")
+    wide, columns = share.shape
+    vmem = pl.BlockSpec(memory_space=pltpu.VMEM)
+    return pl.pallas_call(
+        functools.partial(publish_kernel, replicas, sections),
+        out_shape=jax.ShapeDtypeStruct((2, wide, columns * replicas * 4), jnp.bfloat16),
+        in_specs=[vmem],
+        out_specs=vmem,
+        scratch_shapes=[pltpu.SemaphoreType.DMA, pltpu.SemaphoreType.DMA] + dma_pairs((14, 16)),
+        compiler_params=pltpu.CompilerParams(collective_id=3, has_side_effects=True, vmem_limit_bytes=40 * 2**20),
+        name="publish",
+    )(share)
 
 
 def on_device(
@@ -160,18 +487,19 @@
     params = jnp.concatenate([master_down[0], master_up[0]], axis=0)
     moments = jnp.concatenate([moment_down[0], moment_up[0]], axis=0)
     seconds = jnp.concatenate([second_down[0], second_up[0]], axis=0)
-    rows = lax.all_gather(params.astype(jnp.bfloat16), "section")
-    z = lax.all_gather(z, "section")
-    ups_rows = rows[:, rank:].reshape(layers * rank, -1)
-    part = dot_t(rows[section_at], ups_rows)
-    gram = lax.all_gather(lax.psum(part, plane).astype(jnp.bfloat16), "section")
+    mine = params.astype(jnp.bfloat16)
+    ups_rows, z, gram = collect(mine, z)
     coef, mixing = run_layers(features, per, meta, z, square, gram)
     grads = dot_n(coef[:, :tokens], hidden) + dot_n(coef[:, tokens:], last)
-    gradient = lax.psum_scatter(
-        grads.astype(jnp.bfloat16), plane, scatter_dimension=1, tiled=True
-    ).astype(jnp.float32)
-    mixing = lax.psum(mixing, plane).astype(jnp.bfloat16)
-    gradient = gradient + dot_n(mixing, rows.reshape(2 * layers * rank, -1))
+    gradient, mixed, downs_rows = reduce(grads.astype(jnp.bfloat16), mixing, mine)
+    column_layer = jnp.arange(layers * rank, dtype=jnp.int32)[None] // rank
+    crossing = mixed[:rank]
+    ups_rows = ups_rows.reshape(layers * rank, -1)
+    downs_rows = downs_rows.reshape(layers * rank, -1)
+    nothing = jnp.zeros_like(crossing)
+    from_ups = jnp.concatenate([jnp.where(column_layer < section_at, crossing, nothing), mixed[rank:]], axis=0)
+    from_downs = jnp.concatenate([nothing, jnp.where(column_layer > section_at, crossing, nothing)], axis=0)
+    gradient = gradient + dot_n(from_ups, ups_rows) + dot_n(from_downs, downs_rows)
 
     new_moments = beta_one * moments + (1.0 - beta_one) * gradient
     new_seconds = beta_two * seconds + (1.0 - beta_two) * gradient * gradient
@@ -180,9 +508,7 @@
         + decay_rate * params
     )
     share = new_params.astype(jnp.bfloat16)
-    after = lax.ppermute(share, "section", [(i, i - 1) for i in range(1, layers)])
-    whole = lax.all_gather(jnp.stack([share, after]), plane, axis=2, tiled=True)
-    whole = whole.reshape(2, 2, rank, features)
+    whole = publish(share).reshape(2, 2, rank, features)
     first, end = first_layers[section_at], first_layers[section_at + 1]
     slot_zero = jnp.where(end > first, jnp.where(first == section_at, whole[0], whole[1]), 0)
     slot_one = jnp.where(end > first + 1, whole[1], 0)

time: 352 us -> 149 us (0.42)
  blocking collectives: 173 us -> 0 us
  waiting for transfers between devices: 116 us -> 0 us
  Pallas kernels: 6.03 us -> 121 us
  between operations: 17.2 us -> 4.12 us
  matrix products: 15.3 us -> 7.53 us
  other arithmetic: 13.1 us -> 7.91 us
    psum x2 -> x0, blocking collectives: 141 us -> none  [the longest x1 73.9 us: on_device(): mixing = lax.psum(mixing, plane).astype(jnp.bfloat16)]
    pallas_call x0 -> x3, Pallas kernels: none -> 115 us  [the longest x1 45.4 us: collect(): pl.pallas_call(functools.partial(collect_kernel, replicas, sections), out...]
    all_gather x3 -> x0, waiting for transfers between devices: 107 us -> none  [the longest x1 59.5 us: on_device(): whole = lax.all_gather(jnp.stack([share, after]), plane, axis=2, tiled=True)]
    all_gather x1 -> x0, blocking collectives: 31.9 us -> none  [on_device(): z = lax.all_gather(z, 'section')]
    ppermute x1 -> x0, waiting for transfers between devices: 5.11 us -> none  [on_device(): lax.ppermute(share, 'section', [(i, i - 1) for i in range(1, layers)])]
    dot_general x3 -> x4, matrix products: 9 us -> 4.61 us  [dot_n(): return jnp.dot(left, right, preferred_element_type=jnp.float32)]
    reduce_scatter x1 -> x0, waiting for transfers between devices: 3.77 us -> none  [on_device(): lax.psum_scatter(grads.astype(jnp.bfloat16), plane, scatter_dimension=1,...]
  transfers between devices with their start and end apart: 5 -> 0, of which waited for: 5 -> 0; matrix products, arithmetic and copies ran while one was open for 4% -> 0% of each run, Pallas kernels for 0% -> 0%
where the time goes in v2:
time: 149 us
  Pallas kernels  121 us (81%)
  other arithmetic  7.91 us (5%)
  local copies, waits for them, and re-layouts  7.85 us (5%)
  matrix products  7.53 us (5%)
  between operations  4.12 us (3%)
    pallas_call x1, Pallas kernels, collect(): pl.pallas_call(functools.partial(collect_kernel, replicas, sections), out...  45.4 us
    pallas_call x1, Pallas kernels, publish(): pl.pallas_call(functools.partial(publish_kernel, replicas, sections), out...  35.1 us
    pallas_call x1, Pallas kernels, reduce(): pl.pallas_call(functools.partial(reduce_kernel, replicas, sections), out_...  35 us
    pallas_call x1, Pallas kernels, run_layers(): pl.pallas_call(functools.partial(layers_kernel, features, tokens_per), ou...  5.89 us
    dot_general x4, matrix products, dot_n(): return jnp.dot(left, right, preferred_element_type=jnp.float32)  4.61 us
    another operation x1, other arithmetic, on_device(): placed[1][None, None]  2.99 us

profile of v2, /device:TPU:1, one launch (start us, length us, event | category | flops | bytes accessed | tf_op | source)
XLA Modules:
  0.0 148.8 jit_solution(2211716185891471868)
XLA Ops:
  0.6 0.0 copy-start
  0.7 1.4 fusion.27
  5.4 0.0 copy-start.2
  5.4 1.4 dynamic_slice.15
  6.8 0.7 constant_dynamic-slice_fusion
  7.4 0.0 copy-done
  7.5 0.1 and_select_fusion
  7.6 0.7 pad_add_fusion.meta
  8.3 2.6 %multiply_reduce_fusion = f32[4,32]{1,0:T(4,128)S(1)} fusion(bf16[1,4,32,12288]{3,2,1,0:T(8,128)(2,1)} %param.12), kind=kLoop, calls=%fused_computation.4 | loop fusion | flops 4718464 | bytes 3146240 | tf_op jit(solution)/shard_map/reduce_sum | solution.py:485
  10.9 0.0 copy-done.2
  10.9 0.0 copy-start.1
  10.9 0.0 copy-start.3
  10.9 1.0 fusion.6
  11.9 0.9 copy-done.1
  12.8 1.0 copy-done.3
  13.8 1.0 fusion.4
  14.7 0.0 copy-start.4
  14.8 1.0 fusion.5
  15.8 0.1 broadcast_in_dim.73.square
  15.9 0.0 copy-done.4
  15.9 1.0 fusion.9.mine
  16.8 45.4 %collect.1 = (bf16[8,64,768]{2,1,0:T(8,128)(2,1)S(1)}, bf16[8,3,128,128]{3,2,1,0:T(8,128)(2,1)S(1)}, bf16[8,128,512]{2,1,0:T(8,128)(2,1)S(1)}) custom-call(bf16[128,768]{1,0:T(8,128)(2,1)S(1)} %fusion.9.mine, bf16[3,128,128]{2,1,0:T(8,128)(2,1)S(1)} %pad_maximum_fusion.2.z), custom_call_target="tpu_custom_call" | custom-call | tf_op jit(solution)/shard_map/collect/pallas_call | solution.py:265
  62.2 5.9 %layers.1 = (bf16[128,256]{1,0:T(8,128)(2,1)S(1)}, bf16[128,512]{1,0:T(8,128)(2,1)S(1)}) custom-call(s32[10]{0:T(128)S(1)} %pad_add_fusion.meta, bf16[8,3,128,128]{3,2,1,0:T(8,128)(2,1)S(1)} %get-tuple-element.16.z, f32[128,1]{1,0:T(8,128)S(1)} %broadcast_in_dim.73.square, bf16[8,128,512]{2,1,0:T(8,128)(2,1)S(1)} %get-tuple-element.17.gram), custom_call_target="tpu_custom_call" | custom-call | tf_op jit(solution)/shard_map/layers/pallas_call | solution.py:117
  68.1 2.9 %fusion.15 = f32[128,12288]{1,0:T(8,128)S(1)} fusion(bf16[128,12288]{1,0:T(8,128)(2,1)} %bitcast.65, bf16[128,256]{1,0:T(8,128)(2,1)S(1)} %get-tuple-element.18), kind=kOutput, calls=%fused_computation.41 | convolution fusion | flops 402653184 | bytes 9469952 | tf_op jit(solution)/shard_map/dot_general | solution.py:28
  71.0 1.0 fusion.grads
  71.9 0.0 copy-start.5
  72.0 0.0 copy-start.6
  72.0 0.0 copy-start.7
  72.0 0.0 copy-start.8
  72.0 0.0 copy-start.9
  72.0 35.0 %reduce.2 = (f32[128,768]{1,0:T(8,128)S(1)}, bf16[128,512]{1,0:T(8,128)(2,1)S(1)}, bf16[8,64,768]{2,1,0:T(8,128)(2,1)S(1)}) custom-call(bf16[128,12288]{1,0:T(8,128)(2,1)S(1)} %fusion.grads, bf16[128,512]{1,0:T(8,128)(2,1)S(1)} %get-tuple-element.19.mixing, bf16[128,768]{1,0:T(8,128)(2,1)S(1)} %fusion.9.mine), custom_call_target="tpu_custom_call" | custom-call | tf_op jit(solution)/shard_map/reduce/pallas_call | solution.py:357
  107.0 0.3 convolution_add_fusion.2
  107.3 0.0 copy-done.5
  107.3 0.0 copy-done.6
  107.3 0.0 copy-done.7
  107.3 0.0 copy-done.8
  107.3 0.0 copy-done.9
  107.4 0.5 fusion.24
  107.9 0.8 slice_bitcast_fusion.4
  108.6 0.8 slice_bitcast_fusion.2
  109.4 0.8 slice_bitcast_fusion
  110.2 35.1 %publish.1 = bf16[2,128,12288]{2,1,0:T(8,128)(2,1)S(1)} custom-call(bf16[128,768]{1,0:T(8,128)(2,1)S(1)} %get-tuple-element.24.share), custom_call_target="tpu_custom_call" | custom-call | tf_op jit(solution)/shard_map/publish/pallas_call | solution.py:451
  145.3 0.5 broadcast_select_fusion
  145.8 3.0 %fusion.3 = (bf16[1,1,2,64,12288]{4,3,2,1,0:T(8,128)(2,1)}, bf16[1,1,2,64,12288]{4,3,2,1,0:T(8,128)(2,1)}) fusion(bf16[2,1,64,12288]{3,2,1,0:T(8,128)(2,1)S(1)} %bitcast.70, bf16[2,1,64,12288]{3,2,1,0:T(8,128)(2,1)S(1)} %bitcast.71), kind=kLoop, calls=%fused_computation.8 | loop fusion | flops 3145728 | bytes 12582912 | tf_op jit(solution)/shard_map/broadcast_in_dim;squeeze | solution.py:517
  (4 shorter events, 0.0 us)
Async XLA Ops:
  0.6 6.8 %copy-start = (bf16[1,4,32,12288]{3,2,1,0:T(8,128)(2,1)S(1)}, bf16[1,4,32,12288]{3,2,1,0:T(8,128)(2,1)}, u32[]{:S(2)}) copy-start(bf16[1,4,32,12288]{3,2,1,0:T(8,128)(2,1)} %param.13) | copy-start | bytes 9437188
  5.4 5.6 %copy-start.2 = (bf16[1,1,2,64,12288]{4,3,2,1,0:T(8,128)(2,1)S(1)}, bf16[1,1,2,64,12288]{4,3,2,1,0:T(8,128)(2,1)}, u32[]{:S(2)}) copy-start(bf16[1,1,2,64,12288]{4,3,2,1,0:T(8,128)(2,1)} %param.17) | copy-start | bytes 9437188
  10.9 1.9 %copy-start.1 = (bf16[1,4,32,12288]{3,2,1,0:T(8,128)(2,1)S(1)}, bf16[1,4,32,12288]{3,2,1,0:T(8,128)(2,1)}, u32[]{:S(2)}) copy-start(bf16[1,4,32,12288]{3,2,1,0:T(8,128)(2,1)} %param.12) | copy-start | bytes 9437188
  10.9 2.8 %copy-start.3 = (bf16[1,1,2,64,12288]{4,3,2,1,0:T(8,128)(2,1)S(1)}, bf16[1,1,2,64,12288]{4,3,2,1,0:T(8,128)(2,1)}, u32[]{:S(2)}) copy-start(bf16[1,1,2,64,12288]{4,3,2,1,0:T(8,128)(2,1)} %param.16) | copy-start | bytes 9437188
  14.7 1.1 copy-start.4
  71.9 35.4 %copy-start.5 = (f32[1,64,768]{2,1,0:T(8,128)S(1)}, f32[1,64,768]{2,1,0:T(8,128)}, u32[]{:S(2)}) copy-start(f32[1,64,768]{2,1,0:T(8,128)} %param.18) | copy-start | bytes 589828
  72.0 35.4 %copy-start.6 = (f32[1,64,768]{2,1,0:T(8,128)S(1)}, f32[1,64,768]{2,1,0:T(8,128)}, u32[]{:S(2)}) copy-start(f32[1,64,768]{2,1,0:T(8,128)} %param.21) | copy-start | bytes 589828
  72.0 35.4 %copy-start.7 = (f32[1,64,768]{2,1,0:T(8,128)S(1)}, f32[1,64,768]{2,1,0:T(8,128)}, u32[]{:S(2)}) copy-start(f32[1,64,768]{2,1,0:T(8,128)} %param.20) | copy-start | bytes 589828
  72.0 35.4 %copy-start.8 = (f32[1,64,768]{2,1,0:T(8,128)S(1)}, f32[1,64,768]{2,1,0:T(8,128)}, u32[]{:S(2)}) copy-start(f32[1,64,768]{2,1,0:T(8,128)} %param.23) | copy-start | bytes 589828
  72.0 35.4 %copy-start.9 = (f32[1,64,768]{2,1,0:T(8,128)S(1)}, f32[1,64,768]{2,1,0:T(8,128)}, u32[]{:S(2)}) copy-start(f32[1,64,768]{2,1,0:T(8,128)} %param.22) | copy-start | bytes 589828

commit v3 on v1

v3 whole, which is shorter than its diff:
```python
import functools
import math

import jax
import jax.numpy as jnp
from jax import lax
from jax.experimental import pallas as pl
from jax.experimental.pallas import tpu as pltpu
from jax.sharding import PartitionSpec as P

norm_eps = 1e-06
learn_rate = 0.01
beta_one = 0.9
beta_two = 0.95
decay_rate = 0.1
adam_eps = 1e-08
first_fix = 0.9999734386011124
second_fix = 0.9940794707796659


def dot_t(left, right):
    return lax.dot_general(
        left, right, (((1,), (1,)), ((), ())), preferred_element_type=jnp.float32
    )


def dot_n(left, right):
    return jnp.dot(left, right, preferred_element_type=jnp.float32)


MESH = pl.DeviceIdType.MESH


def place():
    tensor = lax.axis_index("tensor")
    return lax.axis_index("replica"), lax.axis_index("section"), tensor // 2, tensor % 2


def remote(source, target, sems, at, device):
    return pltpu.make_async_remote_copy(
        src_ref=source, dst_ref=target, send_sem=sems[0].at[at], recv_sem=sems[1].at[at],
        device_id=device, device_id_type=MESH,
    )


def greet(devices):
    barrier = pltpu.get_barrier_semaphore()
    for device in devices:
        pl.semaphore_signal(barrier, inc=1, device_id=device, device_id_type=MESH)
    pl.semaphore_wait(barrier, len(devices))


def section_peers(replica, section, chip, core, sections):
    return [(replica, lax.rem(section + d, sections), chip * 2 + core) for d in range(1, sections)]


def plane_peers(replica, section, chip, core, replicas):
    found = []
    for dr in range(replicas):
        for dz in range(2):
            for dc in range(2):
                if dr or dz or dc:
                    there = lax.rem(replica + dr, replicas)
                    tensor = lax.rem(chip + dz, 2) * 2 + lax.rem(core + dc, 2)
                    found.append(((there, section, tensor), there * 4 + tensor))
    return found


def piece_sum(box):
    total = box[0].astype(jnp.float32)
    for i in range(1, box.shape[0]):
        total = total + box[i].astype(jnp.float32)
    return total


def cut(value, pieces):
    _, height, width = pieces.shape
    across = value.shape[1] // width
    for i in range(pieces.shape[0]):
        y, x = i // across * height, i % across * width
        pieces[i] = value[y : y + height, x : x + width].astype(pieces.dtype)


def join(spread, whole):
    height, width = spread.shape[-2:]
    across = whole.shape[-1] // width
    for i in range(spread.shape[0]):
        y, x = i // across * height, i % across * width
        whole[..., y : y + height, x : x + width] = spread[i]


def dma_pairs(counts):
    return [pltpu.SemaphoreType.DMA((n,)) for n in counts for _ in range(2)]


def decayed(params, moments, seconds, gradient):
    new_moments = beta_one * moments + (1.0 - beta_one) * gradient
    new_seconds = beta_two * seconds + (1.0 - beta_two) * gradient * gradient
    new_params = params - learn_rate * (
        new_moments / first_fix / (jnp.sqrt(new_seconds / second_fix) + adam_eps)
        + decay_rate * params
    )
    return new_params, new_moments, new_seconds


def run_layers(features, tokens_per, section, counted, codes, z, square, gram, coef, mixing, hb, rate, a_s, w_s, a_all):
    layers, _, tokens, wide = z.shape
    rank = wide // 2
    root = 1.0 / math.sqrt(features)
    row = lax.broadcasted_iota(jnp.int32, (tokens, 1), 0)
    taken = row < counted * tokens_per

    def picked(kind, layer):
        first = z[layer, kind][:, :rank]
        if layer == 0:
            return first.astype(jnp.float32)
        before = z[layer - 1, kind]
        code = codes[layer]
        other = jnp.where(code == 1, before[:, rank:], before[:, :rank])
        return jnp.where(code == 0, first, other).astype(jnp.float32)

    norm = square[...]
    state = jnp.concatenate([picked(1, l) for l in range(layers)], axis=1)
    a_all[...] = jnp.zeros_like(a_all)
    slopes, inner, rhos = [], [], []
    for l in range(layers):
        at = slice(l * rank, (l + 1) * rank)
        hb[l] = state
        rho = lax.rsqrt(jnp.maximum(norm, 0.0) * (1.0 / features) + norm_eps)
        product = picked(0, l)
        if l:
            product = product + dot_t(a_all[...], gram[l, :rank])
        u = product * (rho * root)
        sigma = jax.nn.sigmoid(u)
        active = (u * sigma * (1.0 / math.sqrt(rank))).astype(jnp.bfloat16)
        a_s[l] = active
        a_all[:, at] = active
        added = dot_n(active, gram[l, rank:])
        wide_a = active.astype(jnp.float32)
        norm = norm + jnp.sum(wide_a * (2.0 * state[:, at] + added[:, at]), axis=1, keepdims=True)
        state = state + added
        slopes.append(sigma * (1.0 + u * (1.0 - sigma)) * (1.0 / math.sqrt(rank)))
        inner.append(u)
        rhos.append(rho)
    back = jnp.concatenate(
        [jnp.where(taken, picked(2, l), 0.0) for l in range(layers)], axis=1
    )
    gamma = jnp.zeros((tokens, 1), jnp.float32)
    for l in reversed(range(layers)):
        at = slice(l * rank, (l + 1) * rank)
        e = back[:, at] * slopes[l]
        rho = rhos[l]
        w = (e * (rho * root)).astype(jnp.bfloat16)
        w_s[l] = w
        rate[l] = gamma
        c = rho * rho * jnp.sum(e * inner[l], axis=1, keepdims=True) * (1.0 / features)
        gamma = gamma + c
        if l:
            back = back + dot_n(w, gram[l, :rank]) - c * hb[l]
    own_w = w_s[section].astype(jnp.float32)
    own_a = a_s[section].astype(jnp.float32)
    own_rate = rate[section]
    nothing = jnp.zeros((tokens, rank), jnp.float32)
    left = jnp.concatenate(
        [
            jnp.concatenate([own_w, -own_rate * own_a], axis=1),
            jnp.concatenate([nothing, jnp.where(taken, own_a, 0.0)], axis=1),
        ],
        axis=0,
    )
    coef[...] = left.T.astype(jnp.bfloat16)
    own_left = own_a.T.astype(jnp.bfloat16)
    own_down = own_w.T.astype(jnp.bfloat16)
    before = jnp.concatenate([jnp.where(l < section, a_s[l], jnp.zeros_like(a_s[l])) for l in range(layers)], axis=1)
    beyond = jnp.concatenate([jnp.where(l > section, w_s[l], jnp.zeros_like(w_s[l])) for l in range(layers)], axis=1)
    scaled = jnp.concatenate(
        [
            (jnp.where(l <= section, own_rate, rate[l]) * a_s[l].astype(jnp.float32)).astype(jnp.bfloat16)
            for l in range(layers)
        ],
        axis=1,
    )
    mixing[:rank] = (dot_n(own_down, before) + dot_n(own_left, beyond)).astype(jnp.bfloat16)
    mixing[rank:] = (-dot_n(own_left, scaled)).astype(jnp.bfloat16)


def publish(replicas, sections, share, out, shift_send, shift_recv, far_sems, core_sems):
    replica, section, chip, core = place()
    columns = share.shape[1]
    before = lax.rem(section + sections - 1, sections)
    other = 1 - chip
    up, down, across = (lax.rem(replica + d, replicas) for d in (1, replicas - 1, 2))
    tensor = chip * 2 + core
    sibling = (replica, section, chip * 2 + 1 - core)
    partner = (replica, section, other * 2 + core)
    above, below = (up, section, tensor), (down, section, tensor)
    def block(window, r, z):
        return out.at[window, :, pl.ds(pl.multiple_of((r * 4 + z * 2 + core) * columns, 128), columns)]

    started = {}
    def send(window, kind, r, z, device):
        copy = remote(block(window, r, z), block(window, r, z), far_sems, window * 7 + kind, device)
        copy.start()
        started[window, kind] = copy

    swaps = []

    def swap(window, r, z):
        number = len(swaps)
        copy = remote(block(window, r, z), block(window, r, z), core_sems, number, sibling)
        copy.start()
        swaps.append(copy)

    own = pl.ds(pl.multiple_of((replica * 4 + tensor) * columns, 128), columns)
    shift = pltpu.make_async_remote_copy(
        src_ref=share, dst_ref=out.at[1, :, own], send_sem=shift_send, recv_sem=shift_recv,
        device_id=(replica, before, tensor), device_id_type=MESH,
    )
    shift.start()
    out[0, :, own] = share[...]
    for window in range(2):
        if window:
            shift.wait()
        send(window, 0, replica, chip, partner)
        send(window, 1, replica, chip, above)
        send(window, 3, replica, chip, below)
        swap(window, replica, chip)
    for window in range(2):
        started[window, 0].wait_recv()
        send(window, 2, replica, other, above)
        send(window, 4, replica, other, below)
        swap(window, replica, other)
    for window in range(2):
        started[window, 1].wait_recv()
        send(window, 5, down, chip, above)
        swap(window, down, chip)
        started[window, 3].wait_recv()
        swap(window, up, chip)
    for window in range(2):
        started[window, 4].wait_recv()
        send(window, 6, up, other, below)
        swap(window, up, other)
        started[window, 2].wait_recv()
        swap(window, down, other)
    for window in range(2):
        started[window, 5].wait_recv()
        swap(window, across, chip)
        started[window, 6].wait_recv()
        swap(window, across, other)
    for copy in started.values():
        copy.wait_send()
    for copy in swaps:
        copy.wait()


COUNTS = dict(rows=7, z=7, gram=15, piece=7, plane=7, core=8, downs=7, mix=15, mixed=15, half=8, chip=7, far=14, swap=16)


def step_kernel(
    replicas, sections, tokens_per,
    bounds, counts, hidden_hbm, last_hbm, downs_hbm, ups_hbm,
    master_down, master_up, moment_down, moment_up, second_down, second_up,
    gradient, out,
    hidden, last, weights, mine, z, acc, zs, rows, down_rows, gram, pieces, box, spread,
    coef, mixing, hb, rate, a_s, w_s, a_all, mix_pieces, mix_box, mix_spread,
    parts, half, chips, inbox, share, local, shift_send, shift_recv, *sems,
):
    sem = {name: sems[2 * i : 2 * i + 2] for i, name in enumerate(COUNTS)}
    replica, section, chip, core = place()
    tensor = chip * 2 + core
    me = replica * 4 + tensor
    rank, columns = master_down.shape
    wide = 2 * rank
    tokens, features = hidden.shape
    along = section_peers(replica, section, chip, core, sections)
    peers = plane_peers(replica, section, chip, core, replicas)
    sibling = (replica, section, chip * 2 + 1 - core)

    loads = [
        pltpu.make_async_copy(downs_hbm, weights.at[pl.ds(0, wide)], local.at[0]),
        pltpu.make_async_copy(ups_hbm, weights.at[pl.ds(wide, wide)], local.at[1]),
        pltpu.make_async_copy(hidden_hbm, hidden, local.at[2]),
        pltpu.make_async_copy(last_hbm, last, local.at[3]),
    ]
    for copy in loads:
        copy.start()
    mine[:rank] = master_down[...].astype(mine.dtype)
    mine[rank:] = master_up[...].astype(mine.dtype)
    greet(along + [device for device, _ in peers])

    row_copies = []
    for i, device in enumerate(along):
        row_copies.append(remote(mine.at[pl.ds(rank, rank)], rows.at[section], sem["rows"], i, device))
        row_copies[-1].start()
    rows[section] = mine[rank:]

    for copy in loads:
        copy.wait()
    acc[...] = jnp.zeros_like(acc)
    step = 1024

    @pl.loop(0, features // step)
    def _(i):
        at = pl.ds(pl.multiple_of(i * step, step), step)
        chunk = hidden[:, at]
        acc[:, : 2 * wide] += dot_t(chunk, weights[:, at])
        acc[:, 2 * wide : 3 * wide] += dot_t(last[:, at], weights[wide:, at])
        squares = chunk.astype(jnp.float32)
        squares = squares * squares
        folded = squares[:, :128]
        for j in range(1, step // 128):
            folded = folded + squares[:, j * 128 : (j + 1) * 128]
        acc[:, 3 * wide :] += folded

    for kind in range(3):
        z[kind] = acc[:, kind * wide : (kind + 1) * wide].astype(z.dtype)
    zs[section] = z[...]

    for copy in row_copies:
        copy.wait()
    cut(dot_t(mine[...], rows[...].reshape(sections * rank, columns)), pieces)
    copies = []
    for i, (device, number) in enumerate(peers):
        copies.append(remote(pieces.at[number], box.at[me], sem["gram"], i, device))
        copies[-1].start()
    z_copies = []
    for i, device in enumerate(along):
        z_copies.append(remote(z, zs.at[section], sem["z"], i, device))
        z_copies[-1].start()
    box[me] = pieces[me]
    for copy in copies:
        copy.wait()
    spread[me, section] = piece_sum(box).astype(spread.dtype)
    copies = []
    for i, device in enumerate(along):
        copies.append(remote(spread.at[me, section], spread.at[me, section], sem["piece"], i, device))
        copies[-1].start()
    for copy in copies:
        copy.wait()
    same = [device for i, (device, number) in enumerate(peers) if i % 2 == 1]
    copies = []
    for i, device in enumerate(same):
        copies.append(remote(spread.at[me], spread.at[me], sem["plane"], i, device))
        copies[-1].start()
    swaps = [remote(spread.at[me], spread.at[me], sem["core"], 7, sibling)]
    swaps[0].start()
    for i, copy in enumerate(copies):
        copy.wait_recv()
        dr, dz = (i + 1) // 2, (i + 1) % 2
        source = lax.rem(replica + replicas - dr, replicas) * 4 + lax.rem(chip + dz, 2) * 2 + core
        swaps.append(remote(spread.at[source], spread.at[source], sem["core"], i, sibling))
        swaps[-1].start()
    for copy in copies:
        copy.wait_send()
    for copy in z_copies:
        copy.wait()
    down_copies = []
    for i, device in enumerate(along):
        down_copies.append(remote(mine.at[pl.ds(0, rank)], down_rows.at[section], sem["downs"], i, device))
        down_copies[-1].start()
    down_rows[section] = mine[:rank]
    for copy in swaps:
        copy.wait()
    join(spread, gram)

    codes = [0]
    for l in range(1, sections):
        here = (bounds[replica, l] == l) & (bounds[replica, l + 1] > l)
        codes.append(jnp.where(here, 0, jnp.where(bounds[replica, l - 1] == l, 2, 1)))
    square = jnp.sum(acc[:, 3 * wide :], axis=1, keepdims=True)
    run_layers(
        features, tokens_per, section, counts[replica], codes, zs, square, gram, coef, mixing, hb, rate, a_s, w_s, a_all
    )

    cut(mixing[...], mix_pieces)
    mix_copies = []
    for i, (device, number) in enumerate(peers):
        mix_copies.append(remote(mix_pieces.at[number], mix_box.at[me], sem["mix"], i, device))
        mix_copies[-1].start()
    mix_box[me] = mix_pieces[me]
    order = [(2, 1), (2, 0), (1, 1), (3, 1), (1, 0), (3, 0), (0, 1), (0, 0)]
    there = [(lax.rem(replica + dr, replicas), lax.rem(chip + dz, 2)) for dr, dz in order]

    def block_gradient(r, z_at, c):
        at = pl.ds(pl.multiple_of((r * 4 + z_at * 2 + c) * columns, 128), columns)
        return dot_n(coef[:, :tokens], hidden[:, at]) + dot_n(coef[:, tokens:], last[:, at])

    halves = []
    for i, (r, z_at) in enumerate(there):
        parts[i] = block_gradient(r, z_at, 1 - core).astype(parts.dtype)
        halves.append(remote(parts.at[i], half.at[i], sem["half"], i, sibling))
        halves[-1].start()
    sends = []
    for i, (r, z_at) in enumerate(there):
        added = block_gradient(r, z_at, core)
        halves[i].wait()
        chips[i] = (added + half[i].astype(jnp.float32)).astype(chips.dtype)
        if i < len(there) - 1:
            sends.append(remote(chips.at[i], inbox.at[i], sem["chip"], i, (r, section, z_at * 2 + core)))
            sends[-1].start()
    for copy in mix_copies:
        copy.wait()
    mix_spread[me] = piece_sum(mix_box).astype(mix_spread.dtype)
    mix_copies = []
    for i, (device, number) in enumerate(peers):
        mix_copies.append(remote(mix_spread.at[me], mix_spread.at[me], sem["mixed"], i, device))
        mix_copies[-1].start()
    for copy in mix_copies:
        copy.wait()
    join(mix_spread, mixing)
    for copy in down_copies:
        copy.wait()
    layer_of = lax.broadcasted_iota(jnp.int32, (rank, sections * rank), 1) // rank
    crossing = mixing[:rank]
    nothing = jnp.zeros_like(crossing)
    ups_all = rows[...].reshape(sections * rank, columns)
    downs_all = down_rows[...].reshape(sections * rank, columns)
    gradient[:rank] = dot_n(jnp.where(layer_of < section, crossing, nothing), ups_all)
    gradient[rank:] = dot_n(mixing[rank:], ups_all) + dot_n(
        jnp.where(layer_of > section, crossing, nothing), downs_all
    )
    gradient[...] += chips[len(there) - 1].astype(jnp.float32)
    for i, copy in enumerate(sends):
        copy.wait()
        gradient[...] += inbox[i].astype(jnp.float32)
    share[:rank] = decayed(master_down[...], moment_down[...], second_down[...], gradient[:rank])[0].astype(share.dtype)
    share[rank:] = decayed(master_up[...], moment_up[...], second_up[...], gradient[rank:])[0].astype(share.dtype)
    publish(replicas, sections, share, out, shift_send, shift_recv, sem["far"], sem["swap"])


def run_step(bounds, counts, hidden, last, downs, ups, owned, tokens_per):
    replicas, sections = lax.axis_size("replica"), lax.axis_size("section")
    rank, columns = owned[0].shape
    wide, layers = 2 * rank, sections
    tokens, features = hidden.shape
    size = replicas * 4
    height, width = 16, wide * layers * rank // size // 16
    b16, f32 = jnp.bfloat16, jnp.float32
    smem, hbm, vmem = (pl.BlockSpec(memory_space=m) for m in (pltpu.SMEM, pl.ANY, pltpu.VMEM))
    piece = pltpu.VMEM((size, height, width), b16)
    block = pltpu.VMEM((size // 2, wide, columns), b16)
    return pl.pallas_call(
        functools.partial(step_kernel, replicas, sections, tokens_per),
        out_shape=(
            jax.ShapeDtypeStruct((wide, columns), f32),
            jax.ShapeDtypeStruct((2, wide, columns * size), b16),
        ),
        in_specs=[smem, smem] + [hbm] * 4 + [vmem] * 6,
        out_specs=(vmem, vmem),
        scratch_shapes=[
            pltpu.VMEM((tokens, features), b16),
            pltpu.VMEM((tokens, features), b16),
            pltpu.VMEM((2 * wide, features), b16),
            pltpu.VMEM((wide, columns), b16),
            pltpu.VMEM((3, tokens, wide), b16),
            pltpu.VMEM((tokens, 3 * wide + 128), f32),
            pltpu.VMEM((layers, 3, tokens, wide), b16),
            pltpu.VMEM((layers, rank, columns), b16),
            pltpu.VMEM((layers, rank, columns), b16),
            pltpu.VMEM((layers, wide, layers * rank), b16),
            piece,
            piece,
            pltpu.VMEM((size, sections, height, width), b16),
            pltpu.VMEM((wide, 2 * tokens), b16),
            pltpu.VMEM((wide, layers * rank), b16),
            pltpu.VMEM((layers, tokens, layers * rank), f32),
            pltpu.VMEM((layers, tokens, 1), f32),
            pltpu.VMEM((layers, tokens, rank), b16),
            pltpu.VMEM((layers, tokens, rank), b16),
            pltpu.VMEM((tokens, layers * rank), b16),
            piece,
            piece,
            piece,
            block,
            block,
            block,
            block,
            pltpu.VMEM((wide, columns), b16),
            pltpu.SemaphoreType.DMA((4,)),
            pltpu.SemaphoreType.DMA,
            pltpu.SemaphoreType.DMA,
        ]
        + dma_pairs(COUNTS.values()),
        compiler_params=pltpu.CompilerParams(collective_id=1, has_side_effects=True, vmem_limit_bytes=56 * 2**20),
        name="step",
    )(bounds, counts, hidden, last, downs, ups, *owned)


def on_device(
    inputs, cotangent, micro_counts, bounds, holder_down, holder_up,
    master_down, master_up, moment_down, moment_up, second_down, second_up,
):
    replica_at = lax.axis_index("replica")
    section_at = lax.axis_index("section")
    micros, per, features = inputs.shape[1:]
    slots, rank = holder_down.shape[2:4]
    tokens = micros * per
    first_layers = bounds[replica_at]
    owned = [array[0] for array in (master_down, master_up, moment_down, moment_up, second_down, second_up)]
    gradient, whole = run_step(
        bounds,
        micro_counts,
        inputs[0].reshape(tokens, features),
        cotangent[0].reshape(tokens, features),
        holder_down[0, 0].reshape(slots * rank, features),
        holder_up[0, 0].reshape(slots * rank, features),
        owned,
        per,
    )
    new_down = decayed(owned[0], owned[2], owned[4], gradient[:rank])
    new_up = decayed(owned[1], owned[3], owned[5], gradient[rank:])
    whole = whole.reshape(2, 2, rank, features)
    first, end = first_layers[section_at], first_layers[section_at + 1]
    slot_zero = jnp.where(end > first, jnp.where(first == section_at, whole[0], whole[1]), 0)
    slot_one = jnp.where(end > first + 1, whole[1], 0)
    placed = jnp.stack([slot_zero, slot_one], axis=1)
    news = [array[None] for pair in zip(new_down, new_up) for array in pair]
    return (placed[0][None, None], placed[1][None, None], *news)


def solution(mesh):
    owned = P("section", None, ("replica", "tensor"))
    held = P("replica", "section", None, None, None)
    tokens = P("replica", None, "tensor", None)
    return jax.shard_map(
        on_device,
        mesh=mesh,
        in_specs=(tokens, tokens, P(), P(), held, held) + (owned,) * 6,
        out_specs=(held, held) + (owned,) * 6,
        check_vma=False,
    )
```

time: 352 us -> 130 us (0.37)
  blocking collectives: 173 us -> 0 us
  waiting for transfers between devices: 116 us -> 0 us
  Pallas kernels: 6.03 us -> 118 us
  matrix products: 15.3 us -> 0 us
  between operations: 17.2 us -> 3.99 us
  local copies, waits for them, and re-layouts: 9.4 us -> 1.39 us
  other arithmetic: 13.1 us -> 7.24 us
    psum x2 -> x0, blocking collectives: 141 us -> none  [the longest x1 73.9 us: on_device(): mixing = lax.psum(mixing, plane).astype(jnp.bfloat16)]
    pallas_call x1, Pallas kernels: 6.03 us -> 118 us  [run_step(): pl.pallas_call(functools.partial(step_kernel, replicas, sections, tokens_...]
    all_gather x3 -> x0, waiting for transfers between devices: 107 us -> none  [the longest x1 59.5 us: on_device(): whole = lax.all_gather(jnp.stack([share, after]), plane, axis=2, tiled=True)]
    all_gather x1 -> x0, blocking collectives: 31.9 us -> none  [on_device(): z = lax.all_gather(z, 'section')]
    dot_general x7 -> x0, matrix products: 15.3 us -> none  [the longest x3 9 us: dot_n(): return jnp.dot(left, right, preferred_element_type=jnp.float32)]
    ppermute x1 -> x0, waiting for transfers between devices: 5.11 us -> none  [on_device(): lax.ppermute(share, 'section', [(i, i - 1) for i in range(1, layers)])]
    unnamed x18 -> x14, local copies, waits for them, and re-layouts: 4.05 us -> 0.04 us
    reduce_scatter x1 -> x0, waiting for transfers between devices: 3.77 us -> none  [on_device(): lax.psum_scatter(grads.astype(jnp.bfloat16), plane, scatter_dimension=1,...]
  transfers between devices with their start and end apart: 5 -> 0, of which waited for: 5 -> 0; matrix products, arithmetic and copies ran while one was open for 4% -> 0% of each run, Pallas kernels for 0% -> 0%
where the time goes in v3:
time: 130 us
  Pallas kernels  118 us (91%)
  other arithmetic  7.24 us (6%)
  between operations  3.99 us (3%)
  local copies, waits for them, and re-layouts  1.39 us (1%)
    pallas_call x1, Pallas kernels, run_step(): pl.pallas_call(functools.partial(step_kernel, replicas, sections, tokens_...  118 us
    select_n x1, other arithmetic, on_device(): slot_one = jnp.where(end > first + 1, whole[1], 0)  3.07 us
    another operation x1, other arithmetic, on_device(): return (placed[0][None, None], placed[1][None, None], *news)  2.99 us

profile of v3, /device:TPU:1, one launch (start us, length us, event | category | flops | bytes accessed | tf_op | source)
XLA Modules:
  0.0 130.1 jit_solution(6707174443845325620)
XLA Ops:
  0.6 1.4 %fusion.9 = (s32[1,1]{1,0:T(1,128)}, s32[1,1]{1,0:T(1,128)}) fusion(s32[4,9]{1,0:T(4,128)} %bounds.1, s32[]{:T(128)S(6)} %select_n.66, s32[]{:T(128)S(6)} %select_n.68, s32[]{:T(128)S(6)} %select_n.70), kind=kLoop, calls=%fused_computation.20 | loop fusion | bytes 28 | tf_op jit(solution)/shard_map/dynamic_slice | solution.py:513
  5.2 117.5 %step.1 = (f32[128,768]{1,0:T(8,128)}, bf16[2,128,12288]{2,1,0:T(8,128)(2,1)}) custom-call(s32[4,9]{1,0:T(4,128)} %bounds.1, s32[4]{0:T(128)} %counts.1, bf16[128,12288]{1,0:T(8,128)(2,1)} %bitcast.46, bf16[128,12288]{1,0:T(8,128)(2,1)} %bitcast.47, bf16[128,12288]{1,0:T(8,128)(2,1)} %bitcast.48, bf16[128,12288]{1,0:T(8,128)(2,1)} %bitcast.49, ...), custom_call_target="tpu_custom_call" | custom-call | tf_op jit(solution)/shard_map/step/pallas_call | solution.py:442
  122.8 3.1 %broadcast_select_fusion = (bf16[1,128,12288]{2,1,0:T(8,128)(2,1)S(1)}, bf16[1,128,12288]{2,1,0:T(8,128)(2,1)S(1)}) fusion(pred[]{:T(512)S(6)} %gt.7, bf16[2,128,12288]{2,1,0:T(8,128)(2,1)} %get-tuple-element.10, pred[]{:T(512)S(6)} %eq.3, pred[]{:T(512)S(6)} %gt.6), kind=kLoop, calls=%fused_computation.7 | loop fusion | flops 4718592 | bytes 12582915 | tf_op jit(solution)/shard_map/jit(_where)/select_n | solution.py:515
  125.8 0.0 copy-start
  125.8 0.0 copy-start.1
  125.9 0.0 copy-start.2
  125.9 0.0 copy-start.3
  125.9 0.0 copy-start.4
  125.9 0.0 copy-start.5
  125.9 0.0 copy-start.6
  125.9 3.0 %fusion.2 = (bf16[1,1,2,64,12288]{4,3,2,1,0:T(8,128)(2,1)}, bf16[1,1,2,64,12288]{4,3,2,1,0:T(8,128)(2,1)}) fusion(bf16[2,1,64,12288]{3,2,1,0:T(8,128)(2,1)S(1)} %bitcast.44, bf16[2,1,64,12288]{3,2,1,0:T(8,128)(2,1)S(1)} %bitcast.45), kind=kLoop, calls=%fused_computation.5 | loop fusion | flops 3145728 | bytes 12582912 | tf_op jit(solution)/shard_map/broadcast_in_dim;squeeze | solution.py:518
  128.9 0.0 copy-done
  128.9 0.0 copy-done.1
  128.9 0.0 copy-done.2
  128.9 0.0 copy-done.3
  128.9 0.0 copy-done.4
  128.9 0.0 copy-done.5
  129.0 0.0 copy-done.6
  129.0 1.2 fusion.7
Async XLA Ops:
  125.8 3.1 %copy-start = (f32[1,64,768]{2,1,0:T(8,128)S(1)}, f32[1,64,768]{2,1,0:T(8,128)}, u32[]{:S(2)}) copy-start(f32[1,64,768]{2,1,0:T(8,128)} %param.18) | copy-start | bytes 589828
  125.8 3.1 %copy-start.1 = (f32[1,64,768]{2,1,0:T(8,128)S(1)}, f32[1,64,768]{2,1,0:T(8,128)}, u32[]{:S(2)}) copy-start(f32[1,64,768]{2,1,0:T(8,128)} %param.19) | copy-start | bytes 589828
  125.9 3.1 %copy-start.2 = (f32[1,64,768]{2,1,0:T(8,128)S(1)}, f32[1,64,768]{2,1,0:T(8,128)}, u32[]{:S(2)}) copy-start(f32[1,64,768]{2,1,0:T(8,128)} %param.20) | copy-start | bytes 589828
  125.9 3.1 %copy-start.3 = (f32[1,64,768]{2,1,0:T(8,128)S(1)}, f32[1,64,768]{2,1,0:T(8,128)}, u32[]{:S(2)}) copy-start(f32[1,64,768]{2,1,0:T(8,128)} %param.21) | copy-start | bytes 589828
  125.9 3.1 %copy-start.4 = (f32[1,64,768]{2,1,0:T(8,128)S(1)}, f32[1,64,768]{2,1,0:T(8,128)}, u32[]{:S(2)}) copy-start(f32[1,64,768]{2,1,0:T(8,128)} %param.22) | copy-start | bytes 589828
  125.9 3.0 %copy-start.5 = (f32[1,64,768]{2,1,0:T(8,128)S(1)}, f32[1,64,768]{2,1,0:T(8,128)}, u32[]{:S(2)}) copy-start(f32[1,64,768]{2,1,0:T(8,128)} %param.23) | copy-start | bytes 589828
  125.9 3.0 %copy-start.6 = (f32[128,768]{1,0:T(8,128)S(1)}, f32[128,768]{1,0:T(8,128)}, u32[]{:S(2)}) copy-start(f32[128,768]{1,0:T(8,128)} %get-tuple-element.11) | copy-start | bytes 1179652

commit v4 on v3

--- a/solution.py
+++ b/solution.py
@@ -194,76 +194,106 @@
     sibling = (replica, section, chip * 2 + 1 - core)
     partner = (replica, section, other * 2 + core)
     above, below = (up, section, tensor), (down, section, tensor)
+    rank = share.shape[0] // 2
+
+    def columns_of(r, z):
+        return pl.ds(pl.multiple_of((r * 4 + z * 2 + core) * columns, 128), columns)
+
     def block(window, r, z):
-        return out.at[window, :, pl.ds(pl.multiple_of((r * 4 + z * 2 + core) * columns, 128), columns)]
+        return out.at[window, :, columns_of(r, z)]
 
     started = {}
-    def send(window, kind, r, z, device):
-        copy = remote(block(window, r, z), block(window, r, z), far_sems, window * 7 + kind, device)
+    def send(number, piece, device):
+        copy = remote(piece, piece, far_sems, number, device)
         copy.start()
-        started[window, kind] = copy
+        started[number] = copy
 
     swaps = []
 
     def swap(window, r, z):
-        number = len(swaps)
-        copy = remote(block(window, r, z), block(window, r, z), core_sems, number, sibling)
+        copy = remote(block(window, r, z), block(window, r, z), core_sems, len(swaps), sibling)
         copy.start()
         swaps.append(copy)
 
-    own = pl.ds(pl.multiple_of((replica * 4 + tensor) * columns, 128), columns)
+    def upper(r):
+        return out.at[1, pl.ds(0, rank), columns_of(r, chip)]
+
+    def lower(r):
+        return out.at[1, pl.ds(rank, rank), columns_of(r, chip)]
+
+    own = columns_of(replica, chip)
     shift = pltpu.make_async_remote_copy(
         src_ref=share, dst_ref=out.at[1, :, own], send_sem=shift_send, recv_sem=shift_recv,
         device_id=(replica, before, tensor), device_id_type=MESH,
     )
     shift.start()
     out[0, :, own] = share[...]
-    for window in range(2):
-        if window:
-            shift.wait()
-        send(window, 0, replica, chip, partner)
-        send(window, 1, replica, chip, above)
-        send(window, 3, replica, chip, below)
-        swap(window, replica, chip)
-    for window in range(2):
-        started[window, 0].wait_recv()
-        send(window, 2, replica, other, above)
-        send(window, 4, replica, other, below)
-        swap(window, replica, other)
-    for window in range(2):
-        started[window, 1].wait_recv()
-        send(window, 5, down, chip, above)
-        swap(window, down, chip)
-        started[window, 3].wait_recv()
-        swap(window, up, chip)
-    for window in range(2):
-        started[window, 4].wait_recv()
-        send(window, 6, up, other, below)
-        swap(window, up, other)
-        started[window, 2].wait_recv()
-        swap(window, down, other)
-    for window in range(2):
-        started[window, 5].wait_recv()
-        swap(window, across, chip)
-        started[window, 6].wait_recv()
-        swap(window, across, other)
+    send(0, block(0, replica, chip), partner)
+    send(1, block(0, replica, chip), above)
+    send(3, block(0, replica, chip), below)
+    swap(0, replica, chip)
+    shift.wait()
+    send(7, block(1, replica, chip), above)
+    send(8, block(1, replica, chip), below)
+    send(11, block(1, replica, chip), partner)
+    swap(1, replica, chip)
+    started[0].wait_recv()
+    send(2, block(0, replica, other), above)
+    send(4, block(0, replica, other), below)
+    swap(0, replica, other)
+    started[1].wait_recv()
+    send(5, block(0, down, chip), above)
+    swap(0, down, chip)
+    started[3].wait_recv()
+    swap(0, up, chip)
+    started[7].wait_recv()
+    send(9, upper(down), above)
+    send(12, block(1, down, chip), partner)
+    swap(1, down, chip)
+    started[8].wait_recv()
+    send(10, lower(up), below)
+    send(13, block(1, up, chip), partner)
+    swap(1, up, chip)
+    started[4].wait_recv()
+    send(6, block(0, up, other), below)
+    swap(0, up, other)
+    started[2].wait_recv()
+    swap(0, down, other)
+    started[11].wait_recv()
+    swap(1, replica, other)
+    started[9].wait_recv()
+    send(14, upper(across), partner)
+    started[10].wait_recv()
+    send(15, lower(across), partner)
+    swap(1, across, chip)
+    started[5].wait_recv()
+    swap(0, across, chip)
+    started[6].wait_recv()
+    swap(0, across, other)
+    started[12].wait_recv()
+    swap(1, down, other)
+    started[13].wait_recv()
+    swap(1, up, other)
+    started[14].wait_recv()
+    started[15].wait_recv()
+    swap(1, across, other)
     for copy in started.values():
         copy.wait_send()
     for copy in swaps:
         copy.wait()
 
 
-COUNTS = dict(rows=7, z=7, gram=15, piece=7, plane=7, core=8, downs=7, mix=15, mixed=15, half=8, chip=7, far=14, swap=16)
+COUNTS = dict(rows=7, z=7, gram=15, piece=7, plane=7, core=8, downs=7, mix=15, mixed=15, half=8, chip=14, far=16, swap=16)
 
 
 def step_kernel(
     replicas, sections, tokens_per,
     bounds, counts, hidden_hbm, last_hbm, downs_hbm, ups_hbm,
     master_down, master_up, moment_down, moment_up, second_down, second_up,
-    gradient, out,
-    hidden, last, weights, mine, z, acc, zs, rows, down_rows, gram, pieces, box, spread,
+    gradient, placed_down, placed_up,
+    out, hidden, last, weights, mine, z, acc, zs, rows, down_rows, gram, pieces, box, spread,
     coef, mixing, hb, rate, a_s, w_s, a_all, mix_pieces, mix_box, mix_spread,
-    parts, half, chips, inbox, share, local, shift_send, shift_recv, *sems,
+    parts, half, chips, inbox, late, share, local, shift_send, shift_recv, *sems,
 ):
     sem = {name: sems[2 * i : 2 * i + 2] for i, name in enumerate(COUNTS)}
     replica, section, chip, core = place()
@@ -378,26 +408,58 @@
         mix_copies.append(remote(mix_pieces.at[number], mix_box.at[me], sem["mix"], i, device))
         mix_copies[-1].start()
     mix_box[me] = mix_pieces[me]
-    order = [(2, 1), (2, 0), (1, 1), (3, 1), (1, 0), (3, 0), (0, 1), (0, 0)]
-    there = [(lax.rem(replica + dr, replicas), lax.rem(chip + dz, 2)) for dr, dz in order]
-
-    def block_gradient(r, z_at, c):
-        at = pl.ds(pl.multiple_of((r * 4 + z_at * 2 + c) * columns, 128), columns)
+    order = [(2, 1), (2, 0), (1, 1), (1, 0), (3, 1), (3, 0), (0, 1), (0, 0)]
+    partner = (replica, section, lax.rem(chip + 1, 2) * 2 + core)
+    first, second = pl.ds(0, rank), pl.ds(rank, rank)
+
+    def ring(dr):
+        return (lax.rem(replica + dr, replicas), section, tensor)
+
+    def block_gradient(dr, dz, c):
+        number = lax.rem(replica + dr, replicas) * 4 + lax.rem(chip + dz, 2) * 2 + c
+        at = pl.ds(pl.multiple_of(number * columns, 128), columns)
         return dot_n(coef[:, :tokens], hidden[:, at]) + dot_n(coef[:, tokens:], last[:, at])
 
     halves = []
-    for i, (r, z_at) in enumerate(there):
-        parts[i] = block_gradient(r, z_at, 1 - core).astype(parts.dtype)
-        halves.append(remote(parts.at[i], half.at[i], sem["half"], i, sibling))
-        halves[-1].start()
-    sends = []
-    for i, (r, z_at) in enumerate(there):
-        added = block_gradient(r, z_at, core)
-        halves[i].wait()
-        chips[i] = (added + half[i].astype(jnp.float32)).astype(chips.dtype)
-        if i < len(there) - 1:
-            sends.append(remote(chips.at[i], inbox.at[i], sem["chip"], i, (r, section, z_at * 2 + core)))
-            sends[-1].start()
+    sends = {}
+
+    def send(number, source, target, device):
+        sends[number] = remote(source, target, sem["chip"], number, device)
+        sends[number].start()
+
+    for i in range(len(order) + 1):
+        if i < len(order):
+            parts[i] = block_gradient(*order[i], 1 - core).astype(parts.dtype)
+            halves.append(remote(parts.at[i], half.at[i], sem["half"], i, sibling))
+            halves[-1].start()
+        if i:
+            dr, dz = order[i - 1]
+            added = block_gradient(dr, dz, core)
+            halves[i - 1].wait()
+            chips[i - 1] = (added + half[i - 1].astype(jnp.float32)).astype(chips.dtype)
+            if dr:
+                send(i - 1, chips.at[i - 1, first], inbox.at[i - 1, first], ring(dr))
+            if dz:
+                send(6 + dr, chips.at[i - 1, second], inbox.at[i - 1, second], partner)
+    at = {distance: i for i, distance in enumerate(order)}
+
+    for dr in (2, 1, 3):
+        sends[6 + dr].wait_recv()
+        i = at[dr, 1]
+        parts[i, second] = (chips[at[dr, 0], second].astype(jnp.float32) + inbox[i, second].astype(jnp.float32)).astype(
+            parts.dtype
+        )
+        send(9 + dr, parts.at[i, second], late.at[dr], ring(dr))
+    for dz in (1, 0):
+        total = chips[at[0, dz], first].astype(jnp.float32)
+        for dr in (2, 1, 3):
+            sends[at[dr, dz]].wait_recv()
+            total = total + inbox[at[dr, dz], first].astype(jnp.float32)
+        if dz:
+            parts[at[0, 1], first] = total.astype(parts.dtype)
+            send(13, parts.at[at[0, 1], first], late.at[0], partner)
+        else:
+            kept = total
     for copy in mix_copies:
         copy.wait()
     mix_spread[me] = piece_sum(mix_box).astype(mix_spread.dtype)
@@ -419,13 +481,30 @@
     gradient[rank:] = dot_n(mixing[rank:], ups_all) + dot_n(
         jnp.where(layer_of > section, crossing, nothing), downs_all
     )
-    gradient[...] += chips[len(there) - 1].astype(jnp.float32)
-    for i, copy in enumerate(sends):
-        copy.wait()
-        gradient[...] += inbox[i].astype(jnp.float32)
+    sends[6].wait_recv()
+    total = chips[at[0, 0], second].astype(jnp.float32) + inbox[at[0, 1], second].astype(jnp.float32)
+    for dr in (2, 1, 3):
+        sends[9 + dr].wait_recv()
+        total = total + late[dr].astype(jnp.float32)
+    gradient[rank:] += total
+    sends[13].wait_recv()
+    gradient[:rank] += kept + late[0].astype(jnp.float32)
+    for copy in sends.values():
+        copy.wait_send()
     share[:rank] = decayed(master_down[...], moment_down[...], second_down[...], gradient[:rank])[0].astype(share.dtype)
     share[rank:] = decayed(master_up[...], moment_up[...], second_up[...], gradient[rank:])[0].astype(share.dtype)
     publish(replicas, sections, share, out, shift_send, shift_recv, sem["far"], sem["swap"])
+    begin, end = bounds[replica, section], bounds[replica, section + 1]
+    held, both, own = end > begin, end > begin + 1, begin == section
+
+    @pl.loop(0, features // step)
+    def _(i):
+        at = pl.ds(pl.multiple_of(i * step, step), step)
+        for placed, rows_of in ((placed_down, first), (placed_up, second)):
+            this, following = out[0, rows_of, at], out[1, rows_of, at]
+            none = jnp.zeros_like(this)
+            placed[0, :, at] = jnp.where(held, jnp.where(own, this, following), none)
+            placed[1, :, at] = jnp.where(both, following, none)
 
 
 def run_step(bounds, counts, hidden, last, downs, ups, owned, tokens_per):
@@ -443,11 +522,13 @@
         functools.partial(step_kernel, replicas, sections, tokens_per),
         out_shape=(
             jax.ShapeDtypeStruct((wide, columns), f32),
-            jax.ShapeDtypeStruct((2, wide, columns * size), b16),
+            jax.ShapeDtypeStruct((2, rank, features), b16),
+            jax.ShapeDtypeStruct((2, rank, features), b16),
         ),
         in_specs=[smem, smem] + [hbm] * 4 + [vmem] * 6,
-        out_specs=(vmem, vmem),
+        out_specs=(vmem,) * 3,
         scratch_shapes=[
+            pltpu.VMEM((2, wide, features), b16),
             pltpu.VMEM((tokens, features), b16),
             pltpu.VMEM((tokens, features), b16),
             pltpu.VMEM((2 * wide, features), b16),
@@ -475,13 +556,14 @@
             block,
             block,
             block,
+            pltpu.VMEM((replicas, rank, columns), b16),
             pltpu.VMEM((wide, columns), b16),
             pltpu.SemaphoreType.DMA((4,)),
             pltpu.SemaphoreType.DMA,
             pltpu.SemaphoreType.DMA,
         ]
         + dma_pairs(COUNTS.values()),
-        compiler_params=pltpu.CompilerParams(collective_id=1, has_side_effects=True, vmem_limit_bytes=56 * 2**20),
+        compiler_params=pltpu.CompilerParams(collective_id=1, has_side_effects=True, vmem_limit_bytes=42 * 2**20),
         name="step",
     )(bounds, counts, hidden, last, downs, ups, *owned)
 
@@ -490,14 +572,11 @@
     inputs, cotangent, micro_counts, bounds, holder_down, holder_up,
     master_down, master_up, moment_down, moment_up, second_down, second_up,
 ):
-    replica_at = lax.axis_index("replica")
-    section_at = lax.axis_index("section")
     micros, per, features = inputs.shape[1:]
     slots, rank = holder_down.shape[2:4]
     tokens = micros * per
-    first_layers = bounds[replica_at]
     owned = [array[0] for array in (master_down, master_up, moment_down, moment_up, second_down, second_up)]
-    gradient, whole = run_step(
+    gradient, placed_down, placed_up = run_step(
         bounds,
         micro_counts,
         inputs[0].reshape(tokens, features),
@@ -509,13 +588,8 @@
     )
     new_down = decayed(owned[0], owned[2], owned[4], gradient[:rank])
     new_up = decayed(owned[1], owned[3], owned[5], gradient[rank:])
-    whole = whole.reshape(2, 2, rank, features)
-    first, end = first_layers[section_at], first_layers[section_at + 1]
-    slot_zero = jnp.where(end > first, jnp.where(first == section_at, whole[0], whole[1]), 0)
-    slot_one = jnp.where(end > first + 1, whole[1], 0)
-    placed = jnp.stack([slot_zero, slot_one], axis=1)
     news = [array[None] for pair in zip(new_down, new_up) for array in pair]
-    return (placed[0][None, None], placed[1][None, None], *news)
+    return (placed_down[None, None], placed_up[None, None], *news)
 
 
 def solution(mesh):

time: 130 us -> 120 us (0.923)
  Pallas kernels: 118 us -> 106 us
  local copies, waits for them, and re-layouts: 1.39 us -> 12.1 us
  other arithmetic: 7.24 us -> 1.18 us
  between operations: 3.99 us -> 0.66 us
    unnamed x14 -> x20, local copies, waits for them, and re-layouts: 0.04 us -> 12.1 us
    pallas_call x1, Pallas kernels: 118 us -> 106 us  [run_step(): pl.pallas_call(functools.partial(step_kernel, replicas, sections, tokens_...]
    select_n x1 -> x0, other arithmetic: 3.07 us -> none  [on_device(): slot_one = jnp.where(end > first + 1, whole[1], 0)]
    another operation x1 -> x0, other arithmetic: 2.99 us -> none  [on_device(): return (placed[0][None, None], placed[1][None, None], *news)]
    dynamic_slice x1 -> x0, local copies, waits for them, and re-layouts: 1.35 us -> none  [on_device(): first, end = (first_layers[section_at], first_layers[section_at + 1])]
where the time goes in v4:
time: 120 us
  Pallas kernels  106 us (88%)
  local copies, waits for them, and re-layouts  12.1 us (10%)
    pallas_call x1, Pallas kernels, run_step(): pl.pallas_call(functools.partial(step_kernel, replicas, sections, tokens_...  106 us
    unnamed x20, local copies, waits for them, and re-layouts  12.1 us

profile of v4, /device:TPU:1, one launch (start us, length us, event | category | flops | bytes accessed | tf_op | source)
XLA Modules:
  0.0 119.6 jit_solution(13079810511402191093)
XLA Ops:
  0.6 0.0 copy-start
  0.6 1.9 %copy-done = bf16[1,4,32,12288]{3,2,1,0:T(8,128)(2,1)S(1)} copy-done((bf16[1,4,32,12288]{3,2,1,0:T(8,128)(2,1)S(1)}, bf16[1,4,32,12288]{3,2,1,0:T(8,128)(2,1)}, u32[]{:S(2)}) %copy-start) | copy-done | bytes 3145752
  2.5 0.0 copy-start.1
  2.5 0.9 copy-done.1
  3.5 0.0 copy-start.2
  3.5 0.9 copy-done.2
  4.4 0.0 copy-start.3
  4.4 0.9 copy-done.3
  5.3 0.0 copy-start.4
  5.3 0.9 copy-done.4
  6.2 0.0 copy-start.5
  6.2 0.9 copy-done.5
  7.2 0.0 copy-start.6
  7.2 0.9 copy-done.6
  8.1 0.0 copy-start.7
  8.1 0.7 copy-done.7
  8.8 0.0 copy-start.8
  8.8 0.7 copy-done.8
  9.4 105.7 %step.1 = (f32[128,768]{1,0:T(8,128)S(1)}, bf16[2,64,12288]{2,1,0:T(8,128)(2,1)S(1)}, bf16[2,64,12288]{2,1,0:T(8,128)(2,1)S(1)}) custom-call(s32[4,9]{1,0:T(4,128)S(1)} %copy-done.7, s32[4]{0:T(128)S(1)} %copy-done.8, bf16[128,12288]{1,0:T(8,128)(2,1)S(1)} %bitcast.36, bf16[128,12288]{1,0:T(8,128)(2,1)} %bitcast.43, bf16[128,12288]{1,0:T(8,128)(2,1)} %bitcast.44, ...), custom_call_target="tpu_custom_call" | custom-call | tf_op jit(solution)/shard_map/step/pallas_call | solution.py:521
  115.1 1.2 fusion.4
  116.3 1.7 %copy.22 = bf16[1,1,2,64,12288]{4,3,2,1,0:T(8,128)(2,1)} copy(bf16[1,1,2,64,12288]{4,3,2,1,0:T(8,128)(2,1)S(1)} %bitcast.35) | data formatting | bytes 6291456
  117.9 1.7 %copy.23 = bf16[1,1,2,64,12288]{4,3,2,1,0:T(8,128)(2,1)} copy(bf16[1,1,2,64,12288]{4,3,2,1,0:T(8,128)(2,1)S(1)} %bitcast.34) | data formatting | bytes 6291456
Async XLA Ops:
  0.6 1.9 %copy-start = (bf16[1,4,32,12288]{3,2,1,0:T(8,128)(2,1)S(1)}, bf16[1,4,32,12288]{3,2,1,0:T(8,128)(2,1)}, u32[]{:S(2)}) copy-start(bf16[1,4,32,12288]{3,2,1,0:T(8,128)(2,1)} %param.12) | copy-start | bytes 9437188
  2.5 0.9 copy-start.1
  3.5 0.9 copy-start.2
  4.4 0.9 copy-start.3
  5.3 0.9 copy-start.4
  6.2 0.9 copy-start.5
  7.2 0.9 copy-start.6
  8.1 0.7 copy-start.7
  8.8 0.7 copy-start.8

commit v5 on v4

--- a/solution.py
+++ b/solution.py
@@ -41,13 +41,6 @@
         src_ref=source, dst_ref=target, send_sem=sems[0].at[at], recv_sem=sems[1].at[at],
         device_id=device, device_id_type=MESH,
     )
-
-
-def greet(devices):
-    barrier = pltpu.get_barrier_semaphore()
-    for device in devices:
-        pl.semaphore_signal(barrier, inc=1, device_id=device, device_id_type=MESH)
-    pl.semaphore_wait(barrier, len(devices))
 
 
 def section_peers(replica, section, chip, core, sections):
@@ -103,21 +96,19 @@
     return new_params, new_moments, new_seconds
 
 
-def run_layers(features, tokens_per, section, counted, codes, z, square, gram, coef, mixing, hb, rate, a_s, w_s, a_all):
-    layers, _, tokens, wide = z.shape
-    rank = wide // 2
+def run_layers(features, tokens_per, section, counted, z, square, gram, coef, mixing, hb, rate, a_s, w_s, a_all):
+    layers, packed, wide = z.shape
+    rank, tokens = wide // 2, packed * 2 // 3
     root = 1.0 / math.sqrt(features)
     row = lax.broadcasted_iota(jnp.int32, (tokens, 1), 0)
     taken = row < counted * tokens_per
 
     def picked(kind, layer):
-        first = z[layer, kind][:, :rank]
-        if layer == 0:
-            return first.astype(jnp.float32)
-        before = z[layer - 1, kind]
-        code = codes[layer]
-        other = jnp.where(code == 1, before[:, rank:], before[:, :rank])
-        return jnp.where(code == 0, first, other).astype(jnp.float32)
+        if kind < 2:
+            found = z[layer, :tokens, kind * rank : (kind + 1) * rank]
+        else:
+            found = jnp.concatenate([z[layer, tokens:, :rank], z[layer, tokens:, rank:]], axis=0)
+        return found.astype(jnp.float32)
 
     norm = square[...]
     state = jnp.concatenate([picked(1, l) for l in range(layers)], axis=1)
@@ -208,6 +199,10 @@
         copy.start()
         started[number] = copy
 
+    def landed(*numbers):
+        for number in numbers:
+            started[number].wait_recv()
+
     swaps = []
 
     def swap(window, r, z):
@@ -215,11 +210,14 @@
         copy.start()
         swaps.append(copy)
 
-    def upper(r):
-        return out.at[1, pl.ds(0, rank), columns_of(r, chip)]
-
-    def lower(r):
-        return out.at[1, pl.ds(rank, rank), columns_of(r, chip)]
+    def rows_of(start, count, r, z):
+        return out.at[0, pl.ds(start, count), columns_of(r, z)]
+
+    def lower(r, z):
+        return rows_of(0, rank, r, z)
+
+    def upper(r, z):
+        return rows_of(rank, rank, r, z)
 
     own = columns_of(replica, chip)
     shift = pltpu.make_async_remote_copy(
@@ -228,54 +226,59 @@
     )
     shift.start()
     out[0, :, own] = share[...]
-    send(0, block(0, replica, chip), partner)
+    send(0, lower(replica, chip), partner)
     send(1, block(0, replica, chip), above)
-    send(3, block(0, replica, chip), below)
+    send(2, block(0, replica, chip), below)
+    send(3, upper(replica, chip), partner)
     swap(0, replica, chip)
+    landed(0)
+    send(4, lower(replica, other), above)
+    send(5, lower(replica, other), below)
+    landed(1)
+    send(6, lower(down, chip), above)
+    send(7, rows_of(rank, rank // 2, down, chip), above)
+    send(8, upper(down, chip), partner)
+    landed(2)
+    send(9, rows_of(rank + rank // 2, rank // 2, up, chip), below)
+    send(10, upper(up, chip), partner)
     shift.wait()
-    send(7, block(1, replica, chip), above)
-    send(8, block(1, replica, chip), below)
-    send(11, block(1, replica, chip), partner)
+    send(13, block(1, replica, chip), above)
+    send(14, block(1, replica, chip), below)
+    send(15, block(1, replica, chip), partner)
+    swap(0, down, chip)
+    swap(0, up, chip)
     swap(1, replica, chip)
-    started[0].wait_recv()
-    send(2, block(0, replica, other), above)
-    send(4, block(0, replica, other), below)
+    landed(5)
+    send(11, lower(up, other), below)
+    landed(3)
     swap(0, replica, other)
-    started[1].wait_recv()
-    send(5, block(0, down, chip), above)
-    swap(0, down, chip)
-    started[3].wait_recv()
-    swap(0, up, chip)
-    started[7].wait_recv()
-    send(9, upper(down), above)
-    send(12, block(1, down, chip), partner)
+    landed(7, 9)
+    send(12, upper(across, chip), partner)
+    landed(15)
+    send(16, block(1, replica, other), above)
+    send(17, block(1, replica, other), below)
+    swap(1, replica, other)
+    landed(13)
+    send(18, block(1, down, chip), above)
     swap(1, down, chip)
-    started[8].wait_recv()
-    send(10, lower(up), below)
-    send(13, block(1, up, chip), partner)
+    landed(14)
     swap(1, up, chip)
-    started[4].wait_recv()
-    send(6, block(0, up, other), below)
+    landed(6)
+    swap(0, across, chip)
+    landed(4, 8)
+    swap(0, down, other)
+    landed(10)
     swap(0, up, other)
-    started[2].wait_recv()
-    swap(0, down, other)
-    started[11].wait_recv()
-    swap(1, replica, other)
-    started[9].wait_recv()
-    send(14, upper(across), partner)
-    started[10].wait_recv()
-    send(15, lower(across), partner)
+    landed(17)
+    send(19, block(1, up, other), below)
+    swap(1, up, other)
+    landed(11, 12)
+    swap(0, across, other)
+    landed(16)
+    swap(1, down, other)
+    landed(18)
     swap(1, across, chip)
-    started[5].wait_recv()
-    swap(0, across, chip)
-    started[6].wait_recv()
-    swap(0, across, other)
-    started[12].wait_recv()
-    swap(1, down, other)
-    started[13].wait_recv()
-    swap(1, up, other)
-    started[14].wait_recv()
-    started[15].wait_recv()
+    landed(19)
     swap(1, across, other)
     for copy in started.values():
         copy.wait_send()
@@ -283,15 +286,23 @@
         copy.wait()
 
 
-COUNTS = dict(rows=7, z=7, gram=15, piece=7, plane=7, core=8, downs=7, mix=15, mixed=15, half=8, chip=14, far=16, swap=16)
+COUNTS = dict(rows=7, zshift=1, z=7, gram=15, piece=7, plane=7, core=8, downs=7, mix=15, mixed=15, half=8, chip=14, far=20, swap=16)
 
 
 def step_kernel(
     replicas, sections, tokens_per,
-    bounds, counts, hidden_hbm, last_hbm, downs_hbm, ups_hbm,
-    master_down, master_up, moment_down, moment_up, second_down, second_up,
+    bounds_hbm, counts_hbm, hidden_hbm, last_hbm, downs_hbm, ups_hbm, *refs,
+):
+    owned_hbm, refs = refs[:6], refs[6:]
+    step_body(
+        replicas, sections, tokens_per, bounds_hbm, counts_hbm, hidden_hbm, last_hbm, downs_hbm, ups_hbm, owned_hbm, *refs
+    )
+
+
+def step_body(
+    replicas, sections, tokens_per, bounds_hbm, counts_hbm, hidden_hbm, last_hbm, downs_hbm, ups_hbm, owned_hbm,
     gradient, placed_down, placed_up,
-    out, hidden, last, weights, mine, z, acc, zs, rows, down_rows, gram, pieces, box, spread,
+    bounds, counts, owned, out, both, weights, mine, z, z_before, acc, zs, rows, down_rows, gram, pieces, box, spread,
     coef, mixing, hb, rate, a_s, w_s, a_all, mix_pieces, mix_box, mix_spread,
     parts, half, chips, inbox, late, share, local, shift_send, shift_recv, *sems,
 ):
@@ -299,9 +310,11 @@
     replica, section, chip, core = place()
     tensor = chip * 2 + core
     me = replica * 4 + tensor
-    rank, columns = master_down.shape
+    _, rank, columns = owned.shape
+    master_down, master_up, moment_down, moment_up, second_down, second_up = (owned.at[i] for i in range(6))
     wide = 2 * rank
-    tokens, features = hidden.shape
+    tokens, features = both.shape[0] // 2, both.shape[1]
+    hidden, last = both.at[pl.ds(0, tokens)], both.at[pl.ds(tokens, tokens)]
     along = section_peers(replica, section, chip, core, sections)
     peers = plane_peers(replica, section, chip, core, replicas)
     sibling = (replica, section, chip * 2 + 1 - core)
@@ -312,11 +325,20 @@
         pltpu.make_async_copy(hidden_hbm, hidden, local.at[2]),
         pltpu.make_async_copy(last_hbm, last, local.at[3]),
     ]
-    for copy in loads:
+    barrier = pltpu.get_barrier_semaphore()
+    everyone = along + [device for device, _ in peers]
+    for device in everyone:
+        pl.semaphore_signal(barrier, inc=1, device_id=device, device_id_type=MESH)
+    firsts = [pltpu.make_async_copy(owned_hbm[i], owned.at[i], local.at[4 + i]) for i in range(6)]
+    firsts.append(pltpu.make_async_copy(bounds_hbm, bounds, local.at[10]))
+    firsts.append(pltpu.make_async_copy(counts_hbm, counts, local.at[11]))
+    for copy in firsts + loads:
         copy.start()
+    for copy in firsts:
+        copy.wait()
     mine[:rank] = master_down[...].astype(mine.dtype)
     mine[rank:] = master_up[...].astype(mine.dtype)
-    greet(along + [device for device, _ in peers])
+    pl.semaphore_wait(barrier, len(everyone))
 
     row_copies = []
     for i, device in enumerate(along):
@@ -344,19 +366,16 @@
 
     for kind in range(3):
         z[kind] = acc[:, kind * wide : (kind + 1) * wide].astype(z.dtype)
-    zs[section] = z[...]
 
     for copy in row_copies:
         copy.wait()
+    z_shift = remote(z, z_before, sem["zshift"], 0, along[0])
+    z_shift.start()
     cut(dot_t(mine[...], rows[...].reshape(sections * rank, columns)), pieces)
     copies = []
     for i, (device, number) in enumerate(peers):
         copies.append(remote(pieces.at[number], box.at[me], sem["gram"], i, device))
         copies[-1].start()
-    z_copies = []
-    for i, device in enumerate(along):
-        z_copies.append(remote(z, zs.at[section], sem["z"], i, device))
-        z_copies[-1].start()
     box[me] = pieces[me]
     for copy in copies:
         copy.wait()
@@ -365,6 +384,15 @@
     for i, device in enumerate(along):
         copies.append(remote(spread.at[me, section], spread.at[me, section], sem["piece"], i, device))
         copies[-1].start()
+    z_shift.wait()
+    here = (bounds[replica, section] == section) & (bounds[replica, section + 1] > section)
+    alone = bounds[replica, jnp.maximum(section - 1, 0)] == section
+    own = []
+    for kind in range(3):
+        moved = jnp.where(alone, z_before[kind][:, :rank], z_before[kind][:, rank:])
+        own.append(jnp.where(here, z[kind][:, :rank], moved))
+    zs[section, :tokens] = jnp.concatenate(own[:2], axis=1)
+    zs[section, tokens:] = jnp.concatenate([own[2][: tokens // 2], own[2][tokens // 2 :]], axis=1)
     for copy in copies:
         copy.wait()
     same = [device for i, (device, number) in enumerate(peers) if i % 2 == 1]
@@ -374,6 +402,10 @@
         copies[-1].start()
     swaps = [remote(spread.at[me], spread.at[me], sem["core"], 7, sibling)]
     swaps[0].start()
+    z_copies = []
+    for i, device in enumerate(along):
+        z_copies.append(remote(zs.at[section], zs.at[section], sem["z"], i, device))
+        z_copies[-1].start()
     for i, copy in enumerate(copies):
         copy.wait_recv()
         dr, dz = (i + 1) // 2, (i + 1) % 2
@@ -393,13 +425,9 @@
         copy.wait()
     join(spread, gram)
 
-    codes = [0]
-    for l in range(1, sections):
-        here = (bounds[replica, l] == l) & (bounds[replica, l + 1] > l)
-        codes.append(jnp.where(here, 0, jnp.where(bounds[replica, l - 1] == l, 2, 1)))
     square = jnp.sum(acc[:, 3 * wide :], axis=1, keepdims=True)
     run_layers(
-        features, tokens_per, section, counts[replica], codes, zs, square, gram, coef, mixing, hb, rate, a_s, w_s, a_all
+        features, tokens_per, section, counts[replica], zs, square, gram, coef, mixing, hb, rate, a_s, w_s, a_all
     )
 
     cut(mixing[...], mix_pieces)
@@ -418,7 +446,7 @@
     def block_gradient(dr, dz, c):
         number = lax.rem(replica + dr, replicas) * 4 + lax.rem(chip + dz, 2) * 2 + c
         at = pl.ds(pl.multiple_of(number * columns, 128), columns)
-        return dot_n(coef[:, :tokens], hidden[:, at]) + dot_n(coef[:, tokens:], last[:, at])
+        return dot_n(coef[...], both[:, at])
 
     halves = []
     sends = {}
@@ -515,7 +543,7 @@
     size = replicas * 4
     height, width = 16, wide * layers * rank // size // 16
     b16, f32 = jnp.bfloat16, jnp.float32
-    smem, hbm, vmem = (pl.BlockSpec(memory_space=m) for m in (pltpu.SMEM, pl.ANY, pltpu.VMEM))
+    hbm, vmem = (pl.BlockSpec(memory_space=m) for m in (pltpu.HBM, pltpu.VMEM))
     piece = pltpu.VMEM((size, height, width), b16)
     block = pltpu.VMEM((size // 2, wide, columns), b16)
     return pl.pallas_call(
@@ -525,17 +553,20 @@
             jax.ShapeDtypeStruct((2, rank, features), b16),
             jax.ShapeDtypeStruct((2, rank, features), b16),
         ),
-        in_specs=[smem, smem] + [hbm] * 4 + [vmem] * 6,
+        in_specs=[hbm] * 12,
         out_specs=(vmem,) * 3,
         scratch_shapes=[
+            pltpu.SMEM(bounds.shape, jnp.int32),
+            pltpu.SMEM(counts.shape, jnp.int32),
+            pltpu.VMEM((6, rank, columns), f32),
             pltpu.VMEM((2, wide, features), b16),
-            pltpu.VMEM((tokens, features), b16),
-            pltpu.VMEM((tokens, features), b16),
+            pltpu.VMEM((2 * tokens, features), b16),
             pltpu.VMEM((2 * wide, features), b16),
             pltpu.VMEM((wide, columns), b16),
             pltpu.VMEM((3, tokens, wide), b16),
+            pltpu.VMEM((3, tokens, wide), b16),
             pltpu.VMEM((tokens, 3 * wide + 128), f32),
-            pltpu.VMEM((layers, 3, tokens, wide), b16),
+            pltpu.VMEM((layers, tokens * 3 // 2, wide), b16),
             pltpu.VMEM((layers, rank, columns), b16),
             pltpu.VMEM((layers, rank, columns), b16),
             pltpu.VMEM((layers, wide, layers * rank), b16),
@@ -558,14 +589,14 @@
             block,
             pltpu.VMEM((replicas, rank, columns), b16),
             pltpu.VMEM((wide, columns), b16),
-            pltpu.SemaphoreType.DMA((4,)),
+            pltpu.SemaphoreType.DMA((12,)),
             pltpu.SemaphoreType.DMA,
             pltpu.SemaphoreType.DMA,
         ]
         + dma_pairs(COUNTS.values()),
         compiler_params=pltpu.CompilerParams(collective_id=1, has_side_effects=True, vmem_limit_bytes=42 * 2**20),
         name="step",
-    )(bounds, counts, hidden, last, downs, ups, *owned)
+    )(*[pltpu.with_memory_space_constraint(array, pltpu.HBM) for array in (bounds, counts, hidden, last, downs, ups, *owned)])
 
 
 def on_device(

time: 120 us -> 110 us (0.917)
  local copies, waits for them, and re-layouts: 12.1 us -> 3.35 us
    unnamed x20 -> x14, local copies, waits for them, and re-layouts: 12.1 us -> 3.35 us
where the time goes in v5:
time: 110 us
  Pallas kernels  105 us (95%)
  local copies, waits for them, and re-layouts  3.35 us (3%)
  other arithmetic  1.18 us (1%)
    pallas_call x1, Pallas kernels, run_step(): pl.pallas_call(functools.partial(step_kernel, replicas, sections, tokens_...  105 us
    unnamed x14, local copies, waits for them, and re-layouts  3.35 us

profile of v5, /device:TPU:1, one launch (start us, length us, event | category | flops | bytes accessed | tf_op | source)
XLA Modules:
  0.0 109.8 jit_solution(2485495100868473108)
XLA Ops:
  0.6 0.0 copy-start
  0.6 0.0 copy-start.1
  0.7 0.0 copy-start.2
  0.7 0.0 copy-start.3
  0.7 0.0 copy-start.4
  0.7 0.0 copy-start.5
  0.7 104.5 %step.1 = (f32[128,768]{1,0:T(8,128)S(1)}, bf16[2,64,12288]{2,1,0:T(8,128)(2,1)S(1)}, bf16[2,64,12288]{2,1,0:T(8,128)(2,1)S(1)}) custom-call(s32[4,9]{1,0:T(4,128)} %bounds_hbm.1, s32[4]{0:T(128)} %counts_hbm.1, bf16[128,12288]{1,0:T(8,128)(2,1)} %bitcast.36, bf16[128,12288]{1,0:T(8,128)(2,1)} %bitcast.37, bf16[128,12288]{1,0:T(8,128)(2,1)} %bitcast.38, ...), custom_call_target="tpu_custom_call" | custom-call | tf_op jit(solution)/shard_map/step/pallas_call | solution.py:549
  105.2 0.0 copy-done
  105.2 0.0 copy-done.1
  105.2 0.0 copy-done.2
  105.2 0.0 copy-done.3
  105.3 0.0 copy-done.4
  105.3 0.0 copy-done.5
  105.3 1.2 %fusion.4 = (f32[1,64,768]{2,1,0:T(8,128)}, f32[1,64,768]{2,1,0:T(8,128)}, f32[1,64,768]{2,1,0:T(8,128)}, f32[1,64,768]{2,1,0:T(8,128)}, f32[1,64,768]{2,1,0:T(8,128)}, /*index=5*/f32[1,64,768]{2,1,0:T(8,128)}) fusion(f32[128,768]{1,0:T(8,128)S(1)} %get-tuple-element.13, f32[1,64,768]{2,1,0:T(8,128)S(1)} %copy-done.5, f32[1,64,768]{2,1,0:T(8,128)S(1)} %copy-done.3, ...), kind=kLoop, calls=%fused_computation.10 | loop fusion | flops 1474560 | bytes 2752512 | tf_op jit(solution)/shard_map/broadcast_in_dim | solution.py:622
  106.5 1.7 %copy.22 = bf16[1,1,2,64,12288]{4,3,2,1,0:T(8,128)(2,1)} copy(bf16[1,1,2,64,12288]{4,3,2,1,0:T(8,128)(2,1)S(1)} %bitcast.35) | data formatting | bytes 6291456
  108.1 1.7 %copy.23 = bf16[1,1,2,64,12288]{4,3,2,1,0:T(8,128)(2,1)} copy(bf16[1,1,2,64,12288]{4,3,2,1,0:T(8,128)(2,1)S(1)} %bitcast.34) | data formatting | bytes 6291456
Async XLA Ops:
  0.6 104.6 %copy-start = (f32[1,64,768]{2,1,0:T(8,128)S(1)}, f32[1,64,768]{2,1,0:T(8,128)}, u32[]{:S(2)}) copy-start(f32[1,64,768]{2,1,0:T(8,128)} %param.18) | copy-start | bytes 589828
  0.6 104.6 %copy-start.1 = (f32[1,64,768]{2,1,0:T(8,128)S(1)}, f32[1,64,768]{2,1,0:T(8,128)}, u32[]{:S(2)}) copy-start(f32[1,64,768]{2,1,0:T(8,128)} %param.19) | copy-start | bytes 589828
  0.7 104.6 %copy-start.2 = (f32[1,64,768]{2,1,0:T(8,128)S(1)}, f32[1,64,768]{2,1,0:T(8,128)}, u32[]{:S(2)}) copy-start(f32[1,64,768]{2,1,0:T(8,128)} %param.20) | copy-start | bytes 589828
  0.7 104.6 %copy-start.3 = (f32[1,64,768]{2,1,0:T(8,128)S(1)}, f32[1,64,768]{2,1,0:T(8,128)}, u32[]{:S(2)}) copy-start(f32[1,64,768]{2,1,0:T(8,128)} %param.21) | copy-start | bytes 589828
  0.7 104.6 %copy-start.4 = (f32[1,64,768]{2,1,0:T(8,128)S(1)}, f32[1,64,768]{2,1,0:T(8,128)}, u32[]{:S(2)}) copy-start(f32[1,64,768]{2,1,0:T(8,128)} %param.22) | copy-start | bytes 589828
  0.7 104.6 %copy-start.5 = (f32[1,64,768]{2,1,0:T(8,128)S(1)}, f32[1,64,768]{2,1,0:T(8,128)}, u32[]{:S(2)}) copy-start(f32[1,64,768]{2,1,0:T(8,128)} %param.23) | copy-start | bytes 589828

commit v6 on v5

--- a/solution.py
+++ b/solution.py
@@ -175,7 +175,7 @@
     mixing[rank:] = (-dot_n(own_left, scaled)).astype(jnp.bfloat16)
 
 
-def publish(replicas, sections, share, out, shift_send, shift_recv, far_sems, core_sems):
+def publish(replicas, sections, share, out, far_sems, core_sems):
     replica, section, chip, core = place()
     columns = share.shape[1]
     before = lax.rem(section + sections - 1, sections)
@@ -210,75 +210,60 @@
         copy.start()
         swaps.append(copy)
 
-    def rows_of(start, count, r, z):
-        return out.at[0, pl.ds(start, count), columns_of(r, z)]
-
-    def lower(r, z):
-        return rows_of(0, rank, r, z)
-
-    def upper(r, z):
-        return rows_of(rank, rank, r, z)
+    def half(which, r):
+        return out.at[0, pl.ds(which * rank, rank), columns_of(r, chip)]
 
     own = columns_of(replica, chip)
-    shift = pltpu.make_async_remote_copy(
-        src_ref=share, dst_ref=out.at[1, :, own], send_sem=shift_send, recv_sem=shift_recv,
-        device_id=(replica, before, tensor), device_id_type=MESH,
-    )
-    shift.start()
+    for number, device in ((3, (replica, before, tensor)), (4, (replica, before, other * 2 + core))):
+        started[number] = remote(share, out.at[1, :, own], far_sems, number, device)
+        started[number].start()
     out[0, :, own] = share[...]
-    send(0, lower(replica, chip), partner)
-    send(1, block(0, replica, chip), above)
-    send(2, block(0, replica, chip), below)
-    send(3, upper(replica, chip), partner)
+    send(0, block(0, replica, chip), above)
+    send(1, block(0, replica, chip), below)
+    send(2, block(0, replica, chip), partner)
     swap(0, replica, chip)
     landed(0)
-    send(4, lower(replica, other), above)
-    send(5, lower(replica, other), below)
+    send(5, half(0, down), above)
+    send(6, block(0, down, chip), partner)
     landed(1)
-    send(6, lower(down, chip), above)
-    send(7, rows_of(rank, rank // 2, down, chip), above)
-    send(8, upper(down, chip), partner)
-    landed(2)
-    send(9, rows_of(rank + rank // 2, rank // 2, up, chip), below)
-    send(10, upper(up, chip), partner)
-    shift.wait()
-    send(13, block(1, replica, chip), above)
-    send(14, block(1, replica, chip), below)
-    send(15, block(1, replica, chip), partner)
+    send(7, half(1, up), below)
+    send(8, block(0, up, chip), partner)
+    landed(3)
+    send(9, block(1, replica, chip), above)
+    send(10, block(1, replica, chip), below)
+    landed(4)
+    send(11, block(1, replica, other), above)
+    send(12, block(1, replica, other), below)
     swap(0, down, chip)
     swap(0, up, chip)
     swap(1, replica, chip)
+    swap(1, replica, other)
+    landed(2)
+    swap(0, replica, other)
     landed(5)
-    send(11, lower(up, other), below)
-    landed(3)
-    swap(0, replica, other)
-    landed(7, 9)
-    send(12, upper(across, chip), partner)
+    send(13, half(0, across), partner)
+    landed(7)
+    send(14, half(1, across), partner)
+    swap(0, across, chip)
+    landed(9)
+    send(15, block(1, down, chip), above)
+    swap(1, down, chip)
+    landed(10)
+    swap(1, up, chip)
+    landed(12)
+    send(16, block(1, up, other), below)
+    swap(1, up, other)
+    landed(11)
+    swap(1, down, other)
+    landed(6)
+    swap(0, down, other)
+    landed(8)
+    swap(0, up, other)
     landed(15)
-    send(16, block(1, replica, other), above)
-    send(17, block(1, replica, other), below)
-    swap(1, replica, other)
-    landed(13)
-    send(18, block(1, down, chip), above)
-    swap(1, down, chip)
-    landed(14)
-    swap(1, up, chip)
-    landed(6)
-    swap(0, across, chip)
-    landed(4, 8)
-    swap(0, down, other)
-    landed(10)
-    swap(0, up, other)
-    landed(17)
-    send(19, block(1, up, other), below)
-    swap(1, up, other)
-    landed(11, 12)
+    swap(1, across, chip)
+    landed(13, 14)
     swap(0, across, other)
     landed(16)
-    swap(1, down, other)
-    landed(18)
-    swap(1, across, chip)
-    landed(19)
     swap(1, across, other)
     for copy in started.values():
         copy.wait_send()
@@ -286,7 +271,7 @@
         copy.wait()
 
 
-COUNTS = dict(rows=7, zshift=1, z=7, gram=15, piece=7, plane=7, core=8, downs=7, mix=15, mixed=15, half=8, chip=14, far=20, swap=16)
+COUNTS = dict(rows=7, zshift=1, z=7, gram=15, piece=7, plane=7, core=8, downs=7, mix=15, mixed=15, half=8, chip=14, far=17, swap=16)
 
 
 def step_kernel(
@@ -304,7 +289,7 @@
     gradient, placed_down, placed_up,
     bounds, counts, owned, out, both, weights, mine, z, z_before, acc, zs, rows, down_rows, gram, pieces, box, spread,
     coef, mixing, hb, rate, a_s, w_s, a_all, mix_pieces, mix_box, mix_spread,
-    parts, half, chips, inbox, late, share, local, shift_send, shift_recv, *sems,
+    parts, half, chips, inbox, late, share, local, *sems,
 ):
     sem = {name: sems[2 * i : 2 * i + 2] for i, name in enumerate(COUNTS)}
     replica, section, chip, core = place()
@@ -327,6 +312,8 @@
     ]
     barrier = pltpu.get_barrier_semaphore()
     everyone = along + [device for device, _ in peers]
+    for d in (1, sections - 1):
+        everyone.append((replica, lax.rem(section + d, sections), (1 - chip) * 2 + core))
     for device in everyone:
         pl.semaphore_signal(barrier, inc=1, device_id=device, device_id_type=MESH)
     firsts = [pltpu.make_async_copy(owned_hbm[i], owned.at[i], local.at[4 + i]) for i in range(6)]
@@ -395,23 +382,35 @@
     zs[section, tokens:] = jnp.concatenate([own[2][: tokens // 2], own[2][tokens // 2 :]], axis=1)
     for copy in copies:
         copy.wait()
-    same = [device for i, (device, number) in enumerate(peers) if i % 2 == 1]
-    copies = []
-    for i, device in enumerate(same):
-        copies.append(remote(spread.at[me], spread.at[me], sem["plane"], i, device))
+    partner = (replica, section, (1 - chip) * 2 + core)
+    theirs = replica * 4 + (1 - chip) * 2 + core
+    copies, swaps = [], []
+
+    def spread_to(number, device):
+        copies.append(remote(spread.at[number], spread.at[number], sem["plane"], len(copies), device))
         copies[-1].start()
-    swaps = [remote(spread.at[me], spread.at[me], sem["core"], 7, sibling)]
-    swaps[0].start()
+
+    def spread_swap(number):
+        swaps.append(remote(spread.at[number], spread.at[number], sem["core"], len(swaps), sibling))
+        swaps[-1].start()
+
+    spread_to(me, partner)
+    distances = (2, 1, 3)
+    for dr in distances:
+        spread_to(me, (lax.rem(replica + dr, replicas), section, tensor))
     z_copies = []
     for i, device in enumerate(along):
         z_copies.append(remote(zs.at[section], zs.at[section], sem["z"], i, device))
         z_copies[-1].start()
-    for i, copy in enumerate(copies):
-        copy.wait_recv()
-        dr, dz = (i + 1) // 2, (i + 1) % 2
-        source = lax.rem(replica + replicas - dr, replicas) * 4 + lax.rem(chip + dz, 2) * 2 + core
-        swaps.append(remote(spread.at[source], spread.at[source], sem["core"], i, sibling))
-        swaps[-1].start()
+    spread_swap(me)
+    copies[0].wait_recv()
+    for dr in distances:
+        spread_to(theirs, (lax.rem(replica + dr, replicas), section, tensor))
+    spread_swap(theirs)
+    for i, z_at in ((1, chip), (4, 1 - chip)):
+        for j, dr in enumerate(distances):
+            copies[i + j].wait_recv()
+            spread_swap(lax.rem(replica + replicas - dr, replicas) * 4 + z_at * 2 + core)
     for copy in copies:
         copy.wait_send()
     for copy in z_copies:
@@ -437,7 +436,6 @@
         mix_copies[-1].start()
     mix_box[me] = mix_pieces[me]
     order = [(2, 1), (2, 0), (1, 1), (1, 0), (3, 1), (3, 0), (0, 1), (0, 0)]
-    partner = (replica, section, lax.rem(chip + 1, 2) * 2 + core)
     first, second = pl.ds(0, rank), pl.ds(rank, rank)
 
     def ring(dr):
@@ -521,7 +519,7 @@
         copy.wait_send()
     share[:rank] = decayed(master_down[...], moment_down[...], second_down[...], gradient[:rank])[0].astype(share.dtype)
     share[rank:] = decayed(master_up[...], moment_up[...], second_up[...], gradient[rank:])[0].astype(share.dtype)
-    publish(replicas, sections, share, out, shift_send, shift_recv, sem["far"], sem["swap"])
+    publish(replicas, sections, share, out, sem["far"], sem["swap"])
     begin, end = bounds[replica, section], bounds[replica, section + 1]
     held, both, own = end > begin, end > begin + 1, begin == section
 
@@ -590,8 +588,6 @@
             pltpu.VMEM((replicas, rank, columns), b16),
             pltpu.VMEM((wide, columns), b16),
             pltpu.SemaphoreType.DMA((12,)),
-            pltpu.SemaphoreType.DMA,
-            pltpu.SemaphoreType.DMA,
         ]
         + dma_pairs(COUNTS.values()),
         compiler_params=pltpu.CompilerParams(collective_id=1, has_side_effects=True, vmem_limit_bytes=42 * 2**20),

time: 110 us -> 113 us (1.027)
  Pallas kernels: 105 us -> 107 us
    pallas_call x1, Pallas kernels: 105 us -> 107 us  [run_step(): pl.pallas_call(functools.partial(step_kernel, replicas, sections, tokens_...]
where the time goes in v6:
time: 113 us
  Pallas kernels  107 us (95%)
  local copies, waits for them, and re-layouts  3.35 us (3%)
  other arithmetic  1.18 us (1%)
    pallas_call x1, Pallas kernels, run_step(): pl.pallas_call(functools.partial(step_kernel, replicas, sections, tokens_...  107 us
    unnamed x14, local copies, waits for them, and re-layouts  3.35 us

profile of v6, /device:TPU:1, one launch (start us, length us, event | category | flops | bytes accessed | tf_op | source)
XLA Modules:
  0.0 112.5 jit_solution(6279769332684320360)
XLA Ops:
  0.6 0.0 copy-start
  0.6 0.0 copy-start.1
  0.7 0.0 copy-start.2
  0.7 0.0 copy-start.3
  0.7 0.0 copy-start.4
  0.7 0.0 copy-start.5
  0.7 107.2 %step.1 = (f32[128,768]{1,0:T(8,128)S(1)}, bf16[2,64,12288]{2,1,0:T(8,128)(2,1)S(1)}, bf16[2,64,12288]{2,1,0:T(8,128)(2,1)S(1)}) custom-call(s32[4,9]{1,0:T(4,128)} %bounds_hbm.1, s32[4]{0:T(128)} %counts_hbm.1, bf16[128,12288]{1,0:T(8,128)(2,1)} %bitcast.36, bf16[128,12288]{1,0:T(8,128)(2,1)} %bitcast.37, bf16[128,12288]{1,0:T(8,128)(2,1)} %bitcast.38, ...), custom_call_target="tpu_custom_call" | custom-call | tf_op jit(solution)/shard_map/step/pallas_call | solution.py:547
  107.9 0.0 copy-done
  108.0 0.0 copy-done.1
  108.0 0.0 copy-done.2
  108.0 0.0 copy-done.3
  108.0 0.0 copy-done.4
  108.0 0.0 copy-done.5
  108.0 1.2 %fusion.4 = (f32[1,64,768]{2,1,0:T(8,128)}, f32[1,64,768]{2,1,0:T(8,128)}, f32[1,64,768]{2,1,0:T(8,128)}, f32[1,64,768]{2,1,0:T(8,128)}, f32[1,64,768]{2,1,0:T(8,128)}, /*index=5*/f32[1,64,768]{2,1,0:T(8,128)}) fusion(f32[128,768]{1,0:T(8,128)S(1)} %get-tuple-element.13, f32[1,64,768]{2,1,0:T(8,128)S(1)} %copy-done.5, f32[1,64,768]{2,1,0:T(8,128)S(1)} %copy-done.3, ...), kind=kLoop, calls=%fused_computation.10 | loop fusion | flops 1474560 | bytes 2752512 | tf_op jit(solution)/shard_map/broadcast_in_dim | solution.py:618
  109.2 1.7 %copy.22 = bf16[1,1,2,64,12288]{4,3,2,1,0:T(8,128)(2,1)} copy(bf16[1,1,2,64,12288]{4,3,2,1,0:T(8,128)(2,1)S(1)} %bitcast.35) | data formatting | bytes 6291456
  110.8 1.7 %copy.23 = bf16[1,1,2,64,12288]{4,3,2,1,0:T(8,128)(2,1)} copy(bf16[1,1,2,64,12288]{4,3,2,1,0:T(8,128)(2,1)S(1)} %bitcast.34) | data formatting | bytes 6291456
Async XLA Ops:
  0.6 107.3 %copy-start = (f32[1,64,768]{2,1,0:T(8,128)S(1)}, f32[1,64,768]{2,1,0:T(8,128)}, u32[]{:S(2)}) copy-start(f32[1,64,768]{2,1,0:T(8,128)} %param.18) | copy-start | bytes 589828
  0.6 107.3 %copy-start.1 = (f32[1,64,768]{2,1,0:T(8,128)S(1)}, f32[1,64,768]{2,1,0:T(8,128)}, u32[]{:S(2)}) copy-start(f32[1,64,768]{2,1,0:T(8,128)} %param.19) | copy-start | bytes 589828
  0.7 107.3 %copy-start.2 = (f32[1,64,768]{2,1,0:T(8,128)S(1)}, f32[1,64,768]{2,1,0:T(8,128)}, u32[]{:S(2)}) copy-start(f32[1,64,768]{2,1,0:T(8,128)} %param.20) | copy-start | bytes 589828
  0.7 107.3 %copy-start.3 = (f32[1,64,768]{2,1,0:T(8,128)S(1)}, f32[1,64,768]{2,1,0:T(8,128)}, u32[]{:S(2)}) copy-start(f32[1,64,768]{2,1,0:T(8,128)} %param.21) | copy-start | bytes 589828
  0.7 107.3 %copy-start.4 = (f32[1,64,768]{2,1,0:T(8,128)S(1)}, f32[1,64,768]{2,1,0:T(8,128)}, u32[]{:S(2)}) copy-start(f32[1,64,768]{2,1,0:T(8,128)} %param.22) | copy-start | bytes 589828
  0.7 107.3 %copy-start.5 = (f32[1,64,768]{2,1,0:T(8,128)S(1)}, f32[1,64,768]{2,1,0:T(8,128)}, u32[]{:S(2)}) copy-start(f32[1,64,768]{2,1,0:T(8,128)} %param.23) | copy-start | bytes 589828

commit v7 on v6

--- a/solution.py
+++ b/solution.py
@@ -216,24 +216,30 @@
     own = columns_of(replica, chip)
     for number, device in ((3, (replica, before, tensor)), (4, (replica, before, other * 2 + core))):
         started[number] = remote(share, out.at[1, :, own], far_sems, number, device)
-        started[number].start()
+        pl.when(section > 0)(started[number].start)
+
+    @pl.when(section == sections - 1)
+    def _():
+        out[1, :, own] = share[...]
+        out[1, :, columns_of(replica, other)] = share[...]
+
     out[0, :, own] = share[...]
     send(0, block(0, replica, chip), above)
     send(1, block(0, replica, chip), below)
+    swap(0, replica, chip)
+    pl.when(section < sections - 1)(started[3].wait_recv)
+    send(9, block(1, replica, chip), above)
+    send(10, block(1, replica, chip), below)
+    pl.when(section < sections - 1)(started[4].wait_recv)
+    send(11, block(1, replica, other), above)
+    send(12, block(1, replica, other), below)
     send(2, block(0, replica, chip), partner)
-    swap(0, replica, chip)
     landed(0)
     send(5, half(0, down), above)
     send(6, block(0, down, chip), partner)
     landed(1)
     send(7, half(1, up), below)
     send(8, block(0, up, chip), partner)
-    landed(3)
-    send(9, block(1, replica, chip), above)
-    send(10, block(1, replica, chip), below)
-    landed(4)
-    send(11, block(1, replica, other), above)
-    send(12, block(1, replica, other), below)
     swap(0, down, chip)
     swap(0, up, chip)
     swap(1, replica, chip)
@@ -265,8 +271,11 @@
     swap(0, across, other)
     landed(16)
     swap(1, across, other)
-    for copy in started.values():
-        copy.wait_send()
+    for number, copy in started.items():
+        if number in (3, 4):
+            pl.when(section > 0)(copy.wait_send)
+        else:
+            copy.wait_send()
     for copy in swaps:
         copy.wait()
 

time: 113 us -> 105 us (0.929)
  Pallas kernels: 107 us -> 98.3 us
    pallas_call x1, Pallas kernels: 107 us -> 98.3 us  [run_step(): pl.pallas_call(functools.partial(step_kernel, replicas, sections, tokens_...]
where the time goes in v7:
time: 105 us; the launch traced here: 104 us
  Pallas kernels  98.3 us (94%)
  local copies, waits for them, and re-layouts  3.35 us (3%)
  other arithmetic  1.18 us (1%)
    pallas_call x1, Pallas kernels, run_step(): pl.pallas_call(functools.partial(step_kernel, replicas, sections, tokens_...  98.3 us
    unnamed x14, local copies, waits for them, and re-layouts  3.35 us

profile of v7, /device:TPU:1, one launch (start us, length us, event | category | flops | bytes accessed | tf_op | source)
XLA Modules:
  0.0 103.6 jit_solution(13443735817318587839)
XLA Ops:
  0.6 0.0 copy-start
  0.6 0.0 copy-start.1
  0.7 0.0 copy-start.2
  0.7 0.0 copy-start.3
  0.7 0.0 copy-start.4
  0.7 0.0 copy-start.5
  0.7 98.3 %step.1 = (f32[128,768]{1,0:T(8,128)S(1)}, bf16[2,64,12288]{2,1,0:T(8,128)(2,1)S(1)}, bf16[2,64,12288]{2,1,0:T(8,128)(2,1)S(1)}) custom-call(s32[4,9]{1,0:T(4,128)} %bounds_hbm.1, s32[4]{0:T(128)} %counts_hbm.1, bf16[128,12288]{1,0:T(8,128)(2,1)} %bitcast.36, bf16[128,12288]{1,0:T(8,128)(2,1)} %bitcast.37, bf16[128,12288]{1,0:T(8,128)(2,1)} %bitcast.38, ...), custom_call_target="tpu_custom_call" | custom-call | tf_op jit(solution)/shard_map/step/pallas_call | solution.py:556
  99.0 0.0 copy-done
  99.0 0.0 copy-done.1
  99.1 0.0 copy-done.2
  99.1 0.0 copy-done.3
  99.1 0.0 copy-done.4
  99.1 0.0 copy-done.5
  99.1 1.2 %fusion.4 = (f32[1,64,768]{2,1,0:T(8,128)}, f32[1,64,768]{2,1,0:T(8,128)}, f32[1,64,768]{2,1,0:T(8,128)}, f32[1,64,768]{2,1,0:T(8,128)}, f32[1,64,768]{2,1,0:T(8,128)}, /*index=5*/f32[1,64,768]{2,1,0:T(8,128)}) fusion(f32[128,768]{1,0:T(8,128)S(1)} %get-tuple-element.13, f32[1,64,768]{2,1,0:T(8,128)S(1)} %copy-done.5, f32[1,64,768]{2,1,0:T(8,128)S(1)} %copy-done.3, ...), kind=kLoop, calls=%fused_computation.10 | loop fusion | flops 1474560 | bytes 2752512 | tf_op jit(solution)/shard_map/broadcast_in_dim | solution.py:627
  100.3 1.7 %copy.22 = bf16[1,1,2,64,12288]{4,3,2,1,0:T(8,128)(2,1)} copy(bf16[1,1,2,64,12288]{4,3,2,1,0:T(8,128)(2,1)S(1)} %bitcast.35) | data formatting | bytes 6291456
  101.9 1.7 %copy.23 = bf16[1,1,2,64,12288]{4,3,2,1,0:T(8,128)(2,1)} copy(bf16[1,1,2,64,12288]{4,3,2,1,0:T(8,128)(2,1)S(1)} %bitcast.34) | data formatting | bytes 6291456
Async XLA Ops:
  0.6 98.4 %copy-start = (f32[1,64,768]{2,1,0:T(8,128)S(1)}, f32[1,64,768]{2,1,0:T(8,128)}, u32[]{:S(2)}) copy-start(f32[1,64,768]{2,1,0:T(8,128)} %param.18) | copy-start | bytes 589828
  0.6 98.4 %copy-start.1 = (f32[1,64,768]{2,1,0:T(8,128)S(1)}, f32[1,64,768]{2,1,0:T(8,128)}, u32[]{:S(2)}) copy-start(f32[1,64,768]{2,1,0:T(8,128)} %param.19) | copy-start | bytes 589828
  0.7 98.4 %copy-start.2 = (f32[1,64,768]{2,1,0:T(8,128)S(1)}, f32[1,64,768]{2,1,0:T(8,128)}, u32[]{:S(2)}) copy-start(f32[1,64,768]{2,1,0:T(8,128)} %param.20) | copy-start | bytes 589828
  0.7 98.4 %copy-start.3 = (f32[1,64,768]{2,1,0:T(8,128)S(1)}, f32[1,64,768]{2,1,0:T(8,128)}, u32[]{:S(2)}) copy-start(f32[1,64,768]{2,1,0:T(8,128)} %param.21) | copy-start | bytes 589828
  0.7 98.4 %copy-start.4 = (f32[1,64,768]{2,1,0:T(8,128)S(1)}, f32[1,64,768]{2,1,0:T(8,128)}, u32[]{:S(2)}) copy-start(f32[1,64,768]{2,1,0:T(8,128)} %param.22) | copy-start | bytes 589828
  0.7 98.4 %copy-start.5 = (f32[1,64,768]{2,1,0:T(8,128)S(1)}, f32[1,64,768]{2,1,0:T(8,128)}, u32[]{:S(2)}) copy-start(f32[1,64,768]{2,1,0:T(8,128)} %param.23) | copy-start | bytes 589828

commit v8 on v7

--- a/solution.py
+++ b/solution.py
@@ -230,9 +230,6 @@
     pl.when(section < sections - 1)(started[3].wait_recv)
     send(9, block(1, replica, chip), above)
     send(10, block(1, replica, chip), below)
-    pl.when(section < sections - 1)(started[4].wait_recv)
-    send(11, block(1, replica, other), above)
-    send(12, block(1, replica, other), below)
     send(2, block(0, replica, chip), partner)
     landed(0)
     send(5, half(0, down), above)
@@ -240,6 +237,9 @@
     landed(1)
     send(7, half(1, up), below)
     send(8, block(0, up, chip), partner)
+    pl.when(section < sections - 1)(started[4].wait_recv)
+    send(11, block(1, replica, other), above)
+    send(12, block(1, replica, other), below)
     swap(0, down, chip)
     swap(0, up, chip)
     swap(1, replica, chip)
@@ -362,24 +362,17 @@
 
     for kind in range(3):
         z[kind] = acc[:, kind * wide : (kind + 1) * wide].astype(z.dtype)
-
-    for copy in row_copies:
-        copy.wait()
     z_shift = remote(z, z_before, sem["zshift"], 0, along[0])
     z_shift.start()
+
+    for copy in row_copies:
+        copy.wait()
     cut(dot_t(mine[...], rows[...].reshape(sections * rank, columns)), pieces)
     copies = []
     for i, (device, number) in enumerate(peers):
         copies.append(remote(pieces.at[number], box.at[me], sem["gram"], i, device))
         copies[-1].start()
     box[me] = pieces[me]
-    for copy in copies:
-        copy.wait()
-    spread[me, section] = piece_sum(box).astype(spread.dtype)
-    copies = []
-    for i, device in enumerate(along):
-        copies.append(remote(spread.at[me, section], spread.at[me, section], sem["piece"], i, device))
-        copies[-1].start()
     z_shift.wait()
     here = (bounds[replica, section] == section) & (bounds[replica, section + 1] > section)
     alone = bounds[replica, jnp.maximum(section - 1, 0)] == section
@@ -389,6 +382,17 @@
         own.append(jnp.where(here, z[kind][:, :rank], moved))
     zs[section, :tokens] = jnp.concatenate(own[:2], axis=1)
     zs[section, tokens:] = jnp.concatenate([own[2][: tokens // 2], own[2][tokens // 2 :]], axis=1)
+    z_copies = []
+    for i, device in enumerate(along):
+        z_copies.append(remote(zs.at[section], zs.at[section], sem["z"], i, device))
+        z_copies[-1].start()
+    for copy in copies:
+        copy.wait()
+    spread[me, section] = piece_sum(box).astype(spread.dtype)
+    copies = []
+    for i, device in enumerate(along):
+        copies.append(remote(spread.at[me, section], spread.at[me, section], sem["piece"], i, device))
+        copies[-1].start()
     for copy in copies:
         copy.wait()
     partner = (replica, section, (1 - chip) * 2 + core)
@@ -407,10 +411,6 @@
     distances = (2, 1, 3)
     for dr in distances:
         spread_to(me, (lax.rem(replica + dr, replicas), section, tensor))
-    z_copies = []
-    for i, device in enumerate(along):
-        z_copies.append(remote(zs.at[section], zs.at[section], sem["z"], i, device))
-        z_copies[-1].start()
     spread_swap(me)
     copies[0].wait_recv()
     for dr in distances:
@@ -604,6 +604,42 @@
     )(*[pltpu.with_memory_space_constraint(array, pltpu.HBM) for array in (bounds, counts, hidden, last, downs, ups, *owned)])
 
 
+def finish_kernel(placed_down, placed_up, gradient, *refs):
+    owned, (new_down, new_up), news = refs[:6], refs[6:8], refs[8:14]
+    held, sems = refs[14:]
+    copies = [
+        pltpu.make_async_copy(placed_down, new_down, sems.at[0]),
+        pltpu.make_async_copy(placed_up, new_up, sems.at[1]),
+    ]
+    for copy in copies:
+        copy.start()
+    rank = owned[0].shape[0]
+    for kind in range(2):
+        rows = slice(kind * rank, (kind + 1) * rank)
+        values = decayed(owned[kind][...], owned[2 + kind][...], owned[4 + kind][...], gradient[rows])
+        for i, value in enumerate(values):
+            number = 2 * i + kind
+            held[number] = value
+            copies.append(pltpu.make_async_copy(held.at[number], news[number], sems.at[2 + number]))
+            copies[-1].start()
+    for copy in copies:
+        copy.wait()
+
+
+def finish(placed_down, placed_up, gradient, owned):
+    hbm, vmem = (pl.BlockSpec(memory_space=m) for m in (pl.ANY, pltpu.VMEM))
+    like = [jax.ShapeDtypeStruct(array.shape, array.dtype) for array in (placed_down, placed_up, *owned)]
+    return pl.pallas_call(
+        finish_kernel,
+        out_shape=like,
+        in_specs=[vmem] * 9,
+        out_specs=[hbm] * 8,
+        scratch_shapes=[pltpu.VMEM((6,) + owned[0].shape, jnp.float32), pltpu.SemaphoreType.DMA((8,))],
+        compiler_params=pltpu.CompilerParams(vmem_limit_bytes=16 * 2**20),
+        name="finish",
+    )(placed_down, placed_up, gradient, *owned)
+
+
 def on_device(
     inputs, cotangent, micro_counts, bounds, holder_down, holder_up,
     master_down, master_up, moment_down, moment_up, second_down, second_up,
@@ -622,10 +658,8 @@
         owned,
         per,
     )
-    new_down = decayed(owned[0], owned[2], owned[4], gradient[:rank])
-    new_up = decayed(owned[1], owned[3], owned[5], gradient[rank:])
-    news = [array[None] for pair in zip(new_down, new_up) for array in pair]
-    return (placed_down[None, None], placed_up[None, None], *news)
+    new_down, new_up, *news = finish(placed_down, placed_up, gradient, owned)
+    return (new_down[None, None], new_up[None, None], *[array[None] for array in news])
 
 
 def solution(mesh):

time: 105 us -> 102 us (0.971)
  local copies, waits for them, and re-layouts: 3.35 us -> 0.03 us
  Pallas kernels: 98.3 us -> 99.9 us
  other arithmetic: 1.18 us -> 0 us
    unnamed x14 -> x12, local copies, waits for them, and re-layouts: 3.35 us -> 0.03 us
    pallas_call x0 -> x1, Pallas kernels: none -> 3.12 us  [finish(): pl.pallas_call(finish_kernel, out_shape=like, in_specs=[vmem] * 9, out_sp...]
    pallas_call x1, Pallas kernels: 98.3 us -> 96.8 us  [run_step(): pl.pallas_call(functools.partial(step_kernel, replicas, sections, tokens_...]
    broadcast_in_dim x1 -> x0, other arithmetic: 1.18 us -> none  [on_device(): news = [array[None] for pair in zip(new_down, new_up) for array in pair]]
where the time goes in v8:
time: 102 us; the launch traced here: 101 us
  Pallas kernels  99.9 us (98%)
    pallas_call x1, Pallas kernels, run_step(): pl.pallas_call(functools.partial(step_kernel, replicas, sections, tokens_...  96.8 us
    pallas_call x1, Pallas kernels, finish(): pl.pallas_call(finish_kernel, out_shape=like, in_specs=[vmem] * 9, out_sp...  3.12 us

profile of v8, /device:TPU:1, one launch (start us, length us, event | category | flops | bytes accessed | tf_op | source)
XLA Modules:
  0.0 100.7 jit_solution(12027222543230760317)
XLA Ops:
  0.6 0.0 copy-start
  0.6 0.0 copy-start.1
  0.7 0.0 copy-start.2
  0.7 0.0 copy-start.3
  0.7 0.0 copy-start.4
  0.7 0.0 copy-start.5
  0.7 96.8 %step.1 = (f32[128,768]{1,0:T(8,128)S(1)}, bf16[2,64,12288]{2,1,0:T(8,128)(2,1)S(1)}, bf16[2,64,12288]{2,1,0:T(8,128)(2,1)S(1)}) custom-call(s32[4,9]{1,0:T(4,128)} %bounds_hbm.1, s32[4]{0:T(128)} %counts_hbm.1, bf16[128,12288]{1,0:T(8,128)(2,1)} %bitcast.30, bf16[128,12288]{1,0:T(8,128)(2,1)} %bitcast.31, bf16[128,12288]{1,0:T(8,128)(2,1)} %bitcast.32, ...), custom_call_target="tpu_custom_call" | custom-call | tf_op jit(solution)/shard_map/step/pallas_call | solution.py:556
  97.5 0.0 copy-done
  97.5 0.0 copy-done.1
  97.5 0.0 copy-done.2
  97.5 0.0 copy-done.3
  97.5 0.0 copy-done.4
  97.6 0.0 copy-done.5
  97.6 3.1 %finish.1 = (bf16[2,64,12288]{2,1,0:T(8,128)(2,1)}, bf16[2,64,12288]{2,1,0:T(8,128)(2,1)}, f32[64,768]{1,0:T(8,128)}, f32[64,768]{1,0:T(8,128)}, f32[64,768]{1,0...) custom-call(bf16[2,64,12288]{2,1,0:T(8,128)(2,1)S(1)} %get-tuple-element.19.placed_down, ...), custom_call_target="tpu_custom_call" | custom-call | tf_op jit(solution)/shard_map/finish/pallas_call | solution.py:632
Async XLA Ops:
  0.6 96.9 %copy-start = (f32[1,64,768]{2,1,0:T(8,128)S(1)}, f32[1,64,768]{2,1,0:T(8,128)}, u32[]{:S(2)}) copy-start(f32[1,64,768]{2,1,0:T(8,128)} %param.18) | copy-start | bytes 589828
  0.6 96.9 %copy-start.1 = (f32[1,64,768]{2,1,0:T(8,128)S(1)}, f32[1,64,768]{2,1,0:T(8,128)}, u32[]{:S(2)}) copy-start(f32[1,64,768]{2,1,0:T(8,128)} %param.19) | copy-start | bytes 589828
  0.7 96.9 %copy-start.2 = (f32[1,64,768]{2,1,0:T(8,128)S(1)}, f32[1,64,768]{2,1,0:T(8,128)}, u32[]{:S(2)}) copy-start(f32[1,64,768]{2,1,0:T(8,128)} %param.20) | copy-start | bytes 589828
  0.7 96.9 %copy-start.3 = (f32[1,64,768]{2,1,0:T(8,128)S(1)}, f32[1,64,768]{2,1,0:T(8,128)}, u32[]{:S(2)}) copy-start(f32[1,64,768]{2,1,0:T(8,128)} %param.21) | copy-start | bytes 589828
  0.7 96.9 %copy-start.4 = (f32[1,64,768]{2,1,0:T(8,128)S(1)}, f32[1,64,768]{2,1,0:T(8,128)}, u32[]{:S(2)}) copy-start(f32[1,64,768]{2,1,0:T(8,128)} %param.22) | copy-start | bytes 589828
  0.7 96.9 %copy-start.5 = (f32[1,64,768]{2,1,0:T(8,128)S(1)}, f32[1,64,768]{2,1,0:T(8,128)}, u32[]{:S(2)}) copy-start(f32[1,64,768]{2,1,0:T(8,128)} %param.23) | copy-start | bytes 589828

commit v9 on v8

--- a/solution.py
+++ b/solution.py
@@ -210,8 +210,19 @@
         copy.start()
         swaps.append(copy)
 
+    few = rank // 2
+
+    def some(start, stop, r, z):
+        return out.at[0, pl.ds(start, stop - start), columns_of(r, z)]
+
     def half(which, r):
-        return out.at[0, pl.ds(which * rank, rank), columns_of(r, chip)]
+        return some(which * rank, (which + 1) * rank, r, chip)
+
+    def rest(r):
+        return some(few, 2 * rank, r, chip)
+
+    def early(r):
+        return some(0, few, r, other)
 
     own = columns_of(replica, chip)
     for number, device in ((3, (replica, before, tensor)), (4, (replica, before, other * 2 + core))):
@@ -233,10 +244,10 @@
     send(2, block(0, replica, chip), partner)
     landed(0)
     send(5, half(0, down), above)
-    send(6, block(0, down, chip), partner)
+    send(6, rest(down), partner)
     landed(1)
     send(7, half(1, up), below)
-    send(8, block(0, up, chip), partner)
+    send(8, rest(up), partner)
     pl.when(section < sections - 1)(started[4].wait_recv)
     send(11, block(1, replica, other), above)
     send(12, block(1, replica, other), below)
@@ -245,9 +256,11 @@
     swap(1, replica, chip)
     swap(1, replica, other)
     landed(2)
+    send(17, early(replica), above)
+    send(18, early(replica), below)
     swap(0, replica, other)
     landed(5)
-    send(13, half(0, across), partner)
+    send(13, some(few, rank, across, chip), partner)
     landed(7)
     send(14, half(1, across), partner)
     swap(0, across, chip)
@@ -261,13 +274,15 @@
     swap(1, up, other)
     landed(11)
     swap(1, down, other)
-    landed(6)
+    landed(18)
+    send(19, early(up), below)
+    landed(6, 17)
     swap(0, down, other)
     landed(8)
     swap(0, up, other)
     landed(15)
     swap(1, across, chip)
-    landed(13, 14)
+    landed(13, 14, 19)
     swap(0, across, other)
     landed(16)
     swap(1, across, other)
@@ -280,7 +295,7 @@
         copy.wait()
 
 
-COUNTS = dict(rows=7, zshift=1, z=7, gram=15, piece=7, plane=7, core=8, downs=7, mix=15, mixed=15, half=8, chip=14, far=17, swap=16)
+COUNTS = dict(rows=7, zshift=1, z=7, gram=15, piece=7, plane=7, core=8, downs=7, mix=15, mixed=15, half=8, chip=14, far=20, swap=16)
 
 
 def step_kernel(

time: 102 us -> 100 us (0.980); the launches traced: 101 us -> 100 us
  no operation moved by 1% of the time
where the time goes in v9:
time: 100 us
  Pallas kernels  99.6 us (100%)
    pallas_call x1, Pallas kernels, run_step(): pl.pallas_call(functools.partial(step_kernel, replicas, sections, tokens_...  96.5 us
    pallas_call x1, Pallas kernels, finish(): pl.pallas_call(finish_kernel, out_shape=like, in_specs=[vmem] * 9, out_sp...  3.12 us

profile of v9, /device:TPU:1, one launch (start us, length us, event | category | flops | bytes accessed | tf_op | source)
XLA Modules:
  0.0 100.3 jit_solution(12496237178943435163)
XLA Ops:
  0.6 0.0 copy-start
  0.6 0.0 copy-start.1
  0.7 0.0 copy-start.2
  0.7 0.0 copy-start.3
  0.7 0.0 copy-start.4
  0.7 0.0 copy-start.5
  0.7 96.5 %step.1 = (f32[128,768]{1,0:T(8,128)S(1)}, bf16[2,64,12288]{2,1,0:T(8,128)(2,1)S(1)}, bf16[2,64,12288]{2,1,0:T(8,128)(2,1)S(1)}) custom-call(s32[4,9]{1,0:T(4,128)} %bounds_hbm.1, s32[4]{0:T(128)} %counts_hbm.1, bf16[128,12288]{1,0:T(8,128)(2,1)} %bitcast.30, bf16[128,12288]{1,0:T(8,128)(2,1)} %bitcast.31, bf16[128,12288]{1,0:T(8,128)(2,1)} %bitcast.32, ...), custom_call_target="tpu_custom_call" | custom-call | tf_op jit(solution)/shard_map/step/pallas_call | solution.py:571
  97.2 0.0 copy-done
  97.2 0.0 copy-done.1
  97.2 0.0 copy-done.2
  97.2 0.0 copy-done.3
  97.2 0.0 copy-done.4
  97.2 0.0 copy-done.5
  97.2 3.1 %finish.1 = (bf16[2,64,12288]{2,1,0:T(8,128)(2,1)}, bf16[2,64,12288]{2,1,0:T(8,128)(2,1)}, f32[64,768]{1,0:T(8,128)}, f32[64,768]{1,0:T(8,128)}, f32[64,768]{1,0...) custom-call(bf16[2,64,12288]{2,1,0:T(8,128)(2,1)S(1)} %get-tuple-element.19.placed_down, ...), custom_call_target="tpu_custom_call" | custom-call | tf_op jit(solution)/shard_map/finish/pallas_call | solution.py:647
Async XLA Ops:
  0.6 96.5 %copy-start = (f32[1,64,768]{2,1,0:T(8,128)S(1)}, f32[1,64,768]{2,1,0:T(8,128)}, u32[]{:S(2)}) copy-start(f32[1,64,768]{2,1,0:T(8,128)} %param.18) | copy-start | bytes 589828
  0.6 96.5 %copy-start.1 = (f32[1,64,768]{2,1,0:T(8,128)S(1)}, f32[1,64,768]{2,1,0:T(8,128)}, u32[]{:S(2)}) copy-start(f32[1,64,768]{2,1,0:T(8,128)} %param.19) | copy-start | bytes 589828
  0.7 96.5 %copy-start.2 = (f32[1,64,768]{2,1,0:T(8,128)S(1)}, f32[1,64,768]{2,1,0:T(8,128)}, u32[]{:S(2)}) copy-start(f32[1,64,768]{2,1,0:T(8,128)} %param.20) | copy-start | bytes 589828
  0.7 96.5 %copy-start.3 = (f32[1,64,768]{2,1,0:T(8,128)S(1)}, f32[1,64,768]{2,1,0:T(8,128)}, u32[]{:S(2)}) copy-start(f32[1,64,768]{2,1,0:T(8,128)} %param.21) | copy-start | bytes 589828
  0.7 96.5 %copy-start.4 = (f32[1,64,768]{2,1,0:T(8,128)S(1)}, f32[1,64,768]{2,1,0:T(8,128)}, u32[]{:S(2)}) copy-start(f32[1,64,768]{2,1,0:T(8,128)} %param.22) | copy-start | bytes 589828
  0.7 96.5 %copy-start.5 = (f32[1,64,768]{2,1,0:T(8,128)S(1)}, f32[1,64,768]{2,1,0:T(8,128)}, u32[]{:S(2)}) copy-start(f32[1,64,768]{2,1,0:T(8,128)} %param.23) | copy-start | bytes 589828

commit v10 on v9

--- a/solution.py
+++ b/solution.py
@@ -352,8 +352,9 @@
     pl.semaphore_wait(barrier, len(everyone))
 
     row_copies = []
-    for i, device in enumerate(along):
-        row_copies.append(remote(mine.at[pl.ds(rank, rank)], rows.at[section], sem["rows"], i, device))
+    far_first = sorted(range(len(along)), key=lambda i: abs(i + 1 - sections // 2))
+    for i in far_first:
+        row_copies.append(remote(mine.at[pl.ds(rank, rank)], rows.at[section], sem["rows"], i, along[i]))
         row_copies[-1].start()
     rows[section] = mine[rank:]
 

time: 100 us -> 98 us (0.980)
  Pallas kernels: 99.6 us -> 97.1 us
    pallas_call x1, Pallas kernels: 96.5 us -> 94 us  [run_step(): pl.pallas_call(functools.partial(step_kernel, replicas, sections, tokens_...]
where the time goes in v10:
time: 98 us; the launch traced here: 97.9 us
  Pallas kernels  97.1 us (99%)
    pallas_call x1, Pallas kernels, run_step(): pl.pallas_call(functools.partial(step_kernel, replicas, sections, tokens_...  94 us
    pallas_call x1, Pallas kernels, finish(): pl.pallas_call(finish_kernel, out_shape=like, in_specs=[vmem] * 9, out_sp...  3.12 us

profile of v10, /device:TPU:1, one launch (start us, length us, event | category | flops | bytes accessed | tf_op | source)
XLA Modules:
  0.0 97.9 jit_solution(13293449182289553500)
XLA Ops:
  0.6 0.0 copy-start
  0.6 0.0 copy-start.1
  0.7 0.0 copy-start.2
  0.7 0.0 copy-start.3
  0.7 0.0 copy-start.4
  0.7 0.0 copy-start.5
  0.7 94.0 %step.1 = (f32[128,768]{1,0:T(8,128)S(1)}, bf16[2,64,12288]{2,1,0:T(8,128)(2,1)S(1)}, bf16[2,64,12288]{2,1,0:T(8,128)(2,1)S(1)}) custom-call(s32[4,9]{1,0:T(4,128)} %bounds_hbm.1, s32[4]{0:T(128)} %counts_hbm.1, bf16[128,12288]{1,0:T(8,128)(2,1)} %bitcast.30, bf16[128,12288]{1,0:T(8,128)(2,1)} %bitcast.31, bf16[128,12288]{1,0:T(8,128)(2,1)} %bitcast.32, ...), custom_call_target="tpu_custom_call" | custom-call | tf_op jit(solution)/shard_map/step/pallas_call | solution.py:572
  94.7 0.0 copy-done
  94.7 0.0 copy-done.1
  94.7 0.0 copy-done.2
  94.7 0.0 copy-done.3
  94.8 0.0 copy-done.4
  94.8 0.0 copy-done.5
  94.8 3.1 %finish.1 = (bf16[2,64,12288]{2,1,0:T(8,128)(2,1)}, bf16[2,64,12288]{2,1,0:T(8,128)(2,1)}, f32[64,768]{1,0:T(8,128)}, f32[64,768]{1,0:T(8,128)}, f32[64,768]{1,0...) custom-call(bf16[2,64,12288]{2,1,0:T(8,128)(2,1)S(1)} %get-tuple-element.19.placed_down, ...), custom_call_target="tpu_custom_call" | custom-call | tf_op jit(solution)/shard_map/finish/pallas_call | solution.py:648
Async XLA Ops:
  0.6 94.1 %copy-start = (f32[1,64,768]{2,1,0:T(8,128)S(1)}, f32[1,64,768]{2,1,0:T(8,128)}, u32[]{:S(2)}) copy-start(f32[1,64,768]{2,1,0:T(8,128)} %param.18) | copy-start | bytes 589828
  0.6 94.1 %copy-start.1 = (f32[1,64,768]{2,1,0:T(8,128)S(1)}, f32[1,64,768]{2,1,0:T(8,128)}, u32[]{:S(2)}) copy-start(f32[1,64,768]{2,1,0:T(8,128)} %param.19) | copy-start | bytes 589828
  0.7 94.1 %copy-start.2 = (f32[1,64,768]{2,1,0:T(8,128)S(1)}, f32[1,64,768]{2,1,0:T(8,128)}, u32[]{:S(2)}) copy-start(f32[1,64,768]{2,1,0:T(8,128)} %param.20) | copy-start | bytes 589828
  0.7 94.1 %copy-start.3 = (f32[1,64,768]{2,1,0:T(8,128)S(1)}, f32[1,64,768]{2,1,0:T(8,128)}, u32[]{:S(2)}) copy-start(f32[1,64,768]{2,1,0:T(8,128)} %param.21) | copy-start | bytes 589828
  0.7 94.1 %copy-start.4 = (f32[1,64,768]{2,1,0:T(8,128)S(1)}, f32[1,64,768]{2,1,0:T(8,128)}, u32[]{:S(2)}) copy-start(f32[1,64,768]{2,1,0:T(8,128)} %param.22) | copy-start | bytes 589828
  0.7 94.1 %copy-start.5 = (f32[1,64,768]{2,1,0:T(8,128)S(1)}, f32[1,64,768]{2,1,0:T(8,128)}, u32[]{:S(2)}) copy-start(f32[1,64,768]{2,1,0:T(8,128)} %param.23) | copy-start | bytes 589828
